TPU v7x, 32 devices: a whole 2x2x4 slice. The times are simulated.
32 devices in a mesh: feed: 16 (over z, y, x), tm: 2 (over core).
Axes of the slice: x: 2, y: 2, z: 4, core: 2. Of those that a mesh axis runs over, the one named last changes fastest.
Arguments:
- samples: bfloat16 [2048, 12288], P('feed', 'tm'), may hold values from -6 to 6
- filter_taps: float32 [4, 1024], replicated, may hold values from -3 to 3
- feed_cylinder: int32 [2048], replicated, may hold values from 0 to 3
- feed_delay: int32 [2048], replicated, may hold values from 0 to 4095
- pointing: int32 [512, 4], replicated, may hold values from 0 to 4095
- chirp_rate: float32 [512], P('feed'), may hold values from 1 to 40
Outputs:
- series: float32 [512, 12, 1024], P('feed', 'tm')
All inputs are finite; a program needn't handle non-finite values.
Results may differ from a plain program's by a relative error of at most 0.0046.
Values may be sent and summed in bfloat16 or wider, within the bound.
No kernel may reach another device: no remote copies, remote signals or barrier semaphores. Data moves between devices by JAX's collectives and lax.ppermute only.
A program may use at most 64 MiB of HBM per device.

v0:
```python
import math

import jax
import jax.numpy as jnp
from jax import lax
from jax.sharding import PartitionSpec as P

FEEDS = 2048
NCHAN = 512
BEAMS = 512
TAPS = 4
CYL = 4
PHASES = 4096


def from_behind(x, axis, by):
    length = lax.axis_size(axis)
    pairs = [(i, i + by) for i in range(length) if 0 <= i + by < length]
    return lax.ppermute(x, axis, pairs)


def forward_basis(length, nchan):
    sample_ids = jnp.arange(length, dtype=jnp.int32)[:, None]
    chan_ids = jnp.arange(nchan, dtype=jnp.int32)[None, :]
    angle = (sample_ids * chan_ids % length).astype(jnp.float32) * (2.0 * math.pi / length)
    scaled = 1.0 / math.sqrt(length)
    return jnp.concatenate([jnp.cos(angle), -jnp.sin(angle)], axis=1) * scaled


def inverse_basis(nchan):
    chan_ids = jnp.arange(nchan, dtype=jnp.int32)[:, None]
    time_ids = jnp.arange(nchan, dtype=jnp.int32)[None, :]
    angle = (chan_ids * time_ids % nchan).astype(jnp.float32) * (2.0 * math.pi / nchan)
    cosine = jnp.cos(angle)
    sine = jnp.sin(angle)
    upper = jnp.concatenate([cosine, sine], axis=1)
    lower = jnp.concatenate([-sine, cosine], axis=1)
    return jnp.concatenate([upper, lower], axis=0) * (1.0 / math.sqrt(nchan))


def spectra_of(frame_block, basis):
    feed_here, batch_frames, length = frame_block.shape
    flat = frame_block.reshape(feed_here * batch_frames, length)
    spectral = jnp.dot(
        flat, basis, precision=lax.Precision.HIGHEST, preferred_element_type=jnp.float32
    )
    spectral = spectral.reshape(feed_here, batch_frames, 2, length // 2)
    return jnp.transpose(spectral, (3, 2, 1, 0)).astype(jnp.bfloat16)


def beamform(turned, steer, feed_delay, first_channel):
    chan_here, _, batch_frames, feeds = turned.shape
    beam_scale = 1.0 / math.sqrt(feeds)

    def one_channel(inputs):
        local, offset = inputs
        channel = first_channel + offset
        turns = (channel + 1) * feed_delay % PHASES
        phase = turns[:, None] * steer % PHASES
        angle = phase.astype(jnp.float32) * (2.0 * math.pi / PHASES)
        w_real = jnp.cos(angle).astype(jnp.bfloat16)
        w_imag = jnp.sin(angle).astype(jnp.bfloat16)
        stacked = local.reshape(2 * batch_frames, feeds)
        with_real = jnp.dot(stacked, w_real, preferred_element_type=jnp.float32)
        with_imag = jnp.dot(stacked, w_imag, preferred_element_type=jnp.float32)
        beam_real = with_real[:batch_frames] - with_imag[batch_frames:]
        beam_imag = with_imag[:batch_frames] + with_real[batch_frames:]
        return (jnp.stack([beam_real, beam_imag]) * beam_scale).astype(jnp.bfloat16)

    offsets = jnp.arange(chan_here, dtype=jnp.int32)
    return lax.map(one_channel, (turned, offsets))


def synthesize(returned, chirp_cos, chirp_sin, basis):
    nchan, _, batch_frames, beams_here = returned.shape
    values = returned.astype(jnp.float32)
    beam_real = values[:, 0]
    beam_imag = values[:, 1]
    chirped_real = beam_real * chirp_cos - beam_imag * chirp_sin
    chirped_imag = beam_real * chirp_sin + beam_imag * chirp_cos
    stacked = jnp.stack([chirped_real, chirped_imag])
    ordered = jnp.transpose(stacked, (3, 2, 0, 1)).reshape(beams_here * batch_frames, 2 * nchan)
    result = jnp.dot(
        ordered, basis, precision=lax.Precision.HIGHEST, preferred_element_type=jnp.float32
    )
    return result.reshape(beams_here, batch_frames, 2 * nchan)


def body(samples, filter_taps, feed_cylinder, feed_delay, pointing, chirp_rate):
    length = 2 * NCHAN
    feed_here = samples.shape[0]
    frames_here = samples.shape[1] // length
    frames = samples.reshape(feed_here, frames_here, length)
    tail = from_behind(frames[:, frames_here - (TAPS - 1) :, :], "tm", 1)
    padded = jnp.concatenate([tail, frames], axis=1).astype(jnp.float32)
    filtered = jnp.zeros((feed_here, frames_here, length), jnp.float32)
    for tap_index in range(TAPS):
        filtered = (
            filtered + filter_taps[tap_index] * padded[:, tap_index : tap_index + frames_here, :]
        )
    basis = forward_basis(length, NCHAN)
    steer = jnp.zeros((FEEDS, BEAMS), jnp.int32)
    for cylinder in range(CYL):
        steer = steer + jnp.where(
            feed_cylinder[:, None] == cylinder, pointing[None, :, cylinder], 0
        )
    chan_here = NCHAN // lax.axis_size("feed")
    first_channel = lax.axis_index("feed") * chan_here
    position = jnp.arange(NCHAN).astype(jnp.float32) / NCHAN
    chirp = (jnp.pi * chirp_rate)[None, :] * (position * position)[:, None]
    chirp_cos = jnp.cos(chirp)[:, None, :]
    chirp_sin = jnp.sin(chirp)[:, None, :]
    back_basis = inverse_basis(NCHAN)
    turned = lax.all_to_all(
        spectra_of(filtered, basis), "feed", split_axis=0, concat_axis=3, tiled=True
    )
    formed = beamform(turned, steer, feed_delay, first_channel)
    returned = lax.all_to_all(formed, "feed", split_axis=3, concat_axis=0, tiled=True)
    series = synthesize(returned, chirp_cos, chirp_sin, back_basis)
    return series


def solution(mesh):
    return jax.shard_map(
        body,
        mesh=mesh,
        in_specs=(P("feed", "tm"), P(), P(), P(), P(), P("feed")),
        out_specs=P("feed", "tm", None),
        check_vma=False,
    )
```

profile of v0, /device:TPU:0, one launch (start us, length us, event | category | flops | bytes accessed | tf_op | source)
XLA Modules:
  0.0 1317.2 jit_solution(10227480374787350754)
XLA Ops:
  13.7 29.6 %fusion.53 = bf16[512,2,6,128]{0,3,1,2:T(8,128)(2,1)S(1)} fusion(f32[2,512,1024,1]{2,1,0,3:T(8,128)S(1)} %bitcast.83, f32[128,9,1024]{0,2,1:T(8,128)S(1)} %maximum_convert_fusion, f32[1024]{0:T(1024)S(1)} %bitcast.87, f32[1024]{0:T(1024)S(1)} %bitcast.88, f32[1024]{0:T(1024)S(1)} %bitcast.86, f32[1024]{0:T(1024)S(1)} %bitcast.85), kind=kOutput, calls=%fused_computation.71 | convolution fusion | flops 9669967872 | bytes 18366464 | tf_op jit(solution)/shard_map/dot_general | solution.py:44
  54.1 33.8 %all-to-all-done = bf16[512,2,6,128]{3,1,2,0:T(2,128)(2,1)S(1)} async-done(((bf16[512,2,6,128]{3,1,2,0:T(2,128)(2,1)}), bf16[512,2,6,128]{3,1,2,0:T(2,128)(2,1)S(1)}, u32[]{:S(2)}, u32[]{:S(2)}) %all-to-all-start) | async-done | bytes 1572896 | tf_op jit(solution)/shard_map/all_to_all | solution.py:114
  91.5 1188.4 %while.13 = (s32[]{:T(128)}, bf16[32,2,6,512]{3,2,1,0:T(8,128)(2,1)S(1)}, bf16[32,2,6,2048]{3,2,1,0:T(8,128)(2,1)}, s32[32]{0:T(128)S(1)}, s32[]{:T(128)}, /*ind...) while((s32[]{:T(128)}, ...), condition=%wide.region_1.2_spmd.clone, body=%wide.region_0.1_spmd.clone.sunk | while | flops 96518144 | bytes 532677 | solution.py:71
  117.1 17.0 %fusion.82 = f32[12,512]{1,0:T(8,128)S(1)} fusion(bf16[12,2048]{1,0:T(8,128)(2,1)S(1)} %reshape.197, s32[512]{0:T(512)S(1)} %get-tuple-element.385, s32[512]{0:T(512)S(1)} %get-tuple-element.383, s32[512]{0:T(512)S(1)} %get-tuple-element.381, s32[512]{0:T(512)S(1)} %get-tuple-element.379, s32[2048]{0:T(1024)S(1)} %add_select_fusion.5, ...), kind=kOutput, calls=%fused_computation.11.clone.1 | convolution fusion | flops 48234496 | bytes 98304 | tf_op jit(solution)/shard_map/while/body/eval_jaxpr/dot_general | solution.py:65
  134.1 16.9 %fusion.83 = f32[12,512]{1,0:T(8,128)S(1)} fusion(bf16[12,2048]{1,0:T(8,128)(2,1)S(1)} %reshape.197, s32[512]{0:T(512)S(1)} %get-tuple-element.385, s32[512]{0:T(512)S(1)} %get-tuple-element.383, s32[512]{0:T(512)S(1)} %get-tuple-element.381, s32[512]{0:T(512)S(1)} %get-tuple-element.379, s32[2048]{0:T(1024)S(1)} %add_select_fusion.5, ...), kind=kOutput, calls=%fused_computation.10.clone.1 | convolution fusion | flops 48234496 | bytes 98304 | tf_op jit(solution)/shard_map/while/body/eval_jaxpr/dot_general | solution.py:64
  153.3 17.0 %fusion.82 = f32[12,512]{1,0:T(8,128)S(1)} fusion(bf16[12,2048]{1,0:T(8,128)(2,1)S(1)} %reshape.197, s32[512]{0:T(512)S(1)} %get-tuple-element.385, s32[512]{0:T(512)S(1)} %get-tuple-element.383, s32[512]{0:T(512)S(1)} %get-tuple-element.381, s32[512]{0:T(512)S(1)} %get-tuple-element.379, s32[2048]{0:T(1024)S(1)} %add_select_fusion.5, ...), kind=kOutput, calls=%fused_computation.11.clone.1 | convolution fusion | flops 48234496 | bytes 98304 | tf_op jit(solution)/shard_map/while/body/eval_jaxpr/dot_general | solution.py:65
  170.2 16.9 %fusion.83 = f32[12,512]{1,0:T(8,128)S(1)} fusion(bf16[12,2048]{1,0:T(8,128)(2,1)S(1)} %reshape.197, s32[512]{0:T(512)S(1)} %get-tuple-element.385, s32[512]{0:T(512)S(1)} %get-tuple-element.383, s32[512]{0:T(512)S(1)} %get-tuple-element.381, s32[512]{0:T(512)S(1)} %get-tuple-element.379, s32[2048]{0:T(1024)S(1)} %add_select_fusion.5, ...), kind=kOutput, calls=%fused_computation.10.clone.1 | convolution fusion | flops 48234496 | bytes 98304 | tf_op jit(solution)/shard_map/while/body/eval_jaxpr/dot_general | solution.py:64
  189.4 17.0 %fusion.82 = f32[12,512]{1,0:T(8,128)S(1)} fusion(bf16[12,2048]{1,0:T(8,128)(2,1)S(1)} %reshape.197, s32[512]{0:T(512)S(1)} %get-tuple-element.385, s32[512]{0:T(512)S(1)} %get-tuple-element.383, s32[512]{0:T(512)S(1)} %get-tuple-element.381, s32[512]{0:T(512)S(1)} %get-tuple-element.379, s32[2048]{0:T(1024)S(1)} %add_select_fusion.5, ...), kind=kOutput, calls=%fused_computation.11.clone.1 | convolution fusion | flops 48234496 | bytes 98304 | tf_op jit(solution)/shard_map/while/body/eval_jaxpr/dot_general | solution.py:65
  206.4 16.9 %fusion.83 = f32[12,512]{1,0:T(8,128)S(1)} fusion(bf16[12,2048]{1,0:T(8,128)(2,1)S(1)} %reshape.197, s32[512]{0:T(512)S(1)} %get-tuple-element.385, s32[512]{0:T(512)S(1)} %get-tuple-element.383, s32[512]{0:T(512)S(1)} %get-tuple-element.381, s32[512]{0:T(512)S(1)} %get-tuple-element.379, s32[2048]{0:T(1024)S(1)} %add_select_fusion.5, ...), kind=kOutput, calls=%fused_computation.10.clone.1 | convolution fusion | flops 48234496 | bytes 98304 | tf_op jit(solution)/shard_map/while/body/eval_jaxpr/dot_general | solution.py:64
  225.6 17.0 %fusion.82 = f32[12,512]{1,0:T(8,128)S(1)} fusion(bf16[12,2048]{1,0:T(8,128)(2,1)S(1)} %reshape.197, s32[512]{0:T(512)S(1)} %get-tuple-element.385, s32[512]{0:T(512)S(1)} %get-tuple-element.383, s32[512]{0:T(512)S(1)} %get-tuple-element.381, s32[512]{0:T(512)S(1)} %get-tuple-element.379, s32[2048]{0:T(1024)S(1)} %add_select_fusion.5, ...), kind=kOutput, calls=%fused_computation.11.clone.1 | convolution fusion | flops 48234496 | bytes 98304 | tf_op jit(solution)/shard_map/while/body/eval_jaxpr/dot_general | solution.py:65
  242.5 16.9 %fusion.83 = f32[12,512]{1,0:T(8,128)S(1)} fusion(bf16[12,2048]{1,0:T(8,128)(2,1)S(1)} %reshape.197, s32[512]{0:T(512)S(1)} %get-tuple-element.385, s32[512]{0:T(512)S(1)} %get-tuple-element.383, s32[512]{0:T(512)S(1)} %get-tuple-element.381, s32[512]{0:T(512)S(1)} %get-tuple-element.379, s32[2048]{0:T(1024)S(1)} %add_select_fusion.5, ...), kind=kOutput, calls=%fused_computation.10.clone.1 | convolution fusion | flops 48234496 | bytes 98304 | tf_op jit(solution)/shard_map/while/body/eval_jaxpr/dot_general | solution.py:64
  261.7 17.0 %fusion.82 = f32[12,512]{1,0:T(8,128)S(1)} fusion(bf16[12,2048]{1,0:T(8,128)(2,1)S(1)} %reshape.197, s32[512]{0:T(512)S(1)} %get-tuple-element.385, s32[512]{0:T(512)S(1)} %get-tuple-element.383, s32[512]{0:T(512)S(1)} %get-tuple-element.381, s32[512]{0:T(512)S(1)} %get-tuple-element.379, s32[2048]{0:T(1024)S(1)} %add_select_fusion.5, ...), kind=kOutput, calls=%fused_computation.11.clone.1 | convolution fusion | flops 48234496 | bytes 98304 | tf_op jit(solution)/shard_map/while/body/eval_jaxpr/dot_general | solution.py:65
  278.7 16.9 %fusion.83 = f32[12,512]{1,0:T(8,128)S(1)} fusion(bf16[12,2048]{1,0:T(8,128)(2,1)S(1)} %reshape.197, s32[512]{0:T(512)S(1)} %get-tuple-element.385, s32[512]{0:T(512)S(1)} %get-tuple-element.383, s32[512]{0:T(512)S(1)} %get-tuple-element.381, s32[512]{0:T(512)S(1)} %get-tuple-element.379, s32[2048]{0:T(1024)S(1)} %add_select_fusion.5, ...), kind=kOutput, calls=%fused_computation.10.clone.1 | convolution fusion | flops 48234496 | bytes 98304 | tf_op jit(solution)/shard_map/while/body/eval_jaxpr/dot_general | solution.py:64
  297.9 17.0 %fusion.82 = f32[12,512]{1,0:T(8,128)S(1)} fusion(bf16[12,2048]{1,0:T(8,128)(2,1)S(1)} %reshape.197, s32[512]{0:T(512)S(1)} %get-tuple-element.385, s32[512]{0:T(512)S(1)} %get-tuple-element.383, s32[512]{0:T(512)S(1)} %get-tuple-element.381, s32[512]{0:T(512)S(1)} %get-tuple-element.379, s32[2048]{0:T(1024)S(1)} %add_select_fusion.5, ...), kind=kOutput, calls=%fused_computation.11.clone.1 | convolution fusion | flops 48234496 | bytes 98304 | tf_op jit(solution)/shard_map/while/body/eval_jaxpr/dot_general | solution.py:65
  314.8 16.9 %fusion.83 = f32[12,512]{1,0:T(8,128)S(1)} fusion(bf16[12,2048]{1,0:T(8,128)(2,1)S(1)} %reshape.197, s32[512]{0:T(512)S(1)} %get-tuple-element.385, s32[512]{0:T(512)S(1)} %get-tuple-element.383, s32[512]{0:T(512)S(1)} %get-tuple-element.381, s32[512]{0:T(512)S(1)} %get-tuple-element.379, s32[2048]{0:T(1024)S(1)} %add_select_fusion.5, ...), kind=kOutput, calls=%fused_computation.10.clone.1 | convolution fusion | flops 48234496 | bytes 98304 | tf_op jit(solution)/shard_map/while/body/eval_jaxpr/dot_general | solution.py:64
  334.0 17.0 %fusion.82 = f32[12,512]{1,0:T(8,128)S(1)} fusion(bf16[12,2048]{1,0:T(8,128)(2,1)S(1)} %reshape.197, s32[512]{0:T(512)S(1)} %get-tuple-element.385, s32[512]{0:T(512)S(1)} %get-tuple-element.383, s32[512]{0:T(512)S(1)} %get-tuple-element.381, s32[512]{0:T(512)S(1)} %get-tuple-element.379, s32[2048]{0:T(1024)S(1)} %add_select_fusion.5, ...), kind=kOutput, calls=%fused_computation.11.clone.1 | convolution fusion | flops 48234496 | bytes 98304 | tf_op jit(solution)/shard_map/while/body/eval_jaxpr/dot_general | solution.py:65
  351.0 16.9 %fusion.83 = f32[12,512]{1,0:T(8,128)S(1)} fusion(bf16[12,2048]{1,0:T(8,128)(2,1)S(1)} %reshape.197, s32[512]{0:T(512)S(1)} %get-tuple-element.385, s32[512]{0:T(512)S(1)} %get-tuple-element.383, s32[512]{0:T(512)S(1)} %get-tuple-element.381, s32[512]{0:T(512)S(1)} %get-tuple-element.379, s32[2048]{0:T(1024)S(1)} %add_select_fusion.5, ...), kind=kOutput, calls=%fused_computation.10.clone.1 | convolution fusion | flops 48234496 | bytes 98304 | tf_op jit(solution)/shard_map/while/body/eval_jaxpr/dot_general | solution.py:64
  370.1 17.0 %fusion.82 = f32[12,512]{1,0:T(8,128)S(1)} fusion(bf16[12,2048]{1,0:T(8,128)(2,1)S(1)} %reshape.197, s32[512]{0:T(512)S(1)} %get-tuple-element.385, s32[512]{0:T(512)S(1)} %get-tuple-element.383, s32[512]{0:T(512)S(1)} %get-tuple-element.381, s32[512]{0:T(512)S(1)} %get-tuple-element.379, s32[2048]{0:T(1024)S(1)} %add_select_fusion.5, ...), kind=kOutput, calls=%fused_computation.11.clone.1 | convolution fusion | flops 48234496 | bytes 98304 | tf_op jit(solution)/shard_map/while/body/eval_jaxpr/dot_general | solution.py:65
  387.1 16.9 %fusion.83 = f32[12,512]{1,0:T(8,128)S(1)} fusion(bf16[12,2048]{1,0:T(8,128)(2,1)S(1)} %reshape.197, s32[512]{0:T(512)S(1)} %get-tuple-element.385, s32[512]{0:T(512)S(1)} %get-tuple-element.383, s32[512]{0:T(512)S(1)} %get-tuple-element.381, s32[512]{0:T(512)S(1)} %get-tuple-element.379, s32[2048]{0:T(1024)S(1)} %add_select_fusion.5, ...), kind=kOutput, calls=%fused_computation.10.clone.1 | convolution fusion | flops 48234496 | bytes 98304 | tf_op jit(solution)/shard_map/while/body/eval_jaxpr/dot_general | solution.py:64
  406.3 17.0 %fusion.82 = f32[12,512]{1,0:T(8,128)S(1)} fusion(bf16[12,2048]{1,0:T(8,128)(2,1)S(1)} %reshape.197, s32[512]{0:T(512)S(1)} %get-tuple-element.385, s32[512]{0:T(512)S(1)} %get-tuple-element.383, s32[512]{0:T(512)S(1)} %get-tuple-element.381, s32[512]{0:T(512)S(1)} %get-tuple-element.379, s32[2048]{0:T(1024)S(1)} %add_select_fusion.5, ...), kind=kOutput, calls=%fused_computation.11.clone.1 | convolution fusion | flops 48234496 | bytes 98304 | tf_op jit(solution)/shard_map/while/body/eval_jaxpr/dot_general | solution.py:65
  423.3 16.9 %fusion.83 = f32[12,512]{1,0:T(8,128)S(1)} fusion(bf16[12,2048]{1,0:T(8,128)(2,1)S(1)} %reshape.197, s32[512]{0:T(512)S(1)} %get-tuple-element.385, s32[512]{0:T(512)S(1)} %get-tuple-element.383, s32[512]{0:T(512)S(1)} %get-tuple-element.381, s32[512]{0:T(512)S(1)} %get-tuple-element.379, s32[2048]{0:T(1024)S(1)} %add_select_fusion.5, ...), kind=kOutput, calls=%fused_computation.10.clone.1 | convolution fusion | flops 48234496 | bytes 98304 | tf_op jit(solution)/shard_map/while/body/eval_jaxpr/dot_general | solution.py:64
  442.4 17.0 %fusion.82 = f32[12,512]{1,0:T(8,128)S(1)} fusion(bf16[12,2048]{1,0:T(8,128)(2,1)S(1)} %reshape.197, s32[512]{0:T(512)S(1)} %get-tuple-element.385, s32[512]{0:T(512)S(1)} %get-tuple-element.383, s32[512]{0:T(512)S(1)} %get-tuple-element.381, s32[512]{0:T(512)S(1)} %get-tuple-element.379, s32[2048]{0:T(1024)S(1)} %add_select_fusion.5, ...), kind=kOutput, calls=%fused_computation.11.clone.1 | convolution fusion | flops 48234496 | bytes 98304 | tf_op jit(solution)/shard_map/while/body/eval_jaxpr/dot_general | solution.py:65
  459.4 16.9 %fusion.83 = f32[12,512]{1,0:T(8,128)S(1)} fusion(bf16[12,2048]{1,0:T(8,128)(2,1)S(1)} %reshape.197, s32[512]{0:T(512)S(1)} %get-tuple-element.385, s32[512]{0:T(512)S(1)} %get-tuple-element.383, s32[512]{0:T(512)S(1)} %get-tuple-element.381, s32[512]{0:T(512)S(1)} %get-tuple-element.379, s32[2048]{0:T(1024)S(1)} %add_select_fusion.5, ...), kind=kOutput, calls=%fused_computation.10.clone.1 | convolution fusion | flops 48234496 | bytes 98304 | tf_op jit(solution)/shard_map/while/body/eval_jaxpr/dot_general | solution.py:64
  478.6 17.0 %fusion.82 = f32[12,512]{1,0:T(8,128)S(1)} fusion(bf16[12,2048]{1,0:T(8,128)(2,1)S(1)} %reshape.197, s32[512]{0:T(512)S(1)} %get-tuple-element.385, s32[512]{0:T(512)S(1)} %get-tuple-element.383, s32[512]{0:T(512)S(1)} %get-tuple-element.381, s32[512]{0:T(512)S(1)} %get-tuple-element.379, s32[2048]{0:T(1024)S(1)} %add_select_fusion.5, ...), kind=kOutput, calls=%fused_computation.11.clone.1 | convolution fusion | flops 48234496 | bytes 98304 | tf_op jit(solution)/shard_map/while/body/eval_jaxpr/dot_general | solution.py:65
  495.6 16.9 %fusion.83 = f32[12,512]{1,0:T(8,128)S(1)} fusion(bf16[12,2048]{1,0:T(8,128)(2,1)S(1)} %reshape.197, s32[512]{0:T(512)S(1)} %get-tuple-element.385, s32[512]{0:T(512)S(1)} %get-tuple-element.383, s32[512]{0:T(512)S(1)} %get-tuple-element.381, s32[512]{0:T(512)S(1)} %get-tuple-element.379, s32[2048]{0:T(1024)S(1)} %add_select_fusion.5, ...), kind=kOutput, calls=%fused_computation.10.clone.1 | convolution fusion | flops 48234496 | bytes 98304 | tf_op jit(solution)/shard_map/while/body/eval_jaxpr/dot_general | solution.py:64
  514.7 17.0 %fusion.82 = f32[12,512]{1,0:T(8,128)S(1)} fusion(bf16[12,2048]{1,0:T(8,128)(2,1)S(1)} %reshape.197, s32[512]{0:T(512)S(1)} %get-tuple-element.385, s32[512]{0:T(512)S(1)} %get-tuple-element.383, s32[512]{0:T(512)S(1)} %get-tuple-element.381, s32[512]{0:T(512)S(1)} %get-tuple-element.379, s32[2048]{0:T(1024)S(1)} %add_select_fusion.5, ...), kind=kOutput, calls=%fused_computation.11.clone.1 | convolution fusion | flops 48234496 | bytes 98304 | tf_op jit(solution)/shard_map/while/body/eval_jaxpr/dot_general | solution.py:65
  531.7 16.9 %fusion.83 = f32[12,512]{1,0:T(8,128)S(1)} fusion(bf16[12,2048]{1,0:T(8,128)(2,1)S(1)} %reshape.197, s32[512]{0:T(512)S(1)} %get-tuple-element.385, s32[512]{0:T(512)S(1)} %get-tuple-element.383, s32[512]{0:T(512)S(1)} %get-tuple-element.381, s32[512]{0:T(512)S(1)} %get-tuple-element.379, s32[2048]{0:T(1024)S(1)} %add_select_fusion.5, ...), kind=kOutput, calls=%fused_computation.10.clone.1 | convolution fusion | flops 48234496 | bytes 98304 | tf_op jit(solution)/shard_map/while/body/eval_jaxpr/dot_general | solution.py:64
  550.9 17.0 %fusion.82 = f32[12,512]{1,0:T(8,128)S(1)} fusion(bf16[12,2048]{1,0:T(8,128)(2,1)S(1)} %reshape.197, s32[512]{0:T(512)S(1)} %get-tuple-element.385, s32[512]{0:T(512)S(1)} %get-tuple-element.383, s32[512]{0:T(512)S(1)} %get-tuple-element.381, s32[512]{0:T(512)S(1)} %get-tuple-element.379, s32[2048]{0:T(1024)S(1)} %add_select_fusion.5, ...), kind=kOutput, calls=%fused_computation.11.clone.1 | convolution fusion | flops 48234496 | bytes 98304 | tf_op jit(solution)/shard_map/while/body/eval_jaxpr/dot_general | solution.py:65
  567.9 16.9 %fusion.83 = f32[12,512]{1,0:T(8,128)S(1)} fusion(bf16[12,2048]{1,0:T(8,128)(2,1)S(1)} %reshape.197, s32[512]{0:T(512)S(1)} %get-tuple-element.385, s32[512]{0:T(512)S(1)} %get-tuple-element.383, s32[512]{0:T(512)S(1)} %get-tuple-element.381, s32[512]{0:T(512)S(1)} %get-tuple-element.379, s32[2048]{0:T(1024)S(1)} %add_select_fusion.5, ...), kind=kOutput, calls=%fused_computation.10.clone.1 | convolution fusion | flops 48234496 | bytes 98304 | tf_op jit(solution)/shard_map/while/body/eval_jaxpr/dot_general | solution.py:64
  587.0 17.0 %fusion.82 = f32[12,512]{1,0:T(8,128)S(1)} fusion(bf16[12,2048]{1,0:T(8,128)(2,1)S(1)} %reshape.197, s32[512]{0:T(512)S(1)} %get-tuple-element.385, s32[512]{0:T(512)S(1)} %get-tuple-element.383, s32[512]{0:T(512)S(1)} %get-tuple-element.381, s32[512]{0:T(512)S(1)} %get-tuple-element.379, s32[2048]{0:T(1024)S(1)} %add_select_fusion.5, ...), kind=kOutput, calls=%fused_computation.11.clone.1 | convolution fusion | flops 48234496 | bytes 98304 | tf_op jit(solution)/shard_map/while/body/eval_jaxpr/dot_general | solution.py:65
  604.0 16.9 %fusion.83 = f32[12,512]{1,0:T(8,128)S(1)} fusion(bf16[12,2048]{1,0:T(8,128)(2,1)S(1)} %reshape.197, s32[512]{0:T(512)S(1)} %get-tuple-element.385, s32[512]{0:T(512)S(1)} %get-tuple-element.383, s32[512]{0:T(512)S(1)} %get-tuple-element.381, s32[512]{0:T(512)S(1)} %get-tuple-element.379, s32[2048]{0:T(1024)S(1)} %add_select_fusion.5, ...), kind=kOutput, calls=%fused_computation.10.clone.1 | convolution fusion | flops 48234496 | bytes 98304 | tf_op jit(solution)/shard_map/while/body/eval_jaxpr/dot_general | solution.py:64
  623.2 17.0 %fusion.82 = f32[12,512]{1,0:T(8,128)S(1)} fusion(bf16[12,2048]{1,0:T(8,128)(2,1)S(1)} %reshape.197, s32[512]{0:T(512)S(1)} %get-tuple-element.385, s32[512]{0:T(512)S(1)} %get-tuple-element.383, s32[512]{0:T(512)S(1)} %get-tuple-element.381, s32[512]{0:T(512)S(1)} %get-tuple-element.379, s32[2048]{0:T(1024)S(1)} %add_select_fusion.5, ...), kind=kOutput, calls=%fused_computation.11.clone.1 | convolution fusion | flops 48234496 | bytes 98304 | tf_op jit(solution)/shard_map/while/body/eval_jaxpr/dot_general | solution.py:65
  640.2 16.9 %fusion.83 = f32[12,512]{1,0:T(8,128)S(1)} fusion(bf16[12,2048]{1,0:T(8,128)(2,1)S(1)} %reshape.197, s32[512]{0:T(512)S(1)} %get-tuple-element.385, s32[512]{0:T(512)S(1)} %get-tuple-element.383, s32[512]{0:T(512)S(1)} %get-tuple-element.381, s32[512]{0:T(512)S(1)} %get-tuple-element.379, s32[2048]{0:T(1024)S(1)} %add_select_fusion.5, ...), kind=kOutput, calls=%fused_computation.10.clone.1 | convolution fusion | flops 48234496 | bytes 98304 | tf_op jit(solution)/shard_map/while/body/eval_jaxpr/dot_general | solution.py:64
  659.3 17.0 %fusion.82 = f32[12,512]{1,0:T(8,128)S(1)} fusion(bf16[12,2048]{1,0:T(8,128)(2,1)S(1)} %reshape.197, s32[512]{0:T(512)S(1)} %get-tuple-element.385, s32[512]{0:T(512)S(1)} %get-tuple-element.383, s32[512]{0:T(512)S(1)} %get-tuple-element.381, s32[512]{0:T(512)S(1)} %get-tuple-element.379, s32[2048]{0:T(1024)S(1)} %add_select_fusion.5, ...), kind=kOutput, calls=%fused_computation.11.clone.1 | convolution fusion | flops 48234496 | bytes 98304 | tf_op jit(solution)/shard_map/while/body/eval_jaxpr/dot_general | solution.py:65
  676.3 16.9 %fusion.83 = f32[12,512]{1,0:T(8,128)S(1)} fusion(bf16[12,2048]{1,0:T(8,128)(2,1)S(1)} %reshape.197, s32[512]{0:T(512)S(1)} %get-tuple-element.385, s32[512]{0:T(512)S(1)} %get-tuple-element.383, s32[512]{0:T(512)S(1)} %get-tuple-element.381, s32[512]{0:T(512)S(1)} %get-tuple-element.379, s32[2048]{0:T(1024)S(1)} %add_select_fusion.5, ...), kind=kOutput, calls=%fused_computation.10.clone.1 | convolution fusion | flops 48234496 | bytes 98304 | tf_op jit(solution)/shard_map/while/body/eval_jaxpr/dot_general | solution.py:64
  695.5 17.0 %fusion.82 = f32[12,512]{1,0:T(8,128)S(1)} fusion(bf16[12,2048]{1,0:T(8,128)(2,1)S(1)} %reshape.197, s32[512]{0:T(512)S(1)} %get-tuple-element.385, s32[512]{0:T(512)S(1)} %get-tuple-element.383, s32[512]{0:T(512)S(1)} %get-tuple-element.381, s32[512]{0:T(512)S(1)} %get-tuple-element.379, s32[2048]{0:T(1024)S(1)} %add_select_fusion.5, ...), kind=kOutput, calls=%fused_computation.11.clone.1 | convolution fusion | flops 48234496 | bytes 98304 | tf_op jit(solution)/shard_map/while/body/eval_jaxpr/dot_general | solution.py:65
  712.5 16.9 %fusion.83 = f32[12,512]{1,0:T(8,128)S(1)} fusion(bf16[12,2048]{1,0:T(8,128)(2,1)S(1)} %reshape.197, s32[512]{0:T(512)S(1)} %get-tuple-element.385, s32[512]{0:T(512)S(1)} %get-tuple-element.383, s32[512]{0:T(512)S(1)} %get-tuple-element.381, s32[512]{0:T(512)S(1)} %get-tuple-element.379, s32[2048]{0:T(1024)S(1)} %add_select_fusion.5, ...), kind=kOutput, calls=%fused_computation.10.clone.1 | convolution fusion | flops 48234496 | bytes 98304 | tf_op jit(solution)/shard_map/while/body/eval_jaxpr/dot_general | solution.py:64
  731.6 17.0 %fusion.82 = f32[12,512]{1,0:T(8,128)S(1)} fusion(bf16[12,2048]{1,0:T(8,128)(2,1)S(1)} %reshape.197, s32[512]{0:T(512)S(1)} %get-tuple-element.385, s32[512]{0:T(512)S(1)} %get-tuple-element.383, s32[512]{0:T(512)S(1)} %get-tuple-element.381, s32[512]{0:T(512)S(1)} %get-tuple-element.379, s32[2048]{0:T(1024)S(1)} %add_select_fusion.5, ...), kind=kOutput, calls=%fused_computation.11.clone.1 | convolution fusion | flops 48234496 | bytes 98304 | tf_op jit(solution)/shard_map/while/body/eval_jaxpr/dot_general | solution.py:65
  748.6 16.9 %fusion.83 = f32[12,512]{1,0:T(8,128)S(1)} fusion(bf16[12,2048]{1,0:T(8,128)(2,1)S(1)} %reshape.197, s32[512]{0:T(512)S(1)} %get-tuple-element.385, s32[512]{0:T(512)S(1)} %get-tuple-element.383, s32[512]{0:T(512)S(1)} %get-tuple-element.381, s32[512]{0:T(512)S(1)} %get-tuple-element.379, s32[2048]{0:T(1024)S(1)} %add_select_fusion.5, ...), kind=kOutput, calls=%fused_computation.10.clone.1 | convolution fusion | flops 48234496 | bytes 98304 | tf_op jit(solution)/shard_map/while/body/eval_jaxpr/dot_general | solution.py:64
  767.8 17.0 %fusion.82 = f32[12,512]{1,0:T(8,128)S(1)} fusion(bf16[12,2048]{1,0:T(8,128)(2,1)S(1)} %reshape.197, s32[512]{0:T(512)S(1)} %get-tuple-element.385, s32[512]{0:T(512)S(1)} %get-tuple-element.383, s32[512]{0:T(512)S(1)} %get-tuple-element.381, s32[512]{0:T(512)S(1)} %get-tuple-element.379, s32[2048]{0:T(1024)S(1)} %add_select_fusion.5, ...), kind=kOutput, calls=%fused_computation.11.clone.1 | convolution fusion | flops 48234496 | bytes 98304 | tf_op jit(solution)/shard_map/while/body/eval_jaxpr/dot_general | solution.py:65
  784.7 16.9 %fusion.83 = f32[12,512]{1,0:T(8,128)S(1)} fusion(bf16[12,2048]{1,0:T(8,128)(2,1)S(1)} %reshape.197, s32[512]{0:T(512)S(1)} %get-tuple-element.385, s32[512]{0:T(512)S(1)} %get-tuple-element.383, s32[512]{0:T(512)S(1)} %get-tuple-element.381, s32[512]{0:T(512)S(1)} %get-tuple-element.379, s32[2048]{0:T(1024)S(1)} %add_select_fusion.5, ...), kind=kOutput, calls=%fused_computation.10.clone.1 | convolution fusion | flops 48234496 | bytes 98304 | tf_op jit(solution)/shard_map/while/body/eval_jaxpr/dot_general | solution.py:64
  803.9 17.0 %fusion.82 = f32[12,512]{1,0:T(8,128)S(1)} fusion(bf16[12,2048]{1,0:T(8,128)(2,1)S(1)} %reshape.197, s32[512]{0:T(512)S(1)} %get-tuple-element.385, s32[512]{0:T(512)S(1)} %get-tuple-element.383, s32[512]{0:T(512)S(1)} %get-tuple-element.381, s32[512]{0:T(512)S(1)} %get-tuple-element.379, s32[2048]{0:T(1024)S(1)} %add_select_fusion.5, ...), kind=kOutput, calls=%fused_computation.11.clone.1 | convolution fusion | flops 48234496 | bytes 98304 | tf_op jit(solution)/shard_map/while/body/eval_jaxpr/dot_general | solution.py:65
  820.9 16.9 %fusion.83 = f32[12,512]{1,0:T(8,128)S(1)} fusion(bf16[12,2048]{1,0:T(8,128)(2,1)S(1)} %reshape.197, s32[512]{0:T(512)S(1)} %get-tuple-element.385, s32[512]{0:T(512)S(1)} %get-tuple-element.383, s32[512]{0:T(512)S(1)} %get-tuple-element.381, s32[512]{0:T(512)S(1)} %get-tuple-element.379, s32[2048]{0:T(1024)S(1)} %add_select_fusion.5, ...), kind=kOutput, calls=%fused_computation.10.clone.1 | convolution fusion | flops 48234496 | bytes 98304 | tf_op jit(solution)/shard_map/while/body/eval_jaxpr/dot_general | solution.py:64
  840.1 17.0 %fusion.82 = f32[12,512]{1,0:T(8,128)S(1)} fusion(bf16[12,2048]{1,0:T(8,128)(2,1)S(1)} %reshape.197, s32[512]{0:T(512)S(1)} %get-tuple-element.385, s32[512]{0:T(512)S(1)} %get-tuple-element.383, s32[512]{0:T(512)S(1)} %get-tuple-element.381, s32[512]{0:T(512)S(1)} %get-tuple-element.379, s32[2048]{0:T(1024)S(1)} %add_select_fusion.5, ...), kind=kOutput, calls=%fused_computation.11.clone.1 | convolution fusion | flops 48234496 | bytes 98304 | tf_op jit(solution)/shard_map/while/body/eval_jaxpr/dot_general | solution.py:65
  857.0 16.9 %fusion.83 = f32[12,512]{1,0:T(8,128)S(1)} fusion(bf16[12,2048]{1,0:T(8,128)(2,1)S(1)} %reshape.197, s32[512]{0:T(512)S(1)} %get-tuple-element.385, s32[512]{0:T(512)S(1)} %get-tuple-element.383, s32[512]{0:T(512)S(1)} %get-tuple-element.381, s32[512]{0:T(512)S(1)} %get-tuple-element.379, s32[2048]{0:T(1024)S(1)} %add_select_fusion.5, ...), kind=kOutput, calls=%fused_computation.10.clone.1 | convolution fusion | flops 48234496 | bytes 98304 | tf_op jit(solution)/shard_map/while/body/eval_jaxpr/dot_general | solution.py:64
  876.2 17.0 %fusion.82 = f32[12,512]{1,0:T(8,128)S(1)} fusion(bf16[12,2048]{1,0:T(8,128)(2,1)S(1)} %reshape.197, s32[512]{0:T(512)S(1)} %get-tuple-element.385, s32[512]{0:T(512)S(1)} %get-tuple-element.383, s32[512]{0:T(512)S(1)} %get-tuple-element.381, s32[512]{0:T(512)S(1)} %get-tuple-element.379, s32[2048]{0:T(1024)S(1)} %add_select_fusion.5, ...), kind=kOutput, calls=%fused_computation.11.clone.1 | convolution fusion | flops 48234496 | bytes 98304 | tf_op jit(solution)/shard_map/while/body/eval_jaxpr/dot_general | solution.py:65
  893.2 16.9 %fusion.83 = f32[12,512]{1,0:T(8,128)S(1)} fusion(bf16[12,2048]{1,0:T(8,128)(2,1)S(1)} %reshape.197, s32[512]{0:T(512)S(1)} %get-tuple-element.385, s32[512]{0:T(512)S(1)} %get-tuple-element.383, s32[512]{0:T(512)S(1)} %get-tuple-element.381, s32[512]{0:T(512)S(1)} %get-tuple-element.379, s32[2048]{0:T(1024)S(1)} %add_select_fusion.5, ...), kind=kOutput, calls=%fused_computation.10.clone.1 | convolution fusion | flops 48234496 | bytes 98304 | tf_op jit(solution)/shard_map/while/body/eval_jaxpr/dot_general | solution.py:64
  912.4 17.0 %fusion.82 = f32[12,512]{1,0:T(8,128)S(1)} fusion(bf16[12,2048]{1,0:T(8,128)(2,1)S(1)} %reshape.197, s32[512]{0:T(512)S(1)} %get-tuple-element.385, s32[512]{0:T(512)S(1)} %get-tuple-element.383, s32[512]{0:T(512)S(1)} %get-tuple-element.381, s32[512]{0:T(512)S(1)} %get-tuple-element.379, s32[2048]{0:T(1024)S(1)} %add_select_fusion.5, ...), kind=kOutput, calls=%fused_computation.11.clone.1 | convolution fusion | flops 48234496 | bytes 98304 | tf_op jit(solution)/shard_map/while/body/eval_jaxpr/dot_general | solution.py:65
  929.3 16.9 %fusion.83 = f32[12,512]{1,0:T(8,128)S(1)} fusion(bf16[12,2048]{1,0:T(8,128)(2,1)S(1)} %reshape.197, s32[512]{0:T(512)S(1)} %get-tuple-element.385, s32[512]{0:T(512)S(1)} %get-tuple-element.383, s32[512]{0:T(512)S(1)} %get-tuple-element.381, s32[512]{0:T(512)S(1)} %get-tuple-element.379, s32[2048]{0:T(1024)S(1)} %add_select_fusion.5, ...), kind=kOutput, calls=%fused_computation.10.clone.1 | convolution fusion | flops 48234496 | bytes 98304 | tf_op jit(solution)/shard_map/while/body/eval_jaxpr/dot_general | solution.py:64
  948.5 17.0 %fusion.82 = f32[12,512]{1,0:T(8,128)S(1)} fusion(bf16[12,2048]{1,0:T(8,128)(2,1)S(1)} %reshape.197, s32[512]{0:T(512)S(1)} %get-tuple-element.385, s32[512]{0:T(512)S(1)} %get-tuple-element.383, s32[512]{0:T(512)S(1)} %get-tuple-element.381, s32[512]{0:T(512)S(1)} %get-tuple-element.379, s32[2048]{0:T(1024)S(1)} %add_select_fusion.5, ...), kind=kOutput, calls=%fused_computation.11.clone.1 | convolution fusion | flops 48234496 | bytes 98304 | tf_op jit(solution)/shard_map/while/body/eval_jaxpr/dot_general | solution.py:65
  965.5 16.9 %fusion.83 = f32[12,512]{1,0:T(8,128)S(1)} fusion(bf16[12,2048]{1,0:T(8,128)(2,1)S(1)} %reshape.197, s32[512]{0:T(512)S(1)} %get-tuple-element.385, s32[512]{0:T(512)S(1)} %get-tuple-element.383, s32[512]{0:T(512)S(1)} %get-tuple-element.381, s32[512]{0:T(512)S(1)} %get-tuple-element.379, s32[2048]{0:T(1024)S(1)} %add_select_fusion.5, ...), kind=kOutput, calls=%fused_computation.10.clone.1 | convolution fusion | flops 48234496 | bytes 98304 | tf_op jit(solution)/shard_map/while/body/eval_jaxpr/dot_general | solution.py:64
  984.6 17.0 %fusion.82 = f32[12,512]{1,0:T(8,128)S(1)} fusion(bf16[12,2048]{1,0:T(8,128)(2,1)S(1)} %reshape.197, s32[512]{0:T(512)S(1)} %get-tuple-element.385, s32[512]{0:T(512)S(1)} %get-tuple-element.383, s32[512]{0:T(512)S(1)} %get-tuple-element.381, s32[512]{0:T(512)S(1)} %get-tuple-element.379, s32[2048]{0:T(1024)S(1)} %add_select_fusion.5, ...), kind=kOutput, calls=%fused_computation.11.clone.1 | convolution fusion | flops 48234496 | bytes 98304 | tf_op jit(solution)/shard_map/while/body/eval_jaxpr/dot_general | solution.py:65
  1020.8 17.0 %fusion.82 = f32[12,512]{1,0:T(8,128)S(1)} fusion(bf16[12,2048]{1,0:T(8,128)(2,1)S(1)} %reshape.197, s32[512]{0:T(512)S(1)} %get-tuple-element.385, s32[512]{0:T(512)S(1)} %get-tuple-element.383, s32[512]{0:T(512)S(1)} %get-tuple-element.381, s32[512]{0:T(512)S(1)} %get-tuple-element.379, s32[2048]{0:T(1024)S(1)} %add_select_fusion.5, ...), kind=kOutput, calls=%fused_computation.11.clone.1 | convolution fusion | flops 48234496 | bytes 98304 | tf_op jit(solution)/shard_map/while/body/eval_jaxpr/dot_general | solution.py:65
  1056.9 17.0 %fusion.82 = f32[12,512]{1,0:T(8,128)S(1)} fusion(bf16[12,2048]{1,0:T(8,128)(2,1)S(1)} %reshape.197, s32[512]{0:T(512)S(1)} %get-tuple-element.385, s32[512]{0:T(512)S(1)} %get-tuple-element.383, s32[512]{0:T(512)S(1)} %get-tuple-element.381, s32[512]{0:T(512)S(1)} %get-tuple-element.379, s32[2048]{0:T(1024)S(1)} %add_select_fusion.5, ...), kind=kOutput, calls=%fused_computation.11.clone.1 | convolution fusion | flops 48234496 | bytes 98304 | tf_op jit(solution)/shard_map/while/body/eval_jaxpr/dot_general | solution.py:65
  1093.1 17.0 %fusion.82 = f32[12,512]{1,0:T(8,128)S(1)} fusion(bf16[12,2048]{1,0:T(8,128)(2,1)S(1)} %reshape.197, s32[512]{0:T(512)S(1)} %get-tuple-element.385, s32[512]{0:T(512)S(1)} %get-tuple-element.383, s32[512]{0:T(512)S(1)} %get-tuple-element.381, s32[512]{0:T(512)S(1)} %get-tuple-element.379, s32[2048]{0:T(1024)S(1)} %add_select_fusion.5, ...), kind=kOutput, calls=%fused_computation.11.clone.1 | convolution fusion | flops 48234496 | bytes 98304 | tf_op jit(solution)/shard_map/while/body/eval_jaxpr/dot_general | solution.py:65
  1110.1 16.9 %fusion.83 = f32[12,512]{1,0:T(8,128)S(1)} fusion(bf16[12,2048]{1,0:T(8,128)(2,1)S(1)} %reshape.197, s32[512]{0:T(512)S(1)} %get-tuple-element.385, s32[512]{0:T(512)S(1)} %get-tuple-element.383, s32[512]{0:T(512)S(1)} %get-tuple-element.381, s32[512]{0:T(512)S(1)} %get-tuple-element.379, s32[2048]{0:T(1024)S(1)} %add_select_fusion.5, ...), kind=kOutput, calls=%fused_computation.10.clone.1 | convolution fusion | flops 48234496 | bytes 98304 | tf_op jit(solution)/shard_map/while/body/eval_jaxpr/dot_general | solution.py:64
  1129.2 17.0 %fusion.82 = f32[12,512]{1,0:T(8,128)S(1)} fusion(bf16[12,2048]{1,0:T(8,128)(2,1)S(1)} %reshape.197, s32[512]{0:T(512)S(1)} %get-tuple-element.385, s32[512]{0:T(512)S(1)} %get-tuple-element.383, s32[512]{0:T(512)S(1)} %get-tuple-element.381, s32[512]{0:T(512)S(1)} %get-tuple-element.379, s32[2048]{0:T(1024)S(1)} %add_select_fusion.5, ...), kind=kOutput, calls=%fused_computation.11.clone.1 | convolution fusion | flops 48234496 | bytes 98304 | tf_op jit(solution)/shard_map/while/body/eval_jaxpr/dot_general | solution.py:65
  1146.2 16.9 %fusion.83 = f32[12,512]{1,0:T(8,128)S(1)} fusion(bf16[12,2048]{1,0:T(8,128)(2,1)S(1)} %reshape.197, s32[512]{0:T(512)S(1)} %get-tuple-element.385, s32[512]{0:T(512)S(1)} %get-tuple-element.383, s32[512]{0:T(512)S(1)} %get-tuple-element.381, s32[512]{0:T(512)S(1)} %get-tuple-element.379, s32[2048]{0:T(1024)S(1)} %add_select_fusion.5, ...), kind=kOutput, calls=%fused_computation.10.clone.1 | convolution fusion | flops 48234496 | bytes 98304 | tf_op jit(solution)/shard_map/while/body/eval_jaxpr/dot_general | solution.py:64
  1165.4 17.0 %fusion.82 = f32[12,512]{1,0:T(8,128)S(1)} fusion(bf16[12,2048]{1,0:T(8,128)(2,1)S(1)} %reshape.197, s32[512]{0:T(512)S(1)} %get-tuple-element.385, s32[512]{0:T(512)S(1)} %get-tuple-element.383, s32[512]{0:T(512)S(1)} %get-tuple-element.381, s32[512]{0:T(512)S(1)} %get-tuple-element.379, s32[2048]{0:T(1024)S(1)} %add_select_fusion.5, ...), kind=kOutput, calls=%fused_computation.11.clone.1 | convolution fusion | flops 48234496 | bytes 98304 | tf_op jit(solution)/shard_map/while/body/eval_jaxpr/dot_general | solution.py:65
  1182.4 16.9 %fusion.83 = f32[12,512]{1,0:T(8,128)S(1)} fusion(bf16[12,2048]{1,0:T(8,128)(2,1)S(1)} %reshape.197, s32[512]{0:T(512)S(1)} %get-tuple-element.385, s32[512]{0:T(512)S(1)} %get-tuple-element.383, s32[512]{0:T(512)S(1)} %get-tuple-element.381, s32[512]{0:T(512)S(1)} %get-tuple-element.379, s32[2048]{0:T(1024)S(1)} %add_select_fusion.5, ...), kind=kOutput, calls=%fused_computation.10.clone.1 | convolution fusion | flops 48234496 | bytes 98304 | tf_op jit(solution)/shard_map/while/body/eval_jaxpr/dot_general | solution.py:64
  1201.5 17.0 %fusion.82 = f32[12,512]{1,0:T(8,128)S(1)} fusion(bf16[12,2048]{1,0:T(8,128)(2,1)S(1)} %reshape.197, s32[512]{0:T(512)S(1)} %get-tuple-element.385, s32[512]{0:T(512)S(1)} %get-tuple-element.383, s32[512]{0:T(512)S(1)} %get-tuple-element.381, s32[512]{0:T(512)S(1)} %get-tuple-element.379, s32[2048]{0:T(1024)S(1)} %add_select_fusion.5, ...), kind=kOutput, calls=%fused_computation.11.clone.1 | convolution fusion | flops 48234496 | bytes 98304 | tf_op jit(solution)/shard_map/while/body/eval_jaxpr/dot_general | solution.py:65
  1218.5 16.9 %fusion.83 = f32[12,512]{1,0:T(8,128)S(1)} fusion(bf16[12,2048]{1,0:T(8,128)(2,1)S(1)} %reshape.197, s32[512]{0:T(512)S(1)} %get-tuple-element.385, s32[512]{0:T(512)S(1)} %get-tuple-element.383, s32[512]{0:T(512)S(1)} %get-tuple-element.381, s32[512]{0:T(512)S(1)} %get-tuple-element.379, s32[2048]{0:T(1024)S(1)} %add_select_fusion.5, ...), kind=kOutput, calls=%fused_computation.10.clone.1 | convolution fusion | flops 48234496 | bytes 98304 | tf_op jit(solution)/shard_map/while/body/eval_jaxpr/dot_general | solution.py:64
  1237.7 17.0 %fusion.82 = f32[12,512]{1,0:T(8,128)S(1)} fusion(bf16[12,2048]{1,0:T(8,128)(2,1)S(1)} %reshape.197, s32[512]{0:T(512)S(1)} %get-tuple-element.385, s32[512]{0:T(512)S(1)} %get-tuple-element.383, s32[512]{0:T(512)S(1)} %get-tuple-element.381, s32[512]{0:T(512)S(1)} %get-tuple-element.379, s32[2048]{0:T(1024)S(1)} %add_select_fusion.5, ...), kind=kOutput, calls=%fused_computation.11.clone.1 | convolution fusion | flops 48234496 | bytes 98304 | tf_op jit(solution)/shard_map/while/body/eval_jaxpr/dot_general | solution.py:65
  1254.7 16.9 %fusion.83 = f32[12,512]{1,0:T(8,128)S(1)} fusion(bf16[12,2048]{1,0:T(8,128)(2,1)S(1)} %reshape.197, s32[512]{0:T(512)S(1)} %get-tuple-element.385, s32[512]{0:T(512)S(1)} %get-tuple-element.383, s32[512]{0:T(512)S(1)} %get-tuple-element.381, s32[512]{0:T(512)S(1)} %get-tuple-element.379, s32[2048]{0:T(1024)S(1)} %add_select_fusion.5, ...), kind=kOutput, calls=%fused_computation.10.clone.1 | convolution fusion | flops 48234496 | bytes 98304 | tf_op jit(solution)/shard_map/while/body/eval_jaxpr/dot_general | solution.py:64
  (250 shorter events, 165.8 us)
Async XLA Ops:
  2.0 11.4 collective-permute-start
  12.6 0.7 copy-start.6
  43.3 10.8 copy-start.7
  43.3 10.8 copy-start.8
  46.4 41.6 %all-to-all-start = ((bf16[512,2,6,128]{3,1,2,0:T(2,128)(2,1)}), bf16[512,2,6,128]{3,1,2,0:T(2,128)(2,1)S(1)}, u32[]{:S(2)}, u32[]{:S(2)}) async-start(bf16[512,2,6,128]{3,1,2,0:T(2,128)(2,1)} %copy.47), calls=%async_computation | async-start | bytes 3145728 | tf_op jit(solution)/shard_map/all_to_all | solution.py:114
  88.3 3.3 copy-start.5
  1280.0 20.2 %copy-start.9 = (f32[32]{0:T(128)S(1)}, f32[32]{0:T(128)}, u32[]{:S(2)}) copy-start(f32[32]{0:T(128)} %param.13) | copy-start | bytes 388
  1283.4 19.1 %all-to-all-start.1 = ((bf16[16,2,6144]{2,1,0:T(2,128)(2,1)}), bf16[16,2,6144]{2,1,0:T(2,128)(2,1)S(1)}, u32[]{:S(2)}, u32[]{:S(2)}) async-start(bf16[16,2,6144]{2,1,0:T(2,128)(2,1)} %reshape.194), calls=%async_computation.1 | async-start | bytes 786432 | tf_op jit(solution)/shard_map/all_to_all | solution.py:118
  1305.9 6.0 copy-start.3
  1305.9 6.0 copy-start.4
  1309.1 3.2 copy-start
  1309.1 3.2 copy-start.1
  1311.9 1.2 copy-start.2
where the time goes:
time: 1330 us; the launch traced here: 1320 us
  matrix products  1120 us (84%)
  local copies, waits for them, and re-layouts  71.9 us (5%)
  loops' own time  55.3 us (4%)
  waiting for transfers between devices  35.1 us (3%)
  other arithmetic  20.9 us (2%)
  starting transfers between devices  17.4 us (1%)
    dot_general x32, matrix products, one_channel(): with_imag = jnp.dot(stacked, w_imag, preferred_element_type=jnp.float32)  543 us
    dot_general x32, matrix products, one_channel(): with_real = jnp.dot(stacked, w_real, preferred_element_type=jnp.float32)  539 us
    another operation x1, loops' own time, beamform(): return lax.map(one_channel, (turned, offsets))  55.3 us
    dynamic_slice x64, local copies, waits for them, and re-layouts, beamform(): return lax.map(one_channel, (turned, offsets))  48.6 us
    all_to_all x1, waiting for transfers between devices, body(): lax.all_to_all(spectra_of(filtered, basis), 'feed', split_axis=0, concat_...  33.8 us
    dot_general x1, matrix products, spectra_of(): jnp.dot(flat, basis, precision=lax.Precision.HIGHEST, preferred_element_t...  29.6 us
  transfers between devices with their start and end apart: 3, of which 2 were waited for; matrix products, arithmetic and copies ran while one was open for 1% of the time, Pallas kernels for 0%

commit v1 on v0

--- a/solution.py
+++ b/solution.py
@@ -1,8 +1,13 @@
+import functools
 import math
 
 import jax
 import jax.numpy as jnp
+import ml_dtypes
+import numpy as np
 from jax import lax
+from jax.experimental import pallas as pl
+from jax.experimental.pallas import tpu as pltpu
 from jax.sharding import PartitionSpec as P
 
 FEEDS = 2048
@@ -86,7 +91,7 @@
     return result.reshape(beams_here, batch_frames, 2 * nchan)
 
 
-def body(samples, filter_taps, feed_cylinder, feed_delay, pointing, chirp_rate):
+def plain_body(samples, filter_taps, feed_cylinder, feed_delay, pointing, chirp_rate):
     length = 2 * NCHAN
     feed_here = samples.shape[0]
     frames_here = samples.shape[1] // length
@@ -120,11 +125,447 @@
     return series
 
 
+LANES = 128
+HALVES = 2
+GROUP = ("near", "tm")
+VMEM = pltpu.CompilerParams(vmem_limit_bytes=56 * 1024 * 1024)
+
+
+def split_bf16(table):
+    high = table.astype(ml_dtypes.bfloat16)
+    low = (table - high.astype(np.float64)).astype(ml_dtypes.bfloat16)
+    return np.stack([high, low])
+
+
+def folded_forward_basis(length):
+    half = length // 2
+    tables = []
+    for parity in range(2):
+        channel = 2 * np.arange(half // 2)[:, None] + parity
+        angle = (channel * np.arange(half)[None, :] % length) * (2.0 * np.pi / length)
+        rows = np.concatenate([np.cos(angle), -np.sin(angle)], axis=0) / math.sqrt(length)
+        tables.append(split_bf16(rows))
+    return np.stack(tables)
+
+
+def folded_inverse_basis(nchan, lane_channels):
+    kappas = nchan // 2 // lane_channels
+    times = np.arange(nchan // 2)[None, :]
+    tables = []
+    for parity in range(2):
+        rows = []
+        for sub in range(lane_channels):
+            channel = 2 * (lane_channels * np.arange(kappas)[:, None] + sub) + parity
+            angle = (channel * times % nchan) * (2.0 * np.pi / nchan)
+            rows.append(np.concatenate([np.cos(angle), np.sin(angle)], axis=1))
+            rows.append(np.concatenate([-np.sin(angle), np.cos(angle)], axis=1))
+        tables.append(split_bf16(np.concatenate(rows, axis=0) / math.sqrt(nchan)))
+    return np.stack(tables)
+
+
+def dot_nt(left, right):
+    return lax.dot_general(
+        left, right, (((1,), (1,)), ((), ())), preferred_element_type=jnp.float32
+    )
+
+
+def spectra_kernel(frames_here, samples_ref, tail_ref, taps_ref, basis_ref, out_ref, folded, rows):
+    feed_here = samples_ref.shape[0]
+    length = taps_ref.shape[1]
+    half = length // 2
+
+    def frame(index, start):
+        lanes = pl.ds((index % frames_here) * length + start, LANES)
+        if index < 0:
+            lanes = pl.ds((index + TAPS - 1) * length + start, LANES)
+            return tail_ref[:, lanes].astype(jnp.float32)
+        return samples_ref[:, lanes].astype(jnp.float32)
+
+    def filtered(index, start):
+        total = None
+        for tap in range(TAPS):
+            term = taps_ref[tap : tap + 1, start : start + LANES] * frame(
+                index + tap - (TAPS - 1), start
+            )
+            total = term if total is None else total + term
+        return total
+
+    for index in range(frames_here):
+        where = pl.ds(index * feed_here, feed_here)
+        for start in range(0, half, LANES):
+            near = filtered(index, start)
+            far = filtered(index, start + half)
+            for parity, value in enumerate((near + far, near - far)):
+                high = value.astype(jnp.bfloat16)
+                folded[parity, 0, where, start : start + LANES] = high
+                folded[parity, 1, where, start : start + LANES] = (
+                    value - high.astype(jnp.float32)
+                ).astype(jnp.bfloat16)
+
+    per_channel = 2 * frames_here
+    together = 2
+    for parity in range(2):
+        for first in range(0, frames_here, together):
+            where = pl.ds(first * feed_here, together * feed_here)
+            high = folded[parity, 0, where, :]
+            low = folded[parity, 1, where, :]
+            result = (
+                dot_nt(basis_ref[parity, 0], high)
+                + dot_nt(basis_ref[parity, 1], high)
+                + dot_nt(basis_ref[parity, 0], low)
+            )
+            count = half // 2
+            for part in range(2):
+                for ahead in range(together):
+                    start = parity * count * per_channel + part * frames_here + first + ahead
+                    rows[pl.ds(start, count, stride=per_channel), :] = result[
+                        part * count : (part + 1) * count,
+                        ahead * feed_here : (ahead + 1) * feed_here,
+                    ]
+    out_ref[...] = rows[...].astype(jnp.bfloat16)
+
+
+def spectra_rows(samples, tail, taps, basis):
+    feed_here = samples.shape[0]
+    length = taps.shape[1]
+    frames_here = samples.shape[1] // length
+    total_rows = length * frames_here
+    return pl.pallas_call(
+        functools.partial(spectra_kernel, frames_here),
+        out_shape=jax.ShapeDtypeStruct((total_rows, feed_here), jnp.bfloat16),
+        scratch_shapes=[
+            pltpu.VMEM((2, 2, frames_here * feed_here, length // 2), jnp.bfloat16),
+            pltpu.VMEM((total_rows, feed_here), jnp.float32),
+        ],
+        compiler_params=VMEM,
+        name="spectra",
+    )(samples, tail, taps, basis)
+
+
+def sine_turns(turns):
+    square = turns * turns
+    total = None
+    for power in range(11, 0, -2):
+        factor = (2.0 * math.pi) ** power / math.factorial(power) * (-1) ** (power // 2)
+        total = factor if total is None else total * square + factor
+    return total * turns
+
+
+def unit_vector(turns):
+    cosine = sine_turns(0.25 - jnp.abs(turns))
+    sine = sine_turns(jnp.maximum(jnp.minimum(turns, 0.5 - turns), -0.5 - turns))
+    return cosine, sine
+
+
+def centred(turns):
+    return turns - jnp.floor(turns + 0.5)
+
+
+def weights_kernel(block_rows, step, first_ref, delay_ref, cylinder_ref, pointing_ref, out_ref):
+    channels, rows, width = out_ref.shape
+    beams = width // 2
+    repeat = beams // LANES
+    middle = channels // 2
+    first = (first_ref[0] + step * (middle - 1)).astype(jnp.float32)
+
+    def one_block(index, carry):
+        where = pl.ds(pl.multiple_of(index * block_rows, block_rows), block_rows)
+        delay = jnp.concatenate([delay_ref[where]] * repeat, axis=1)
+        cylinder = jnp.concatenate([cylinder_ref[where]] * repeat, axis=1)
+        steer = jnp.broadcast_to(pointing_ref[0:1, :], (block_rows, beams))
+        for other in range(1, CYL):
+            steer = jnp.where(cylinder == other, pointing_ref[other : other + 1, :], steer)
+        turns = centred(delay * steer * (1.0 / PHASES))
+        low_cos, low_sin = unit_vector(centred(first * turns))
+        step_cos, step_sin = unit_vector(centred(float(step) * turns))
+        high_cos = low_cos * step_cos - low_sin * step_sin
+        high_sin = low_cos * step_sin + low_sin * step_cos
+        twice = step_cos + step_cos
+
+        def put(channel, cosine, sine):
+            out_ref[channel, where, :beams] = cosine.astype(jnp.bfloat16)
+            out_ref[channel, where, beams:] = sine.astype(jnp.bfloat16)
+
+        put(middle - 1, low_cos, low_sin)
+        put(middle, high_cos, high_sin)
+        up = (low_cos, low_sin, high_cos, high_sin)
+        down = (high_cos, high_sin, low_cos, low_sin)
+        for away in range(1, middle):
+            up = (up[2], up[3], twice * up[2] - up[0], twice * up[3] - up[1])
+            down = (down[2], down[3], twice * down[2] - down[0], twice * down[3] - down[1])
+            put(middle + away, up[2], up[3])
+            put(middle - 1 - away, down[2], down[3])
+        return carry
+
+    lax.fori_loop(0, rows // block_rows, one_block, 0)
+
+
+def make_weights(first, delay, cylinder, pointing, channels, step):
+    feeds = delay.shape[0]
+    beams = pointing.shape[1]
+    rows = 128
+    return pl.pallas_call(
+        functools.partial(weights_kernel, 32, step),
+        grid=(feeds // rows,),
+        in_specs=[
+            pl.BlockSpec(memory_space=pltpu.SMEM),
+            pl.BlockSpec((rows, LANES), lambda i: (i, 0)),
+            pl.BlockSpec((rows, LANES), lambda i: (i, 0)),
+            pl.BlockSpec(pointing.shape, lambda i: (0, 0)),
+        ],
+        out_specs=pl.BlockSpec((channels, rows, 2 * beams), lambda i: (0, i, 0)),
+        out_shape=jax.ShapeDtypeStruct((channels, feeds, 2 * beams), jnp.bfloat16),
+        compiler_params=VMEM,
+        cost_estimate=pl.CostEstimate(
+            flops=channels * feeds * beams * 8,
+            bytes_accessed=channels * feeds * beams * 4,
+            transcendentals=0,
+        ),
+        name="weights",
+    )(first, delay, cylinder, pointing)
+
+
+def beams_kernel(layout, received_ref, weights_ref, out_ref, wide, lined):
+    near, cores, channels, frames_here = layout
+    together = weights_ref.shape[0]
+    beams = weights_ref.shape[2] // 2
+    per_source = 2 * frames_here
+    per_channel = per_source * cores
+    feed_here = received_ref.shape[1]
+
+    @pl.when(pl.program_id(0) == 0)
+    def _():
+        wide[...] = received_ref[...].astype(jnp.float32)
+        for place in range(near):
+            for core in range(cores):
+                base = (place * cores + core) * channels * per_source
+                for part in range(2):
+                    for index in range(frames_here):
+                        source = base + part * frames_here + index
+                        target = (part * cores + core) * frames_here + index
+                        lined[place, pl.ds(target, channels, stride=per_channel), :] = wide[
+                            pl.ds(source, channels, stride=per_source), :
+                        ]
+
+    half = per_channel // 2
+    for local in range(together):
+        start = pl.multiple_of((pl.program_id(0) * together + local) * per_channel, 8)
+        spectra = jnp.concatenate(
+            [lined[place, pl.ds(start, per_channel), :] for place in range(near)], axis=1
+        ).astype(jnp.bfloat16)
+        both = jnp.dot(spectra, weights_ref[local], preferred_element_type=jnp.float32)
+        by_real = both[:, :beams]
+        by_imag = both[:, beams:]
+        turned = jnp.concatenate([-by_imag[half:], by_imag[:half]], axis=0)
+        out_ref[local * per_channel : (local + 1) * per_channel, :] = (by_real + turned).astype(
+            out_ref.dtype
+        )
+
+
+def partial_beams(received, weights, layout, dtype):
+    near, cores, channels, frames_here = layout
+    feeds, width = weights.shape[1:]
+    per_channel = 2 * cores * frames_here
+    together = 4
+    return pl.pallas_call(
+        functools.partial(beams_kernel, layout),
+        grid=(channels // together,),
+        in_specs=[
+            pl.BlockSpec(received.shape, lambda i: (0, 0)),
+            pl.BlockSpec((together, feeds, width), lambda i: (i, 0, 0)),
+        ],
+        out_specs=pl.BlockSpec((together * per_channel, width // 2), lambda i: (i, 0)),
+        out_shape=jax.ShapeDtypeStruct((channels * per_channel, width // 2), dtype),
+        scratch_shapes=[
+            pltpu.VMEM(received.shape, jnp.float32),
+            pltpu.VMEM((near, channels * per_channel, feeds // near), jnp.float32),
+        ],
+        compiler_params=VMEM,
+        cost_estimate=pl.CostEstimate(
+            flops=channels * feeds * width * 2 * 128,
+            bytes_accessed=weights.size * 2,
+            transcendentals=0,
+        ),
+        name="beams",
+    )(received, weights)
+
+
+def gather_kernel(layout, beams_here, scale, own_ref, other_ref, out_ref, total, rows):
+    near, cores, channels, frames_here = layout
+    lane_channels = LANES // beams_here
+    per_core = 2 * frames_here
+    per_channel = per_core * cores
+    groups = channels // lane_channels
+    total[...] = (own_ref[...] + other_ref[...].astype(jnp.float32)) * scale
+    for group in range(groups):
+        values = [
+            total[pl.ds((group * lane_channels + sub) * per_channel, per_channel), :]
+            for sub in range(lane_channels)
+        ]
+        for place in range(near):
+            lanes = slice(place * beams_here, (place + 1) * beams_here)
+            tile = jnp.concatenate([value[:, lanes] for value in values], axis=1)
+            for core in range(cores):
+                start = ((place * cores + core) * groups + group) * per_core
+                for part in range(2):
+                    source = (part * cores + core) * frames_here
+                    rows[pl.ds(start + part * frames_here, frames_here), :] = tile[
+                        source : source + frames_here
+                    ]
+    out_ref[...] = rows[...].astype(jnp.bfloat16)
+
+
+def gather_beams(own, other, layout, beams_here, scale):
+    near, cores, channels, frames_here = layout
+    total_rows = near * cores * channels // (LANES // beams_here) * 2 * frames_here
+    return pl.pallas_call(
+        functools.partial(gather_kernel, layout, beams_here, scale),
+        out_shape=jax.ShapeDtypeStruct((total_rows, LANES), jnp.bfloat16),
+        scratch_shapes=[
+            pltpu.VMEM(own.shape, jnp.float32),
+            pltpu.VMEM((total_rows, LANES), jnp.float32),
+        ],
+        compiler_params=VMEM,
+        name="gather",
+    )(own, other)
+
+
+def series_kernel(beams_here, received_ref, cos_ref, sin_ref, basis_ref, out_ref, wide, lined):
+    _, frames_here, _ = out_ref.shape
+    kappas = cos_ref.shape[0]
+    lane_channels = LANES // beams_here
+    side = kappas // 2
+    slot = 8
+    wide[...] = received_ref[...].astype(jnp.float32)
+    lined[...] = jnp.zeros_like(lined)
+    for index in range(frames_here):
+        real = wide[pl.ds(index, kappas, stride=2 * frames_here), :]
+        imag = wide[pl.ds(frames_here + index, kappas, stride=2 * frames_here), :]
+        chirped_real = real * cos_ref[...] - imag * sin_ref[...]
+        chirped_imag = real * sin_ref[...] + imag * cos_ref[...]
+        for parity in range(2):
+            where = slice(parity * side, (parity + 1) * side)
+            both = jnp.concatenate([chirped_real[where], chirped_imag[where]], axis=0)
+            turned = both.T
+            for sub in range(lane_channels):
+                lined[parity, sub, pl.ds(index, beams_here, stride=slot), :] = turned[sub * beams_here : (sub + 1) * beams_here]
+    sides = []
+    for parity in range(2):
+        value = jnp.concatenate([lined[parity, sub] for sub in range(lane_channels)], axis=1)
+        high = value.astype(jnp.bfloat16)
+        low = (value - high.astype(jnp.float32)).astype(jnp.bfloat16)
+        sides.append(
+            jnp.dot(high, basis_ref[parity, 0], preferred_element_type=jnp.float32)
+            + jnp.dot(low, basis_ref[parity, 0], preferred_element_type=jnp.float32)
+            + jnp.dot(high, basis_ref[parity, 1], preferred_element_type=jnp.float32)
+        )
+    times = sides[0].shape[1] // 2
+    for part in range(2):
+        even = sides[0][:, part * times : (part + 1) * times]
+        odd = sides[1][:, part * times : (part + 1) * times]
+        for which, value in enumerate((even + odd, even - odd)):
+            start = (2 * part + which) * times
+            out_ref[:, :, start : start + times] = value.reshape(beams_here, slot, times)[
+                :, :frames_here, :
+            ]
+
+
+def make_series(received, chirp_cos, chirp_sin, basis, beams_here, frames_here):
+    slot = 8
+    lane_channels = LANES // beams_here
+    return pl.pallas_call(
+        functools.partial(series_kernel, beams_here),
+        out_shape=jax.ShapeDtypeStruct(
+            (beams_here, frames_here, 2 * basis.shape[3]), jnp.float32
+        ),
+        scratch_shapes=[
+            pltpu.VMEM(received.shape, jnp.float32),
+            pltpu.VMEM((2, lane_channels, beams_here * slot, LANES), jnp.float32),
+        ],
+        compiler_params=VMEM,
+        name="series",
+    )(received, chirp_cos, chirp_sin, basis)
+
+
+def halves_body(samples, filter_taps, feed_cylinder, feed_delay, pointing, chirp_rate):
+    length = filter_taps.shape[1]
+    nchan = length // 2
+    feed_here = samples.shape[0]
+    frames_here = samples.shape[1] // length
+    feeds = feed_delay.shape[0]
+    beams = pointing.shape[0]
+    beams_here = chirp_rate.shape[0]
+    near = lax.axis_size("near")
+    cores = lax.axis_size("tm")
+    group = near * cores
+    channels = nchan // group
+    half_feeds = feeds // HALVES
+    half_beams = beams // HALVES
+    layout = (near, cores, channels, frames_here)
+    half_index = lax.axis_index("half")
+    place = lax.axis_index(GROUP)
+
+    tail = from_behind(samples[:, (frames_here - (TAPS - 1)) * length :], "tm", 1)
+    forward = jnp.asarray(folded_forward_basis(length))
+    spectra = spectra_rows(samples, tail, filter_taps, forward)
+    spectra = spectra.reshape(group, channels * 2 * frames_here, feed_here)
+    received = lax.all_to_all(spectra, GROUP, 0, 0, tiled=True)
+    received = received.reshape(-1, feed_here)
+
+    in_parity = group // 2
+    first = 2 * (place % in_parity) * channels + place // in_parity + 1
+    first = jnp.reshape(first, (1,)).astype(jnp.int32)
+    delay = lax.dynamic_slice_in_dim(feed_delay, half_index * half_feeds, half_feeds)
+    delay = jnp.broadcast_to(delay.astype(jnp.float32)[:, None], (half_feeds, LANES))
+    cylinder = lax.dynamic_slice_in_dim(feed_cylinder, half_index * half_feeds, half_feeds)
+    cylinder = jnp.broadcast_to(cylinder[:, None], (half_feeds, LANES))
+    aim = jnp.transpose(pointing).astype(jnp.float32)
+    own_aim = lax.dynamic_slice_in_dim(aim, half_index * half_beams, half_beams, 1)
+    other_aim = lax.dynamic_slice_in_dim(aim, (1 - half_index) * half_beams, half_beams, 1)
+
+    other_weights = make_weights(first, delay, cylinder, other_aim, channels, 2)
+    to_send = partial_beams(received, other_weights, layout, jnp.bfloat16)
+    swap = [(i, HALVES - 1 - i) for i in range(HALVES)]
+    arrived = lax.ppermute(to_send, "half", swap)
+    own_aim, _ = lax.optimization_barrier((own_aim, to_send))
+    own_weights = make_weights(first, delay, cylinder, own_aim, channels, 2)
+    own = partial_beams(received, own_weights, layout, jnp.float32)
+    gathered = gather_beams(own, arrived, layout, beams_here, 1.0 / math.sqrt(feeds))
+    lane_channels = LANES // beams_here
+    gathered = gathered.reshape(group, -1, LANES)
+    returned = lax.all_to_all(gathered, GROUP, 0, 0, tiled=True).reshape(-1, LANES)
+
+    kappa = jnp.arange(nchan // lane_channels, dtype=jnp.int32)[:, None]
+    sub = jnp.arange(LANES, dtype=jnp.int32)[None, :] // beams_here
+    side = nchan // lane_channels // 2
+    channel = 2 * (lane_channels * (kappa % side) + sub) + kappa // side
+    position = channel.astype(jnp.float32) / nchan
+    rate = jnp.tile(jnp.pi * chirp_rate, lane_channels)[None, :]
+    chirp = rate * (position * position)
+    inverse = jnp.asarray(folded_inverse_basis(nchan, lane_channels))
+    return make_series(
+        returned, jnp.cos(chirp), jnp.sin(chirp), inverse, beams_here, frames_here
+    )
+
+
 def solution(mesh):
+    feed_size = mesh.shape["feed"]
+    wide_enough = FEEDS // feed_size % LANES == 0 and BEAMS // feed_size * 4 == LANES
+    if not wide_enough:
+        return jax.shard_map(
+            plain_body,
+            mesh=mesh,
+            in_specs=(P("feed", "tm"), P(), P(), P(), P(), P("feed")),
+            out_specs=P("feed", "tm", None),
+            check_vma=False,
+        )
+    devices = mesh.devices.reshape(HALVES, feed_size // HALVES, mesh.shape["tm"])
+    halved = jax.sharding.Mesh(devices, ("half", "near", "tm"))
+    feed = ("half", "near")
     return jax.shard_map(
-        body,
-        mesh=mesh,
-        in_specs=(P("feed", "tm"), P(), P(), P(), P(), P("feed")),
-        out_specs=P("feed", "tm", None),
+        halves_body,
+        mesh=halved,
+        in_specs=(P(feed, "tm"), P(), P(), P(), P(), P(feed)),
+        out_specs=P(feed, "tm", None),
         check_vma=False,
     )

time: 1330 us -> 117 us (0.09)
  matrix products: 1120 us -> 0 us
  Pallas kernels: 0 us -> 74.7 us
  local copies, waits for them, and re-layouts: 71.9 us -> 9.97 us
  loops' own time: 55.3 us -> 0 us
  other arithmetic: 20.9 us -> 1.03 us
  waiting for transfers between devices: 35.1 us -> 15.6 us
    dot_general x66 -> x0, matrix products: 1120 us -> none  [the longest x32 543 us: one_channel(): with_imag = jnp.dot(stacked, w_imag, preferred_element_type=jnp.float32)]
    pallas_call x0 -> x7, Pallas kernels: none -> 74.7 us  [the longest x2 32.1 us: partial_beams(): pl.pallas_call(functools.partial(beams_kernel, layout), grid=(channels //...]
    another operation x1 -> x0, loops' own time: 55.3 us -> none  [beamform(): return lax.map(one_channel, (turned, offsets))]
    dynamic_slice x64 -> x2, local copies, waits for them, and re-layouts: 48.6 us -> 0.63 us  [the longest x1 0.62 us: halves_body(): lax.dynamic_slice_in_dim(aim, (1 - half_index) * half_beams, half_beams, 1)]
    all_to_all x2, waiting for transfers between devices: 35.1 us -> 13.8 us  [the longest x1 8.02 us: halves_body(): lax.all_to_all(gathered, GROUP, 0, 0, tiled=True).reshape(-1, LANES)]
  transfers between devices with their start and end apart: 3 -> 4, of which waited for: 2 -> 3; matrix products, arithmetic and copies ran while one was open for 1% -> 3% of each run, Pallas kernels for 0% -> 38%
where the time goes in v1:
time: 117 us; the launch traced here: 116 us
  Pallas kernels  74.7 us (64%)
  waiting for transfers between devices  15.6 us (13%)
  starting transfers between devices  14.7 us (13%)
  local copies, waits for them, and re-layouts  9.97 us (9%)
    pallas_call x2, Pallas kernels, partial_beams(): pl.pallas_call(functools.partial(beams_kernel, layout), grid=(channels //...  32.1 us
    pallas_call x2, Pallas kernels, make_weights(): pl.pallas_call(functools.partial(weights_kernel, 32, step), grid=(feeds /...  28.6 us
    all_to_all x1, waiting for transfers between devices, halves_body(): lax.all_to_all(gathered, GROUP, 0, 0, tiled=True).reshape(-1, LANES)  8.02 us
    pallas_call x1, Pallas kernels, spectra_rows(): pl.pallas_call(functools.partial(spectra_kernel, frames_here), out_shape=...  7.33 us
    all_to_all x1, starting transfers between devices, halves_body(): received = lax.all_to_all(spectra, GROUP, 0, 0, tiled=True)  5.82 us
    all_to_all x1, waiting for transfers between devices, halves_body(): received = lax.all_to_all(spectra, GROUP, 0, 0, tiled=True)  5.75 us
    pallas_call x1, Pallas kernels, make_series(): pl.pallas_call(functools.partial(series_kernel, beams_here), out_shape=ja...  3.95 us
    all_to_all x1, starting transfers between devices, halves_body(): lax.all_to_all(gathered, GROUP, 0, 0, tiled=True).reshape(-1, LANES)  3.91 us
  transfers between devices with their start and end apart: 4, of which 3 were waited for; matrix products, arithmetic and copies ran while one was open for 3% of the time, Pallas kernels for 38%

profile of v1, /device:TPU:0, one launch (start us, length us, event | category | flops | bytes accessed | tf_op | source)
XLA Modules:
  0.0 116.2 jit_solution(1705942547210341650)
XLA Ops:
  0.0 1.2 %slice.3 = bf16[128,3072]{1,0:T(8,128)(2,1)S(1)} slice(bf16[128,6144]{1,0:T(8,128)(2,1)} %samples_ref.1), slice={[0:128], [3072:6144]} | slice | bytes 1572864 | tf_op jit(solution)/shard_map/slice | solution.py:508
  1.2 2.4 %collective-permute-start = (bf16[128,3072]{1,0:T(8,128)(2,1)S(1)}, bf16[128,3072]{1,0:T(8,128)(2,1)S(1)}, u32[]{:S(2)}, u32[]{:S(2)}) collective-permute-start(bf16[128,3072]{1,0:T(8,128)(2,1)S(1)} %slice.3), channel_id=1, source_target_pairs={{0,1},{2,3},{4,5},{6,7},{8,9},{10,11},{12,13},{14,15},{16,17},{18,... | collective-permute-start | bytes 2359304 | tf_op jit(solution)/shard_map/ppermute | solution.py:24
  3.6 1.8 %collective-permute-done.tail_ref = bf16[128,3072]{1,0:T(8,128)(2,1)S(1)} collective-permute-done((bf16[128,3072]{1,0:T(8,128)(2,1)S(1)}, bf16[128,3072]{1,0:T(8,128)(2,1)S(1)}, u32[]{:S(2)}, u32[]{:S(2)}) %collective-permute-start) | collective-permute-done | bytes 786464 | tf_op jit(solution)/shard_map/ppermute | solution.py:24
  5.4 0.0 copy-start.2
  5.4 0.9 copy-done.2
  6.3 7.3 %spectra.1 = bf16[6144,128]{1,0:T(8,128)(2,1)} custom-call(bf16[128,6144]{1,0:T(8,128)(2,1)} %samples_ref.1, bf16[128,3072]{1,0:T(8,128)(2,1)} %copy-done.2, f32[4,1024]{1,0:T(4,128)} %taps_ref.1, bf16[2,2,512,512]{3,2,1,0:T(8,128)(2,1)} %constant.106.clone.basis_ref), custom_call_target="tpu_custom_call" | custom-call | tf_op jit(solution)/shard_map/spectra/pallas_call | solution.py:233
  13.7 0.0 copy-start.4
  13.7 0.0 copy-start.5
  13.7 0.0 copy-start.6
  13.7 5.8 %all-to-all-start = ((bf16[16,384,128]{2,1,0:T(8,128)(2,1)}), bf16[16,384,128]{2,1,0:T(8,128)(2,1)S(1)}, u32[]{:S(2)}, u32[]{:S(2)}) async-start(bf16[16,384,128]{2,1,0:T(8,128)(2,1)} %bitcast.11), calls=%async_computation | async-start | bytes 3145728 | tf_op jit(solution)/shard_map/all_to_all | solution.py:512
  19.5 0.0 copy-done.4
  19.5 0.0 copy-done.5
  19.6 0.0 copy-done.6
  19.6 0.6 dynamic-slice_bitcast_fusion
  20.2 1.0 broadcast_in_dim.4.delay_ref
  21.2 1.0 broadcast_in_dim.5.cylinder_ref
  22.2 14.3 %weights.2.weights_ref = bf16[32,1024,512]{2,1,0:T(8,128)(2,1)} custom-call(s32[1]{0:T(128)} %bitcast.2.first_ref, f32[1024,128]{1,0:T(8,128)} %broadcast_in_dim.4.delay_ref, s32[1024,128]{1,0:T(8,128)} %broadcast_in_dim.5.cylinder_ref, f32[4,256]{1,0:T(4,128)} %get-tuple-element.7.pointing_ref), custom_call_target="tpu_custom_call" | custom-call | flops 67108864 | bytes 33554432 | tf_op jit(solution)/shard_map/weights/pallas_call | solution.py:307
  36.5 5.8 %all-to-all-done = bf16[16,384,128]{2,1,0:T(8,128)(2,1)S(1)} async-done(((bf16[16,384,128]{2,1,0:T(8,128)(2,1)}), bf16[16,384,128]{2,1,0:T(8,128)(2,1)S(1)}, u32[]{:S(2)}, u32[]{:S(2)}) %all-to-all-start) | async-done | bytes 1572896 | tf_op jit(solution)/shard_map/all_to_all | solution.py:512
  42.3 0.0 copy-start
  42.3 1.1 copy-done
  43.4 16.0 %beams.2 = bf16[768,256]{1,0:T(8,128)(2,1)} custom-call(bf16[6144,128]{1,0:T(8,128)(2,1)} %bitcast.9, bf16[32,1024,512]{2,1,0:T(8,128)(2,1)} %weights.2.weights_ref), custom_call_target="tpu_custom_call" | custom-call | flops 4294967296 | bytes 33554432 | tf_op jit(solution)/shard_map/beams/pallas_call | solution.py:370
  59.4 2.6 %collective-permute-start.1 = (bf16[768,256]{1,0:T(8,128)(2,1)}, bf16[768,256]{1,0:T(8,128)(2,1)S(1)}, u32[]{:S(2)}, u32[]{:S(2)}) collective-permute-start(bf16[768,256]{1,0:T(8,128)(2,1)} %beams.2), channel_id=1, source_target_pairs={{0,16},{16,0},{1,17},{17,1},{2,18},{18,2},{3,19},{19,3},{4,20},{20... | collective-permute-start | bytes 1179656 | tf_op jit(solution)/shard_map/ppermute | solution.py:529
  62.0 14.3 %weights.3.weights_ref = bf16[32,1024,512]{2,1,0:T(8,128)(2,1)} custom-call(s32[1]{0:T(128)} %bitcast.2.first_ref, f32[1024,128]{1,0:T(8,128)} %broadcast_in_dim.4.delay_ref, s32[1024,128]{1,0:T(8,128)} %broadcast_in_dim.5.cylinder_ref, f32[4,256]{1,0:T(4,128)} %get-tuple-element.6.pointing_ref), custom_call_target="tpu_custom_call" | custom-call | flops 67108864 | bytes 33554432 | tf_op jit(solution)/shard_map/weights/pallas_call | solution.py:307
  76.3 16.1 %beams.3.own_ref = f32[768,256]{1,0:T(8,128)} custom-call(bf16[6144,128]{1,0:T(8,128)(2,1)} %bitcast.10, bf16[32,1024,512]{2,1,0:T(8,128)(2,1)} %weights.3.weights_ref), custom_call_target="tpu_custom_call" | custom-call | flops 4294967296 | bytes 33554432 | tf_op jit(solution)/shard_map/beams/pallas_call | solution.py:370
  92.4 0.0 copy-start.7
  92.4 0.0 collective-permute-done.1.other_ref
  92.4 0.0 copy-start.3
  92.4 0.7 copy-done.3
  93.1 2.7 %gather.1 = bf16[1536,128]{1,0:T(8,128)(2,1)} custom-call(f32[768,256]{1,0:T(8,128)} %beams.3.own_ref, bf16[768,256]{1,0:T(8,128)(2,1)} %copy-done.3), custom_call_target="tpu_custom_call" | custom-call | tf_op jit(solution)/shard_map/gather/pallas_call | solution.py:421
  95.9 3.9 %all-to-all-start.1 = ((bf16[16,96,128]{2,1,0:T(8,128)(2,1)}), bf16[16,96,128]{2,1,0:T(8,128)(2,1)S(1)}, u32[]{:S(2)}, u32[]{:S(2)}) async-start(bf16[16,96,128]{2,1,0:T(8,128)(2,1)} %bitcast.13), calls=%async_computation.1 | async-start | bytes 786432 | tf_op jit(solution)/shard_map/all_to_all | solution.py:536
  99.8 0.0 copy-done.7
  99.8 0.1 mul.60
  99.9 1.0 fusion
  100.9 8.0 %all-to-all-done.1 = bf16[16,96,128]{2,1,0:T(8,128)(2,1)S(1)} async-done(((bf16[16,96,128]{2,1,0:T(8,128)(2,1)}), bf16[16,96,128]{2,1,0:T(8,128)(2,1)S(1)}, u32[]{:S(2)}, u32[]{:S(2)}) %all-to-all-start.1) | async-done | bytes 393248 | tf_op jit(solution)/shard_map/all_to_all | solution.py:536
  108.9 0.0 copy-start.1
  108.9 0.7 copy-done.1
  109.7 3.9 %series.1 = f32[32,6,1024]{2,1,0:T(8,128)} custom-call(bf16[1536,128]{1,0:T(8,128)(2,1)} %bitcast.12, f32[128,128]{1,0:T(8,128)} %get-tuple-element.10.cos_ref, f32[128,128]{1,0:T(8,128)} %get-tuple-element.9.sin_ref, bf16[2,2,512,512]{3,2,1,0:T(8,128)(2,1)} %constant.107.clone.basis_ref), custom_call_target="tpu_custom_call" | custom-call | tf_op jit(solution)/shard_map/series/pallas_call | solution.py:476
  113.6 2.6 %copy.9 = f32[32,6,1024]{2,0,1:T(8,128)} copy(f32[32,6,1024]{2,1,0:T(8,128)} %series.1) | data formatting | bytes 1572864 | tf_op jit(solution)/shard_map/series/pallas_call | solution.py:476
  (7 shorter events, 0.0 us)
Async XLA Ops:
  1.2 4.3 %collective-permute-start = (bf16[128,3072]{1,0:T(8,128)(2,1)S(1)}, bf16[128,3072]{1,0:T(8,128)(2,1)S(1)}, u32[]{:S(2)}, u32[]{:S(2)}) collective-permute-start(bf16[128,3072]{1,0:T(8,128)(2,1)S(1)} %slice.3), channel_id=1, source_target_pairs={{0,1},{2,3},{4,5},{6,7},{8,9},{10,11},{12,13},{14,15},{16,17},{18,... | collective-permute-start | bytes 2359304 | tf_op jit(solution)/shard_map/ppermute | solution.py:24
  5.4 0.9 copy-start.2
  13.7 5.9 %copy-start.4 = (s32[512,4]{0,1:T(4,128)S(1)}, s32[512,4]{0,1:T(4,128)}, u32[]{:S(2)}) copy-start(s32[512,4]{0,1:T(4,128)} %param.12) | copy-start | bytes 24580
  13.7 5.9 %copy-start.5 = (s32[2048]{0:T(1024)S(1)}, s32[2048]{0:T(1024)}, u32[]{:S(2)}) copy-start(s32[2048]{0:T(1024)} %param.10) | copy-start | bytes 24580
  13.7 5.9 %copy-start.6 = (s32[2048]{0:T(1024)S(1)}, s32[2048]{0:T(1024)}, u32[]{:S(2)}) copy-start(s32[2048]{0:T(1024)} %param.11) | copy-start | bytes 24580
  13.7 28.6 %all-to-all-start = ((bf16[16,384,128]{2,1,0:T(8,128)(2,1)}), bf16[16,384,128]{2,1,0:T(8,128)(2,1)S(1)}, u32[]{:S(2)}, u32[]{:S(2)}) async-start(bf16[16,384,128]{2,1,0:T(8,128)(2,1)} %bitcast.11), calls=%async_computation | async-start | bytes 3145728 | tf_op jit(solution)/shard_map/all_to_all | solution.py:512
  42.3 1.1 copy-start
  59.4 33.0 %collective-permute-start.1 = (bf16[768,256]{1,0:T(8,128)(2,1)}, bf16[768,256]{1,0:T(8,128)(2,1)S(1)}, u32[]{:S(2)}, u32[]{:S(2)}) collective-permute-start(bf16[768,256]{1,0:T(8,128)(2,1)} %beams.2), channel_id=1, source_target_pairs={{0,16},{16,0},{1,17},{17,1},{2,18},{18,2},{3,19},{19,3},{4,20},{20... | collective-permute-start | bytes 1179656 | tf_op jit(solution)/shard_map/ppermute | solution.py:529
  92.4 7.4 %copy-start.7 = (f32[32]{0:T(128)S(1)}, f32[32]{0:T(128)}, u32[]{:S(2)}) copy-start(f32[32]{0:T(128)} %param.13) | copy-start | bytes 388
  92.4 0.8 copy-start.3
  95.9 13.1 %all-to-all-start.1 = ((bf16[16,96,128]{2,1,0:T(8,128)(2,1)}), bf16[16,96,128]{2,1,0:T(8,128)(2,1)S(1)}, u32[]{:S(2)}, u32[]{:S(2)}) async-start(bf16[16,96,128]{2,1,0:T(8,128)(2,1)} %bitcast.13), calls=%async_computation.1 | async-start | bytes 786432 | tf_op jit(solution)/shard_map/all_to_all | solution.py:536
  108.9 0.7 copy-start.1

commit v2 on v1

--- a/solution.py
+++ b/solution.py
@@ -261,40 +261,51 @@
     return turns - jnp.floor(turns + 0.5)
 
 
-def weights_kernel(block_rows, step, first_ref, delay_ref, cylinder_ref, pointing_ref, out_ref):
-    channels, rows, width = out_ref.shape
+def chain_start(first, channels, step):
+    return (first + step * (channels // 2 - 1)).astype(jnp.float32)
+
+
+def chain_of_weights(first, step, delay, cylinder, pointing_ref, out_ref, where):
+    channels, _, width = out_ref.shape
     beams = width // 2
     repeat = beams // LANES
     middle = channels // 2
-    first = (first_ref[0] + step * (middle - 1)).astype(jnp.float32)
+    delay = jnp.concatenate([delay] * repeat, axis=1)
+    cylinder = jnp.concatenate([cylinder] * repeat, axis=1)
+    steer = jnp.broadcast_to(pointing_ref[0:1, :], delay.shape)
+    for other in range(1, CYL):
+        steer = jnp.where(cylinder == other, pointing_ref[other : other + 1, :], steer)
+    turns = centred(delay * steer * (1.0 / PHASES))
+    low_cos, low_sin = unit_vector(centred(first * turns))
+    step_cos, step_sin = unit_vector(centred(float(step) * turns))
+    high_cos = low_cos * step_cos - low_sin * step_sin
+    high_sin = low_cos * step_sin + low_sin * step_cos
+    twice = step_cos + step_cos
+
+    def put(channel, cosine, sine):
+        out_ref[channel, where, :beams] = cosine.astype(jnp.bfloat16)
+        out_ref[channel, where, beams:] = sine.astype(jnp.bfloat16)
+
+    put(middle - 1, low_cos, low_sin)
+    put(middle, high_cos, high_sin)
+    up = (low_cos, low_sin, high_cos, high_sin)
+    down = (high_cos, high_sin, low_cos, low_sin)
+    for away in range(1, middle):
+        up = (up[2], up[3], twice * up[2] - up[0], twice * up[3] - up[1])
+        down = (down[2], down[3], twice * down[2] - down[0], twice * down[3] - down[1])
+        put(middle + away, up[2], up[3])
+        put(middle - 1 - away, down[2], down[3])
+
+
+def weights_kernel(block_rows, step, first_ref, delay_ref, cylinder_ref, pointing_ref, out_ref):
+    channels, rows, _ = out_ref.shape
+    first = chain_start(first_ref[0], channels, step)
 
     def one_block(index, carry):
         where = pl.ds(pl.multiple_of(index * block_rows, block_rows), block_rows)
-        delay = jnp.concatenate([delay_ref[where]] * repeat, axis=1)
-        cylinder = jnp.concatenate([cylinder_ref[where]] * repeat, axis=1)
-        steer = jnp.broadcast_to(pointing_ref[0:1, :], (block_rows, beams))
-        for other in range(1, CYL):
-            steer = jnp.where(cylinder == other, pointing_ref[other : other + 1, :], steer)
-        turns = centred(delay * steer * (1.0 / PHASES))
-        low_cos, low_sin = unit_vector(centred(first * turns))
-        step_cos, step_sin = unit_vector(centred(float(step) * turns))
-        high_cos = low_cos * step_cos - low_sin * step_sin
-        high_sin = low_cos * step_sin + low_sin * step_cos
-        twice = step_cos + step_cos
-
-        def put(channel, cosine, sine):
-            out_ref[channel, where, :beams] = cosine.astype(jnp.bfloat16)
-            out_ref[channel, where, beams:] = sine.astype(jnp.bfloat16)
-
-        put(middle - 1, low_cos, low_sin)
-        put(middle, high_cos, high_sin)
-        up = (low_cos, low_sin, high_cos, high_sin)
-        down = (high_cos, high_sin, low_cos, low_sin)
-        for away in range(1, middle):
-            up = (up[2], up[3], twice * up[2] - up[0], twice * up[3] - up[1])
-            down = (down[2], down[3], twice * down[2] - down[0], twice * down[3] - down[1])
-            put(middle + away, up[2], up[3])
-            put(middle - 1 - away, down[2], down[3])
+        chain_of_weights(
+            first, step, delay_ref[where], cylinder_ref[where], pointing_ref, out_ref, where
+        )
         return carry
 
     lax.fori_loop(0, rows // block_rows, one_block, 0)
@@ -325,13 +336,24 @@
     )(first, delay, cylinder, pointing)
 
 
-def beams_kernel(layout, received_ref, weights_ref, out_ref, wide, lined):
+def padded_rows(rows):
+    return -(-rows // 16) * 16
+
+
+def turn_products(both):
+    beams = both.shape[1] // 2
+    half = both.shape[0] // 2
+    by_imag = both[:, beams:]
+    return both[:, :beams] + jnp.concatenate([-by_imag[half:], by_imag[:half]], axis=0)
+
+
+def beams_kernel(layout, received_ref, weights_ref, out_ref, lined_ref, wide, lined):
     near, cores, channels, frames_here = layout
     together = weights_ref.shape[0]
-    beams = weights_ref.shape[2] // 2
     per_source = 2 * frames_here
     per_channel = per_source * cores
     feed_here = received_ref.shape[1]
+    spare = lined_ref.shape[1] - per_channel
 
     @pl.when(pl.program_id(0) == 0)
     def _():
@@ -347,26 +369,32 @@
                             pl.ds(source, channels, stride=per_source), :
                         ]
 
-    half = per_channel // 2
     for local in range(together):
         start = pl.multiple_of((pl.program_id(0) * together + local) * per_channel, 8)
-        spectra = jnp.concatenate(
-            [lined[place, pl.ds(start, per_channel), :] for place in range(near)], axis=1
-        ).astype(jnp.bfloat16)
+        spectra = [
+            jnp.concatenate(
+                [
+                    lined[place, pl.ds(start, per_channel), :],
+                    jnp.zeros((spare, feed_here), jnp.float32),
+                ],
+                axis=0,
+            )
+            for place in range(near)
+        ]
+        spectra = jnp.concatenate(spectra, axis=1).astype(jnp.bfloat16)
+        lined_ref[local] = spectra
         both = jnp.dot(spectra, weights_ref[local], preferred_element_type=jnp.float32)
-        by_real = both[:, :beams]
-        by_imag = both[:, beams:]
-        turned = jnp.concatenate([-by_imag[half:], by_imag[:half]], axis=0)
-        out_ref[local * per_channel : (local + 1) * per_channel, :] = (by_real + turned).astype(
-            out_ref.dtype
-        )
+        out_ref[local * per_channel : (local + 1) * per_channel, :] = turn_products(
+            both[:per_channel]
+        ).astype(out_ref.dtype)
 
 
 def partial_beams(received, weights, layout, dtype):
     near, cores, channels, frames_here = layout
     feeds, width = weights.shape[1:]
     per_channel = 2 * cores * frames_here
-    together = 4
+    padded = padded_rows(per_channel)
+    together = 8
     return pl.pallas_call(
         functools.partial(beams_kernel, layout),
         grid=(channels // together,),
@@ -374,8 +402,14 @@
             pl.BlockSpec(received.shape, lambda i: (0, 0)),
             pl.BlockSpec((together, feeds, width), lambda i: (i, 0, 0)),
         ],
-        out_specs=pl.BlockSpec((together * per_channel, width // 2), lambda i: (i, 0)),
-        out_shape=jax.ShapeDtypeStruct((channels * per_channel, width // 2), dtype),
+        out_specs=[
+            pl.BlockSpec((together * per_channel, width // 2), lambda i: (i, 0)),
+            pl.BlockSpec((together, padded, feeds), lambda i: (i, 0, 0)),
+        ],
+        out_shape=[
+            jax.ShapeDtypeStruct((channels * per_channel, width // 2), dtype),
+            jax.ShapeDtypeStruct((channels, padded, feeds), jnp.bfloat16),
+        ],
         scratch_shapes=[
             pltpu.VMEM(received.shape, jnp.float32),
             pltpu.VMEM((near, channels * per_channel, feeds // near), jnp.float32),
@@ -388,6 +422,73 @@
         ),
         name="beams",
     )(received, weights)
+
+
+def own_beams_kernel(
+    per_channel, step, first_ref, lined_ref, delay_ref, cylinder_ref, pointing_ref, out_ref, total, weights
+):
+    channels, _, feeds = lined_ref.shape
+    _, rows, width = weights.shape
+    block_rows = 32
+    together = 4
+    first = chain_start(first_ref[0], channels, step)
+    for start in range(0, feeds, rows):
+
+        def one_block(index, carry):
+            target = pl.ds(pl.multiple_of(index * block_rows, block_rows), block_rows)
+            source = pl.ds(pl.multiple_of(start + index * block_rows, block_rows), block_rows)
+            chain_of_weights(
+                first, step, delay_ref[source], cylinder_ref[source], pointing_ref, weights, target
+            )
+            return carry
+
+        lax.fori_loop(0, rows // block_rows, one_block, 0)
+
+        def some_channels(index, carry):
+            ids = [index * together + local for local in range(together)]
+            places = [pl.ds(pl.multiple_of(i * per_channel, 8), per_channel) for i in ids]
+            olds = [total[place, :] if start else None for place in places]
+            news = [
+                jnp.dot(
+                    lined_ref[i, :, start : start + rows],
+                    weights[i],
+                    preferred_element_type=jnp.float32,
+                )[:per_channel]
+                for i in ids
+            ]
+            for place, old, new in zip(places, olds, news):
+                value = new if old is None else old + new
+                if start + rows < feeds:
+                    total[place, :] = value
+                else:
+                    out_ref[place, :] = turn_products(value)
+            return carry
+
+        lax.fori_loop(0, channels // together, some_channels, 0)
+
+
+def own_beams(first, lined, delay, cylinder, pointing, per_channel, step):
+    channels, _, feeds = lined.shape
+    beams = pointing.shape[1]
+    rows = 256
+    in_vmem = pl.BlockSpec(memory_space=pltpu.VMEM)
+    return pl.pallas_call(
+        functools.partial(own_beams_kernel, per_channel, step),
+        in_specs=[pl.BlockSpec(memory_space=pltpu.SMEM)] + [in_vmem] * 4,
+        out_specs=in_vmem,
+        out_shape=jax.ShapeDtypeStruct((channels * per_channel, beams), jnp.float32),
+        scratch_shapes=[
+            pltpu.VMEM((channels * per_channel, 2 * beams), jnp.float32),
+            pltpu.VMEM((channels, rows, 2 * beams), jnp.bfloat16),
+        ],
+        compiler_params=VMEM,
+        cost_estimate=pl.CostEstimate(
+            flops=channels * feeds * beams * 4 * 128,
+            bytes_accessed=channels * feeds * beams * 4,
+            transcendentals=0,
+        ),
+        name="own_beams",
+    )(first, lined, delay, cylinder, pointing)
 
 
 def gather_kernel(layout, beams_here, scale, own_ref, other_ref, out_ref, total, rows):
@@ -431,29 +532,32 @@
 
 
 def series_kernel(beams_here, received_ref, cos_ref, sin_ref, basis_ref, out_ref, wide, lined):
-    _, frames_here, _ = out_ref.shape
+    frames_here = out_ref.shape[0]
     kappas = cos_ref.shape[0]
     lane_channels = LANES // beams_here
     side = kappas // 2
-    slot = 8
     wide[...] = received_ref[...].astype(jnp.float32)
-    lined[...] = jnp.zeros_like(lined)
     for index in range(frames_here):
         real = wide[pl.ds(index, kappas, stride=2 * frames_here), :]
         imag = wide[pl.ds(frames_here + index, kappas, stride=2 * frames_here), :]
         chirped_real = real * cos_ref[...] - imag * sin_ref[...]
         chirped_imag = real * sin_ref[...] + imag * cos_ref[...]
+        target = slice(index * beams_here, (index + 1) * beams_here)
         for parity in range(2):
             where = slice(parity * side, (parity + 1) * side)
             both = jnp.concatenate([chirped_real[where], chirped_imag[where]], axis=0)
             turned = both.T
+            high = turned.astype(jnp.bfloat16)
+            low = (turned - high.astype(jnp.float32)).astype(jnp.bfloat16)
             for sub in range(lane_channels):
-                lined[parity, sub, pl.ds(index, beams_here, stride=slot), :] = turned[sub * beams_here : (sub + 1) * beams_here]
+                source = slice(sub * beams_here, (sub + 1) * beams_here)
+                lanes = slice(sub * 2 * side, (sub + 1) * 2 * side)
+                lined[parity, 0, target, lanes] = high[source]
+                lined[parity, 1, target, lanes] = low[source]
     sides = []
     for parity in range(2):
-        value = jnp.concatenate([lined[parity, sub] for sub in range(lane_channels)], axis=1)
-        high = value.astype(jnp.bfloat16)
-        low = (value - high.astype(jnp.float32)).astype(jnp.bfloat16)
+        high = lined[parity, 0]
+        low = lined[parity, 1]
         sides.append(
             jnp.dot(high, basis_ref[parity, 0], preferred_element_type=jnp.float32)
             + jnp.dot(low, basis_ref[parity, 0], preferred_element_type=jnp.float32)
@@ -465,26 +569,23 @@
         odd = sides[1][:, part * times : (part + 1) * times]
         for which, value in enumerate((even + odd, even - odd)):
             start = (2 * part + which) * times
-            out_ref[:, :, start : start + times] = value.reshape(beams_here, slot, times)[
-                :, :frames_here, :
-            ]
+            out_ref[:, :, start : start + times] = value.reshape(frames_here, beams_here, times)
 
 
 def make_series(received, chirp_cos, chirp_sin, basis, beams_here, frames_here):
-    slot = 8
-    lane_channels = LANES // beams_here
-    return pl.pallas_call(
+    series = pl.pallas_call(
         functools.partial(series_kernel, beams_here),
         out_shape=jax.ShapeDtypeStruct(
-            (beams_here, frames_here, 2 * basis.shape[3]), jnp.float32
+            (frames_here, beams_here, 2 * basis.shape[3]), jnp.float32
         ),
         scratch_shapes=[
             pltpu.VMEM(received.shape, jnp.float32),
-            pltpu.VMEM((2, lane_channels, beams_here * slot, LANES), jnp.float32),
+            pltpu.VMEM((2, 2, frames_here * beams_here, basis.shape[2]), jnp.bfloat16),
         ],
         compiler_params=VMEM,
         name="series",
     )(received, chirp_cos, chirp_sin, basis)
+    return jnp.transpose(series, (1, 0, 2))
 
 
 def halves_body(samples, filter_taps, feed_cylinder, feed_delay, pointing, chirp_rate):
@@ -524,12 +625,10 @@
     other_aim = lax.dynamic_slice_in_dim(aim, (1 - half_index) * half_beams, half_beams, 1)
 
     other_weights = make_weights(first, delay, cylinder, other_aim, channels, 2)
-    to_send = partial_beams(received, other_weights, layout, jnp.bfloat16)
+    to_send, lined = partial_beams(received, other_weights, layout, jnp.bfloat16)
     swap = [(i, HALVES - 1 - i) for i in range(HALVES)]
     arrived = lax.ppermute(to_send, "half", swap)
-    own_aim, _ = lax.optimization_barrier((own_aim, to_send))
-    own_weights = make_weights(first, delay, cylinder, own_aim, channels, 2)
-    own = partial_beams(received, own_weights, layout, jnp.float32)
+    own = own_beams(first, lined, delay, cylinder, own_aim, 2 * cores * frames_here, 2)
     gathered = gather_beams(own, arrived, layout, beams_here, 1.0 / math.sqrt(feeds))
     lane_channels = LANES // beams_here
     gathered = gathered.reshape(group, -1, LANES)

time: 117 us -> 103 us (0.88)
  Pallas kernels: 74.7 us -> 63.6 us
  local copies, waits for them, and re-layouts: 9.97 us -> 7.46 us
    pallas_call x0 -> x1, Pallas kernels: none -> 20.9 us  [own_beams(): pl.pallas_call(functools.partial(own_beams_kernel, per_channel, step), in...]
    pallas_call x2 -> x1, Pallas kernels: 32.1 us -> 14.7 us  [partial_beams(): pl.pallas_call(functools.partial(beams_kernel, layout), grid=(channels //...]
    pallas_call x2 -> x1, Pallas kernels: 28.6 us -> 14.3 us  [make_weights(): pl.pallas_call(functools.partial(weights_kernel, 32, step), grid=(feeds /...]
    pallas_call x1 -> x0, local copies, waits for them, and re-layouts: 2.56 us -> none  [make_series(): pl.pallas_call(functools.partial(series_kernel, beams_here), out_shape=ja...]
  transfers between devices with their start and end apart: 4 -> 4, of which waited for: 3 -> 3; matrix products, arithmetic and copies ran while one was open for 3% -> 4% of each run, Pallas kernels for 38% -> 34%
where the time goes in v2:
time: 103 us
  Pallas kernels  63.6 us (62%)
  waiting for transfers between devices  15.6 us (15%)
  starting transfers between devices  14.7 us (14%)
  local copies, waits for them, and re-layouts  7.46 us (7%)
    pallas_call x1, Pallas kernels, own_beams(): pl.pallas_call(functools.partial(own_beams_kernel, per_channel, step), in...  20.9 us
    pallas_call x1, Pallas kernels, partial_beams(): pl.pallas_call(functools.partial(beams_kernel, layout), grid=(channels //...  14.7 us
    pallas_call x1, Pallas kernels, make_weights(): pl.pallas_call(functools.partial(weights_kernel, 32, step), grid=(feeds /...  14.3 us
    all_to_all x1, waiting for transfers between devices, halves_body(): lax.all_to_all(gathered, GROUP, 0, 0, tiled=True).reshape(-1, LANES)  8.03 us
    pallas_call x1, Pallas kernels, spectra_rows(): pl.pallas_call(functools.partial(spectra_kernel, frames_here), out_shape=...  7.33 us
    all_to_all x1, starting transfers between devices, halves_body(): received = lax.all_to_all(spectra, GROUP, 0, 0, tiled=True)  5.82 us
    all_to_all x1, waiting for transfers between devices, halves_body(): received = lax.all_to_all(spectra, GROUP, 0, 0, tiled=True)  5.73 us
    all_to_all x1, starting transfers between devices, halves_body(): lax.all_to_all(gathered, GROUP, 0, 0, tiled=True).reshape(-1, LANES)  3.91 us
  transfers between devices with their start and end apart: 4, of which 3 were waited for; matrix products, arithmetic and copies ran while one was open for 4% of the time, Pallas kernels for 34%

profile of v2, /device:TPU:0, one launch (start us, length us, event | category | flops | bytes accessed | tf_op | source)
XLA Modules:
  0.0 102.6 jit_solution(17255808616207915488)
XLA Ops:
  0.0 1.2 %slice.3 = bf16[128,3072]{1,0:T(8,128)(2,1)S(1)} slice(bf16[128,6144]{1,0:T(8,128)(2,1)} %samples_ref.1), slice={[0:128], [3072:6144]} | slice | bytes 1572864 | tf_op jit(solution)/shard_map/slice | solution.py:609
  1.2 2.4 %collective-permute-start = (bf16[128,3072]{1,0:T(8,128)(2,1)S(1)}, bf16[128,3072]{1,0:T(8,128)(2,1)S(1)}, u32[]{:S(2)}, u32[]{:S(2)}) collective-permute-start(bf16[128,3072]{1,0:T(8,128)(2,1)S(1)} %slice.3), channel_id=1, source_target_pairs={{0,1},{2,3},{4,5},{6,7},{8,9},{10,11},{12,13},{14,15},{16,17},{18,... | collective-permute-start | bytes 2359304 | tf_op jit(solution)/shard_map/ppermute | solution.py:24
  3.6 1.8 %collective-permute-done.tail_ref = bf16[128,3072]{1,0:T(8,128)(2,1)S(1)} collective-permute-done((bf16[128,3072]{1,0:T(8,128)(2,1)S(1)}, bf16[128,3072]{1,0:T(8,128)(2,1)S(1)}, u32[]{:S(2)}, u32[]{:S(2)}) %collective-permute-start) | collective-permute-done | bytes 786464 | tf_op jit(solution)/shard_map/ppermute | solution.py:24
  5.4 0.0 copy-start.2
  5.4 0.9 copy-done.2
  6.3 7.3 %spectra.1 = bf16[6144,128]{1,0:T(8,128)(2,1)} custom-call(bf16[128,6144]{1,0:T(8,128)(2,1)} %samples_ref.1, bf16[128,3072]{1,0:T(8,128)(2,1)} %copy-done.2, f32[4,1024]{1,0:T(4,128)} %taps_ref.1, bf16[2,2,512,512]{3,2,1,0:T(8,128)(2,1)} %constant.106.clone.basis_ref), custom_call_target="tpu_custom_call" | custom-call | tf_op jit(solution)/shard_map/spectra/pallas_call | solution.py:233
  13.7 0.0 copy-start.4
  13.7 0.0 copy-start.5
  13.7 0.0 copy-start.6
  13.7 5.8 %all-to-all-start = ((bf16[16,384,128]{2,1,0:T(8,128)(2,1)}), bf16[16,384,128]{2,1,0:T(8,128)(2,1)S(1)}, u32[]{:S(2)}, u32[]{:S(2)}) async-start(bf16[16,384,128]{2,1,0:T(8,128)(2,1)} %bitcast.11), calls=%async_computation | async-start | bytes 3145728 | tf_op jit(solution)/shard_map/all_to_all | solution.py:613
  19.5 0.0 copy-done.4
  19.5 0.0 copy-done.5
  19.6 0.0 copy-done.6
  19.6 0.6 dynamic-slice_bitcast_fusion
  20.2 1.0 broadcast_in_dim.4.delay_ref
  21.2 1.0 broadcast_in_dim.5.cylinder_ref
  22.2 14.3 %weights.1.weights_ref = bf16[32,1024,512]{2,1,0:T(8,128)(2,1)} custom-call(s32[1]{0:T(128)} %bitcast.first_ref, f32[1024,128]{1,0:T(8,128)} %broadcast_in_dim.4.delay_ref, s32[1024,128]{1,0:T(8,128)} %broadcast_in_dim.5.cylinder_ref, f32[4,256]{1,0:T(4,128)} %get-tuple-element.10.pointing_ref), custom_call_target="tpu_custom_call" | custom-call | flops 67108864 | bytes 33554432 | tf_op jit(solution)/shard_map/weights/pallas_call | solution.py:318
  36.5 5.7 %all-to-all-done = bf16[16,384,128]{2,1,0:T(8,128)(2,1)S(1)} async-done(((bf16[16,384,128]{2,1,0:T(8,128)(2,1)}), bf16[16,384,128]{2,1,0:T(8,128)(2,1)S(1)}, u32[]{:S(2)}, u32[]{:S(2)}) %all-to-all-start) | async-done | bytes 1572896 | tf_op jit(solution)/shard_map/all_to_all | solution.py:613
  42.3 0.0 copy-start
  42.3 1.2 %copy-done = bf16[16,384,128]{2,1,0:T(8,128)(2,1)} copy-done((bf16[16,384,128]{2,1,0:T(8,128)(2,1)}, bf16[16,384,128]{2,1,0:T(8,128)(2,1)S(1)}, u32[]{:S(2)}) %copy-start) | copy-done | bytes 1572888
  43.4 14.7 %beams.1 = (bf16[768,256]{1,0:T(8,128)(2,1)}, bf16[32,32,1024]{2,1,0:T(8,128)(2,1)}) custom-call(bf16[6144,128]{1,0:T(8,128)(2,1)} %bitcast.10, bf16[32,1024,512]{2,1,0:T(8,128)(2,1)} %weights.1.weights_ref), custom_call_target="tpu_custom_call" | custom-call | flops 4294967296 | bytes 33554432 | tf_op jit(solution)/shard_map/beams/pallas_call | solution.py:398
  58.2 2.6 %collective-permute-start.1 = (bf16[768,256]{1,0:T(8,128)(2,1)}, bf16[768,256]{1,0:T(8,128)(2,1)S(1)}, u32[]{:S(2)}, u32[]{:S(2)}) collective-permute-start(bf16[768,256]{1,0:T(8,128)(2,1)} %get-tuple-element.8), channel_id=1, source_target_pairs={{0,16},{16,0},{1,17},{17,1},{2,18},{18,2},{3,19},{19,3},{4,20},{20... | collective-permute-start | bytes 1179656 | tf_op jit(solution)/shard_map/ppermute | solution.py:630
  60.8 20.9 %own_beams.1.own_ref = f32[768,256]{1,0:T(8,128)} custom-call(s32[1]{0:T(128)} %bitcast.first_ref, bf16[32,32,1024]{2,1,0:T(8,128)(2,1)} %get-tuple-element.7.lined_ref, f32[1024,128]{1,0:T(8,128)} %broadcast_in_dim.4.delay_ref, s32[1024,128]{1,0:T(8,128)} %broadcast_in_dim.5.cylinder_ref, f32[4,256]{1,0:T(4,128)} %get-tuple-element.9.pointing_ref), custom_call_target="tpu_custom_call" | custom-call | flops 4294967296 | bytes 33554432 | tf_op jit(solution)/shard_map/own_beams/pallas_call | solution.py:475
  81.7 0.0 copy-start.7
  81.7 0.0 collective-permute-done.1.other_ref
  81.7 0.0 copy-start.3
  81.7 0.7 copy-done.3
  82.4 2.7 %gather.1 = bf16[1536,128]{1,0:T(8,128)(2,1)} custom-call(f32[768,256]{1,0:T(8,128)} %own_beams.1.own_ref, bf16[768,256]{1,0:T(8,128)(2,1)} %copy-done.3), custom_call_target="tpu_custom_call" | custom-call | tf_op jit(solution)/shard_map/gather/pallas_call | solution.py:522
  85.2 3.9 %all-to-all-start.1 = ((bf16[16,96,128]{2,1,0:T(8,128)(2,1)}), bf16[16,96,128]{2,1,0:T(8,128)(2,1)S(1)}, u32[]{:S(2)}, u32[]{:S(2)}) async-start(bf16[16,96,128]{2,1,0:T(8,128)(2,1)} %bitcast.12), calls=%async_computation.1 | async-start | bytes 786432 | tf_op jit(solution)/shard_map/all_to_all | solution.py:635
  89.1 0.0 copy-done.7
  89.1 0.1 mul.60
  89.2 1.0 fusion
  90.2 8.0 %all-to-all-done.1 = bf16[16,96,128]{2,1,0:T(8,128)(2,1)S(1)} async-done(((bf16[16,96,128]{2,1,0:T(8,128)(2,1)}), bf16[16,96,128]{2,1,0:T(8,128)(2,1)S(1)}, u32[]{:S(2)}, u32[]{:S(2)}) %all-to-all-start.1) | async-done | bytes 393248 | tf_op jit(solution)/shard_map/all_to_all | solution.py:635
  98.3 0.0 copy-start.1
  98.3 0.8 copy-done.1
  99.0 3.6 %series.1 = f32[6,32,1024]{2,1,0:T(8,128)} custom-call(bf16[1536,128]{1,0:T(8,128)(2,1)} %bitcast.13, f32[128,128]{1,0:T(8,128)} %get-tuple-element.12.cos_ref, f32[128,128]{1,0:T(8,128)} %get-tuple-element.11.sin_ref, bf16[2,2,512,512]{3,2,1,0:T(8,128)(2,1)} %constant.107.clone.basis_ref), custom_call_target="tpu_custom_call" | custom-call | tf_op jit(solution)/shard_map/series/pallas_call | solution.py:576
  (7 shorter events, 0.0 us)
Async XLA Ops:
  1.2 4.3 %collective-permute-start = (bf16[128,3072]{1,0:T(8,128)(2,1)S(1)}, bf16[128,3072]{1,0:T(8,128)(2,1)S(1)}, u32[]{:S(2)}, u32[]{:S(2)}) collective-permute-start(bf16[128,3072]{1,0:T(8,128)(2,1)S(1)} %slice.3), channel_id=1, source_target_pairs={{0,1},{2,3},{4,5},{6,7},{8,9},{10,11},{12,13},{14,15},{16,17},{18,... | collective-permute-start | bytes 2359304 | tf_op jit(solution)/shard_map/ppermute | solution.py:24
  5.4 0.9 copy-start.2
  13.7 5.9 %copy-start.4 = (s32[512,4]{0,1:T(4,128)S(1)}, s32[512,4]{0,1:T(4,128)}, u32[]{:S(2)}) copy-start(s32[512,4]{0,1:T(4,128)} %param.12) | copy-start | bytes 24580
  13.7 5.9 %copy-start.5 = (s32[2048]{0:T(1024)S(1)}, s32[2048]{0:T(1024)}, u32[]{:S(2)}) copy-start(s32[2048]{0:T(1024)} %param.10) | copy-start | bytes 24580
  13.7 5.9 %copy-start.6 = (s32[2048]{0:T(1024)S(1)}, s32[2048]{0:T(1024)}, u32[]{:S(2)}) copy-start(s32[2048]{0:T(1024)} %param.11) | copy-start | bytes 24580
  13.7 28.6 %all-to-all-start = ((bf16[16,384,128]{2,1,0:T(8,128)(2,1)}), bf16[16,384,128]{2,1,0:T(8,128)(2,1)S(1)}, u32[]{:S(2)}, u32[]{:S(2)}) async-start(bf16[16,384,128]{2,1,0:T(8,128)(2,1)} %bitcast.11), calls=%async_computation | async-start | bytes 3145728 | tf_op jit(solution)/shard_map/all_to_all | solution.py:613
  42.3 1.2 %copy-start = (bf16[16,384,128]{2,1,0:T(8,128)(2,1)}, bf16[16,384,128]{2,1,0:T(8,128)(2,1)S(1)}, u32[]{:S(2)}) copy-start(bf16[16,384,128]{2,1,0:T(8,128)(2,1)S(1)} %all-to-all-done) | copy-start | bytes 4718596
  58.2 23.5 %collective-permute-start.1 = (bf16[768,256]{1,0:T(8,128)(2,1)}, bf16[768,256]{1,0:T(8,128)(2,1)S(1)}, u32[]{:S(2)}, u32[]{:S(2)}) collective-permute-start(bf16[768,256]{1,0:T(8,128)(2,1)} %get-tuple-element.8), channel_id=1, source_target_pairs={{0,16},{16,0},{1,17},{17,1},{2,18},{18,2},{3,19},{19,3},{4,20},{20... | collective-permute-start | bytes 1179656 | tf_op jit(solution)/shard_map/ppermute | solution.py:630
  81.7 7.4 %copy-start.7 = (f32[32]{0:T(128)S(1)}, f32[32]{0:T(128)}, u32[]{:S(2)}) copy-start(f32[32]{0:T(128)} %param.13) | copy-start | bytes 388
  81.7 0.7 copy-start.3
  85.2 13.1 %all-to-all-start.1 = ((bf16[16,96,128]{2,1,0:T(8,128)(2,1)}), bf16[16,96,128]{2,1,0:T(8,128)(2,1)S(1)}, u32[]{:S(2)}, u32[]{:S(2)}) async-start(bf16[16,96,128]{2,1,0:T(8,128)(2,1)} %bitcast.12), calls=%async_computation.1 | async-start | bytes 786432 | tf_op jit(solution)/shard_map/all_to_all | solution.py:635
  98.3 0.8 copy-start.1

commit v3 on v2

--- a/solution.py
+++ b/solution.py
@@ -126,6 +126,7 @@
 
 
 LANES = 128
+PHASE_BITS = PHASES.bit_length() - 1
 HALVES = 2
 GROUP = ("near", "tm")
 VMEM = pltpu.CompilerParams(vmem_limit_bytes=56 * 1024 * 1024)
@@ -169,32 +170,53 @@
     )
 
 
-def spectra_kernel(frames_here, samples_ref, tail_ref, taps_ref, basis_ref, out_ref, folded, rows):
+def spectra_kernel(
+    frames_here, half_ref, samples_ref, tail_ref, taps_in_ref, basis_ref, out_ref,
+    samples, tail, taps_ref, basis, folded, rows, packed, in_sems, out_sems,
+):
     feed_here = samples_ref.shape[0]
     length = taps_ref.shape[1]
     half = length // 2
+    before = TAPS - 1
+    side = half_ref[0]
+    sign = (1 - 2 * side).astype(jnp.float32)
+    fetch_samples = pltpu.make_async_copy(samples_ref, samples, in_sems.at[0])
+    fetch_tail = pltpu.make_async_copy(tail_ref, tail, in_sems.at[1])
+    fetch_taps = pltpu.make_async_copy(taps_in_ref, taps_ref, in_sems.at[4])
+    fetch_basis = [
+        pltpu.make_async_copy(
+            basis_ref.at[parity + side * (1 - 2 * parity)], basis.at[parity], in_sems.at[2 + parity]
+        )
+        for parity in range(2)
+    ]
+    fetches = [fetch_taps, fetch_samples, fetch_tail] + fetch_basis
+    for fetch in fetches:
+        fetch.start()
+    fetch_taps.wait()
+    fetch_samples.wait()
 
     def frame(index, start):
-        lanes = pl.ds((index % frames_here) * length + start, LANES)
         if index < 0:
-            lanes = pl.ds((index + TAPS - 1) * length + start, LANES)
-            return tail_ref[:, lanes].astype(jnp.float32)
-        return samples_ref[:, lanes].astype(jnp.float32)
+            lanes = pl.ds((index + before) * length + start, LANES)
+            return tail[:, lanes].astype(jnp.float32)
+        return samples[:, pl.ds(index * length + start, LANES)].astype(jnp.float32)
 
     def filtered(index, start):
         total = None
         for tap in range(TAPS):
             term = taps_ref[tap : tap + 1, start : start + LANES] * frame(
-                index + tap - (TAPS - 1), start
+                index + tap - before, start
             )
             total = term if total is None else total + term
         return total
 
-    for index in range(frames_here):
+    for index in list(range(before, frames_here)) + list(range(before)):
+        if index == 0:
+            fetch_tail.wait()
         where = pl.ds(index * feed_here, feed_here)
         for start in range(0, half, LANES):
             near = filtered(index, start)
-            far = filtered(index, start + half)
+            far = filtered(index, start + half) * sign
             for parity, value in enumerate((near + far, near - far)):
                 high = value.astype(jnp.bfloat16)
                 folded[parity, 0, where, start : start + LANES] = high
@@ -204,17 +226,19 @@
 
     per_channel = 2 * frames_here
     together = 2
+    count = half // 2
+    stores = []
     for parity in range(2):
+        fetch_basis[parity].wait()
         for first in range(0, frames_here, together):
             where = pl.ds(first * feed_here, together * feed_here)
             high = folded[parity, 0, where, :]
             low = folded[parity, 1, where, :]
             result = (
-                dot_nt(basis_ref[parity, 0], high)
-                + dot_nt(basis_ref[parity, 1], high)
-                + dot_nt(basis_ref[parity, 0], low)
+                dot_nt(basis[parity, 0], high)
+                + dot_nt(basis[parity, 1], high)
+                + dot_nt(basis[parity, 0], low)
             )
-            count = half // 2
             for part in range(2):
                 for ahead in range(together):
                     start = parity * count * per_channel + part * frames_here + first + ahead
@@ -222,24 +246,61 @@
                         part * count : (part + 1) * count,
                         ahead * feed_here : (ahead + 1) * feed_here,
                     ]
-    out_ref[...] = rows[...].astype(jnp.bfloat16)
-
-
-def spectra_rows(samples, tail, taps, basis):
+        block = pl.ds(parity * count * per_channel, count * per_channel)
+        packed[block, :] = rows[block, :].astype(jnp.bfloat16)
+        store = pltpu.make_async_copy(packed.at[block], out_ref.at[block], out_sems.at[parity])
+        store.start()
+        stores.append(store)
+    for store in stores:
+        store.wait()
+
+
+def spectra_rows(half_index, samples, tail, taps, basis):
     feed_here = samples.shape[0]
     length = taps.shape[1]
     frames_here = samples.shape[1] // length
     total_rows = length * frames_here
+    anywhere = pl.BlockSpec(memory_space=pl.ANY)
+    in_hbm = pl.BlockSpec(memory_space=pltpu.HBM)
     return pl.pallas_call(
         functools.partial(spectra_kernel, frames_here),
+        in_specs=[pl.BlockSpec(memory_space=pltpu.SMEM), in_hbm, anywhere, in_hbm, in_hbm],
+        out_specs=anywhere,
         out_shape=jax.ShapeDtypeStruct((total_rows, feed_here), jnp.bfloat16),
         scratch_shapes=[
+            pltpu.VMEM(samples.shape, samples.dtype),
+            pltpu.VMEM(tail.shape, tail.dtype),
+            pltpu.VMEM(taps.shape, taps.dtype),
+            pltpu.VMEM(basis.shape, basis.dtype),
             pltpu.VMEM((2, 2, frames_here * feed_here, length // 2), jnp.bfloat16),
             pltpu.VMEM((total_rows, feed_here), jnp.float32),
+            pltpu.VMEM((total_rows, feed_here), jnp.bfloat16),
+            pltpu.SemaphoreType.DMA((5,)),
+            pltpu.SemaphoreType.DMA((2,)),
         ],
-        compiler_params=VMEM,
+        compiler_params=pltpu.CompilerParams(vmem_limit_bytes=24 * 1024 * 1024),
         name="spectra",
-    )(samples, tail, taps, basis)
+    )(half_index, samples, tail, taps, basis)
+
+
+def tail_kernel(samples_ref, out_ref, sem):
+    count = out_ref.shape[1]
+    where = pl.ds(samples_ref.shape[1] - count, count)
+    copy = pltpu.make_async_copy(samples_ref.at[:, where], out_ref, sem)
+    copy.start()
+    copy.wait()
+
+
+def last_samples(samples, count):
+    return pl.pallas_call(
+        tail_kernel,
+        in_specs=[pl.BlockSpec(memory_space=pltpu.HBM)],
+        out_specs=pl.BlockSpec(memory_space=pl.ANY),
+        out_shape=jax.ShapeDtypeStruct((samples.shape[0], count), samples.dtype),
+        scratch_shapes=[pltpu.SemaphoreType.DMA],
+        compiler_params=pltpu.CompilerParams(vmem_limit_bytes=4 * 1024 * 1024),
+        name="tail",
+    )(samples)
 
 
 def sine_turns(turns):
@@ -265,13 +326,13 @@
     return (first + step * (channels // 2 - 1)).astype(jnp.float32)
 
 
-def chain_of_weights(first, step, delay, cylinder, pointing_ref, out_ref, where):
+def chain_of_weights(first, step, code, pointing_ref, out_ref, where):
     channels, _, width = out_ref.shape
     beams = width // 2
     repeat = beams // LANES
     middle = channels // 2
-    delay = jnp.concatenate([delay] * repeat, axis=1)
-    cylinder = jnp.concatenate([cylinder] * repeat, axis=1)
+    cylinder = jnp.concatenate([lax.shift_right_logical(code, PHASE_BITS)] * repeat, axis=1)
+    delay = jnp.concatenate([(code & (PHASES - 1)).astype(jnp.float32)] * repeat, axis=1)
     steer = jnp.broadcast_to(pointing_ref[0:1, :], delay.shape)
     for other in range(1, CYL):
         steer = jnp.where(cylinder == other, pointing_ref[other : other + 1, :], steer)
@@ -297,43 +358,40 @@
         put(middle - 1 - away, down[2], down[3])
 
 
-def weights_kernel(block_rows, step, first_ref, delay_ref, cylinder_ref, pointing_ref, out_ref):
+def weights_kernel(block_rows, step, first_ref, code_ref, pointing_ref, out_ref):
     channels, rows, _ = out_ref.shape
     first = chain_start(first_ref[0], channels, step)
 
     def one_block(index, carry):
         where = pl.ds(pl.multiple_of(index * block_rows, block_rows), block_rows)
-        chain_of_weights(
-            first, step, delay_ref[where], cylinder_ref[where], pointing_ref, out_ref, where
-        )
+        chain_of_weights(first, step, code_ref[where], pointing_ref.at[0], out_ref, where)
         return carry
 
     lax.fori_loop(0, rows // block_rows, one_block, 0)
 
 
-def make_weights(first, delay, cylinder, pointing, channels, step):
-    feeds = delay.shape[0]
-    beams = pointing.shape[1]
+def make_weights(first, code, pointing, channels, step, feeds):
+    sets, cylinders, beams = pointing.shape
     rows = 128
+    tiles = feeds // rows
     return pl.pallas_call(
         functools.partial(weights_kernel, 32, step),
-        grid=(feeds // rows,),
+        grid=(sets * tiles,),
         in_specs=[
             pl.BlockSpec(memory_space=pltpu.SMEM),
-            pl.BlockSpec((rows, LANES), lambda i: (i, 0)),
-            pl.BlockSpec((rows, LANES), lambda i: (i, 0)),
-            pl.BlockSpec(pointing.shape, lambda i: (0, 0)),
+            pl.BlockSpec((rows, LANES), lambda i: (i % tiles, 0)),
+            pl.BlockSpec((1, cylinders, beams), lambda i: (i // tiles, 0, 0)),
         ],
         out_specs=pl.BlockSpec((channels, rows, 2 * beams), lambda i: (0, i, 0)),
-        out_shape=jax.ShapeDtypeStruct((channels, feeds, 2 * beams), jnp.bfloat16),
+        out_shape=jax.ShapeDtypeStruct((channels, sets * feeds, 2 * beams), jnp.bfloat16),
         compiler_params=VMEM,
         cost_estimate=pl.CostEstimate(
-            flops=channels * feeds * beams * 8,
-            bytes_accessed=channels * feeds * beams * 4,
+            flops=channels * sets * feeds * beams * 8,
+            bytes_accessed=channels * sets * feeds * beams * 4,
             transcendentals=0,
         ),
         name="weights",
-    )(first, delay, cylinder, pointing)
+    )(first, code, pointing)
 
 
 def padded_rows(rows):
@@ -347,157 +405,155 @@
     return both[:, :beams] + jnp.concatenate([-by_imag[half:], by_imag[:half]], axis=0)
 
 
-def beams_kernel(layout, received_ref, weights_ref, out_ref, lined_ref, wide, lined):
+def line_up(layout, arrived, wide, lined, spectra):
     near, cores, channels, frames_here = layout
-    together = weights_ref.shape[0]
     per_source = 2 * frames_here
     per_channel = per_source * cores
-    feed_here = received_ref.shape[1]
-    spare = lined_ref.shape[1] - per_channel
-
-    @pl.when(pl.program_id(0) == 0)
-    def _():
-        wide[...] = received_ref[...].astype(jnp.float32)
-        for place in range(near):
-            for core in range(cores):
-                base = (place * cores + core) * channels * per_source
-                for part in range(2):
-                    for index in range(frames_here):
-                        source = base + part * frames_here + index
-                        target = (part * cores + core) * frames_here + index
-                        lined[place, pl.ds(target, channels, stride=per_channel), :] = wide[
-                            pl.ds(source, channels, stride=per_source), :
-                        ]
-
-    for local in range(together):
-        start = pl.multiple_of((pl.program_id(0) * together + local) * per_channel, 8)
-        spectra = [
-            jnp.concatenate(
-                [
-                    lined[place, pl.ds(start, per_channel), :],
-                    jnp.zeros((spare, feed_here), jnp.float32),
-                ],
-                axis=0,
-            )
-            for place in range(near)
+    spare = spectra.shape[1] - per_channel
+    wide[...] = arrived[...].astype(jnp.float32)
+    for place in range(near):
+        for core in range(cores):
+            base = (place * cores + core) * channels * per_source
+            for part in range(2):
+                for index in range(frames_here):
+                    source = base + part * frames_here + index
+                    target = (part * cores + core) * frames_here + index
+                    lined[place, pl.ds(target, channels, stride=per_channel), :] = wide[
+                        pl.ds(source, channels, stride=per_source), :
+                    ]
+    blank = jnp.zeros((spare, arrived.shape[1]), jnp.float32)
+    for channel in range(channels):
+        rows = slice(channel * per_channel, (channel + 1) * per_channel)
+        blocks = [
+            jnp.concatenate([lined[place, rows, :], blank], axis=0) for place in range(near)
         ]
-        spectra = jnp.concatenate(spectra, axis=1).astype(jnp.bfloat16)
-        lined_ref[local] = spectra
-        both = jnp.dot(spectra, weights_ref[local], preferred_element_type=jnp.float32)
-        out_ref[local * per_channel : (local + 1) * per_channel, :] = turn_products(
-            both[:per_channel]
-        ).astype(out_ref.dtype)
-
-
-def partial_beams(received, weights, layout, dtype):
+        spectra[channel] = jnp.concatenate(blocks, axis=1).astype(jnp.bfloat16)
+
+
+def beams_kernel(
+    layout, which, step, pieces, first_ref, code_ref, pointing_ref, weights_ref, spectra_ref,
+    *rest,
+):
     near, cores, channels, frames_here = layout
-    feeds, width = weights.shape[1:]
+    per_channel = 2 * frames_here * cores
+    raw = which == 0
+    if raw:
+        out_ref, spectra, stored, own, total, spectra_sem, sems, arrived, wide, lined = rest
+        fetch = pltpu.make_async_copy(spectra_ref, arrived, spectra_sem)
+    else:
+        out_ref, stored, own, total, spectra_sem, sems, spectra = rest
+        fetch = pltpu.make_async_copy(spectra_ref, spectra, spectra_sem)
+    fetch.start()
+    made_feeds = stored.shape[1]
+    own_rows = own.shape[1]
+    count = channels // pieces
+    copies = []
+    for piece in range(pieces):
+        place = pl.ds(piece * count, count)
+        source = weights_ref.at[place, pl.ds(which * made_feeds, made_feeds)]
+        copies.append(pltpu.make_async_copy(source, stored.at[place], sems.at[piece]))
+    ahead = 5
+    for copy in copies[:ahead]:
+        copy.start()
+
+    block_rows = 32
+    first = chain_start(first_ref[0], channels, step)
+
+    def one_block(index, carry):
+        target = pl.ds(pl.multiple_of(index * block_rows, block_rows), block_rows)
+        source = pl.ds(pl.multiple_of(made_feeds + index * block_rows, block_rows), block_rows)
+        chain_of_weights(first, step, code_ref[source], pointing_ref.at[which], own, target)
+        return carry
+
+    lax.fori_loop(0, own_rows // block_rows, one_block, 0)
+    fetch.wait()
+    if raw:
+        line_up(layout, arrived, wide, lined, spectra)
+
+    for channel in range(channels):
+        rows = slice(channel * per_channel, (channel + 1) * per_channel)
+        total[rows, :] = jnp.dot(
+            spectra[channel, :, made_feeds:], own[channel], preferred_element_type=jnp.float32
+        )[:per_channel]
+    for piece in range(pieces):
+        copies[piece].wait()
+        if piece + ahead < pieces:
+            copies[piece + ahead].start()
+        for channel in range(piece * count, (piece + 1) * count):
+            rows = slice(channel * per_channel, (channel + 1) * per_channel)
+            both = jnp.dot(
+                spectra[channel, :, :made_feeds],
+                stored[channel],
+                preferred_element_type=jnp.float32,
+            )[:per_channel]
+            out_ref[rows, :] = turn_products(total[rows, :] + both).astype(out_ref.dtype)
+
+
+def partial_beams(first, code, pointing, weights, spectra, layout, which, step, dtype):
+    near, cores, channels, frames_here = layout
+    feeds = code.shape[0]
+    made_feeds = weights.shape[1] // pointing.shape[0]
+    width = weights.shape[2]
     per_channel = 2 * cores * frames_here
-    padded = padded_rows(per_channel)
-    together = 8
+    pieces = 8
+    in_vmem = pl.BlockSpec(memory_space=pltpu.VMEM)
+    lined_shape = (channels, padded_rows(per_channel), feeds)
+    out_shape = [jax.ShapeDtypeStruct((channels * per_channel, width // 2), dtype)]
+    scratch = [
+        pltpu.VMEM((channels, made_feeds, width), weights.dtype),
+        pltpu.VMEM((channels, feeds - made_feeds, width), weights.dtype),
+        pltpu.VMEM((channels * per_channel, width), jnp.float32),
+        pltpu.SemaphoreType.DMA,
+        pltpu.SemaphoreType.DMA((pieces,)),
+    ]
+    if which == 0:
+        out_shape.append(jax.ShapeDtypeStruct(lined_shape, jnp.bfloat16))
+        scratch += [
+            pltpu.VMEM(spectra.shape, spectra.dtype),
+            pltpu.VMEM(spectra.shape, jnp.float32),
+            pltpu.VMEM((near, channels * per_channel, feeds // near), jnp.float32),
+        ]
+    else:
+        scratch.append(pltpu.VMEM(lined_shape, jnp.bfloat16))
     return pl.pallas_call(
-        functools.partial(beams_kernel, layout),
-        grid=(channels // together,),
+        functools.partial(beams_kernel, layout, which, step, pieces),
         in_specs=[
-            pl.BlockSpec(received.shape, lambda i: (0, 0)),
-            pl.BlockSpec((together, feeds, width), lambda i: (i, 0, 0)),
+            pl.BlockSpec(memory_space=pltpu.SMEM),
+            in_vmem,
+            in_vmem,
+            pl.BlockSpec(memory_space=pltpu.HBM),
+            pl.BlockSpec(memory_space=pl.ANY if which == 0 else pltpu.HBM),
         ],
-        out_specs=[
-            pl.BlockSpec((together * per_channel, width // 2), lambda i: (i, 0)),
-            pl.BlockSpec((together, padded, feeds), lambda i: (i, 0, 0)),
-        ],
-        out_shape=[
-            jax.ShapeDtypeStruct((channels * per_channel, width // 2), dtype),
-            jax.ShapeDtypeStruct((channels, padded, feeds), jnp.bfloat16),
-        ],
-        scratch_shapes=[
-            pltpu.VMEM(received.shape, jnp.float32),
-            pltpu.VMEM((near, channels * per_channel, feeds // near), jnp.float32),
-        ],
-        compiler_params=VMEM,
+        out_specs=[in_vmem] * len(out_shape),
+        out_shape=out_shape,
+        scratch_shapes=scratch,
+        compiler_params=pltpu.CompilerParams(vmem_limit_bytes=50 * 1024 * 1024),
         cost_estimate=pl.CostEstimate(
             flops=channels * feeds * width * 2 * 128,
-            bytes_accessed=weights.size * 2,
+            bytes_accessed=channels * feeds * width * 2,
             transcendentals=0,
         ),
         name="beams",
-    )(received, weights)
-
-
-def own_beams_kernel(
-    per_channel, step, first_ref, lined_ref, delay_ref, cylinder_ref, pointing_ref, out_ref, total, weights
+    )(first, code, pointing, weights, spectra)
+
+
+def gather_kernel(
+    layout, beams_here, scale, own_ref, other_ref, out_ref, own, other, total, rows, sems
 ):
-    channels, _, feeds = lined_ref.shape
-    _, rows, width = weights.shape
-    block_rows = 32
-    together = 4
-    first = chain_start(first_ref[0], channels, step)
-    for start in range(0, feeds, rows):
-
-        def one_block(index, carry):
-            target = pl.ds(pl.multiple_of(index * block_rows, block_rows), block_rows)
-            source = pl.ds(pl.multiple_of(start + index * block_rows, block_rows), block_rows)
-            chain_of_weights(
-                first, step, delay_ref[source], cylinder_ref[source], pointing_ref, weights, target
-            )
-            return carry
-
-        lax.fori_loop(0, rows // block_rows, one_block, 0)
-
-        def some_channels(index, carry):
-            ids = [index * together + local for local in range(together)]
-            places = [pl.ds(pl.multiple_of(i * per_channel, 8), per_channel) for i in ids]
-            olds = [total[place, :] if start else None for place in places]
-            news = [
-                jnp.dot(
-                    lined_ref[i, :, start : start + rows],
-                    weights[i],
-                    preferred_element_type=jnp.float32,
-                )[:per_channel]
-                for i in ids
-            ]
-            for place, old, new in zip(places, olds, news):
-                value = new if old is None else old + new
-                if start + rows < feeds:
-                    total[place, :] = value
-                else:
-                    out_ref[place, :] = turn_products(value)
-            return carry
-
-        lax.fori_loop(0, channels // together, some_channels, 0)
-
-
-def own_beams(first, lined, delay, cylinder, pointing, per_channel, step):
-    channels, _, feeds = lined.shape
-    beams = pointing.shape[1]
-    rows = 256
-    in_vmem = pl.BlockSpec(memory_space=pltpu.VMEM)
-    return pl.pallas_call(
-        functools.partial(own_beams_kernel, per_channel, step),
-        in_specs=[pl.BlockSpec(memory_space=pltpu.SMEM)] + [in_vmem] * 4,
-        out_specs=in_vmem,
-        out_shape=jax.ShapeDtypeStruct((channels * per_channel, beams), jnp.float32),
-        scratch_shapes=[
-            pltpu.VMEM((channels * per_channel, 2 * beams), jnp.float32),
-            pltpu.VMEM((channels, rows, 2 * beams), jnp.bfloat16),
-        ],
-        compiler_params=VMEM,
-        cost_estimate=pl.CostEstimate(
-            flops=channels * feeds * beams * 4 * 128,
-            bytes_accessed=channels * feeds * beams * 4,
-            transcendentals=0,
-        ),
-        name="own_beams",
-    )(first, lined, delay, cylinder, pointing)
-
-
-def gather_kernel(layout, beams_here, scale, own_ref, other_ref, out_ref, total, rows):
     near, cores, channels, frames_here = layout
     lane_channels = LANES // beams_here
     per_core = 2 * frames_here
     per_channel = per_core * cores
     groups = channels // lane_channels
-    total[...] = (own_ref[...] + other_ref[...].astype(jnp.float32)) * scale
+    fetches = [
+        pltpu.make_async_copy(own_ref, own, sems.at[0]),
+        pltpu.make_async_copy(other_ref, other, sems.at[1]),
+    ]
+    for fetch in fetches:
+        fetch.start()
+    for fetch in fetches:
+        fetch.wait()
+    total[...] = (own[...] + other[...].astype(jnp.float32)) * scale
     for group in range(groups):
         values = [
             total[pl.ds((group * lane_channels + sub) * per_channel, per_channel), :]
@@ -521,22 +577,42 @@
     total_rows = near * cores * channels // (LANES // beams_here) * 2 * frames_here
     return pl.pallas_call(
         functools.partial(gather_kernel, layout, beams_here, scale),
+        in_specs=[pl.BlockSpec(memory_space=pltpu.HBM), pl.BlockSpec(memory_space=pl.ANY)],
         out_shape=jax.ShapeDtypeStruct((total_rows, LANES), jnp.bfloat16),
         scratch_shapes=[
+            pltpu.VMEM(own.shape, own.dtype),
+            pltpu.VMEM(other.shape, other.dtype),
             pltpu.VMEM(own.shape, jnp.float32),
             pltpu.VMEM((total_rows, LANES), jnp.float32),
+            pltpu.SemaphoreType.DMA((2,)),
         ],
-        compiler_params=VMEM,
+        compiler_params=pltpu.CompilerParams(vmem_limit_bytes=16 * 1024 * 1024),
         name="gather",
     )(own, other)
 
 
-def series_kernel(beams_here, received_ref, cos_ref, sin_ref, basis_ref, out_ref, wide, lined):
+def series_kernel(
+    beams_here, half_ref, received_ref, cos_ref, sin_ref, basis_ref, out_ref,
+    arrived, basis, wide, lined, sems,
+):
     frames_here = out_ref.shape[0]
     kappas = cos_ref.shape[0]
     lane_channels = LANES // beams_here
     side = kappas // 2
-    wide[...] = received_ref[...].astype(jnp.float32)
+    half = half_ref[0]
+    sign = (1 - 2 * half).astype(jnp.float32)
+    fetch = pltpu.make_async_copy(received_ref, arrived, sems.at[2])
+    fetch.start()
+    fetch_basis = [
+        pltpu.make_async_copy(
+            basis_ref.at[parity + half * (1 - 2 * parity)], basis.at[parity], sems.at[parity]
+        )
+        for parity in range(2)
+    ]
+    for copy in fetch_basis:
+        copy.start()
+    fetch.wait()
+    wide[...] = arrived[...].astype(jnp.float32)
     for index in range(frames_here):
         real = wide[pl.ds(index, kappas, stride=2 * frames_here), :]
         imag = wide[pl.ds(frames_here + index, kappas, stride=2 * frames_here), :]
@@ -558,33 +634,42 @@
     for parity in range(2):
         high = lined[parity, 0]
         low = lined[parity, 1]
+        fetch_basis[parity].wait()
         sides.append(
-            jnp.dot(high, basis_ref[parity, 0], preferred_element_type=jnp.float32)
-            + jnp.dot(low, basis_ref[parity, 0], preferred_element_type=jnp.float32)
-            + jnp.dot(high, basis_ref[parity, 1], preferred_element_type=jnp.float32)
+            jnp.dot(high, basis[parity, 0], preferred_element_type=jnp.float32)
+            + jnp.dot(low, basis[parity, 0], preferred_element_type=jnp.float32)
+            + jnp.dot(high, basis[parity, 1], preferred_element_type=jnp.float32)
         )
     times = sides[0].shape[1] // 2
     for part in range(2):
         even = sides[0][:, part * times : (part + 1) * times]
         odd = sides[1][:, part * times : (part + 1) * times]
-        for which, value in enumerate((even + odd, even - odd)):
+        for which, value in enumerate((even + odd, (even - odd) * sign)):
             start = (2 * part + which) * times
             out_ref[:, :, start : start + times] = value.reshape(frames_here, beams_here, times)
 
 
-def make_series(received, chirp_cos, chirp_sin, basis, beams_here, frames_here):
+def make_series(half_index, received, chirp_cos, chirp_sin, basis, beams_here, frames_here):
+    in_vmem = pl.BlockSpec(memory_space=pltpu.VMEM)
+    anywhere = pl.BlockSpec(memory_space=pl.ANY)
     series = pl.pallas_call(
         functools.partial(series_kernel, beams_here),
+        in_specs=[
+            pl.BlockSpec(memory_space=pltpu.SMEM), anywhere, in_vmem, in_vmem, anywhere,
+        ],
         out_shape=jax.ShapeDtypeStruct(
             (frames_here, beams_here, 2 * basis.shape[3]), jnp.float32
         ),
         scratch_shapes=[
+            pltpu.VMEM(received.shape, received.dtype),
+            pltpu.VMEM(basis.shape, basis.dtype),
             pltpu.VMEM(received.shape, jnp.float32),
             pltpu.VMEM((2, 2, frames_here * beams_here, basis.shape[2]), jnp.bfloat16),
+            pltpu.SemaphoreType.DMA((3,)),
         ],
-        compiler_params=VMEM,
+        compiler_params=pltpu.CompilerParams(vmem_limit_bytes=24 * 1024 * 1024),
         name="series",
-    )(received, chirp_cos, chirp_sin, basis)
+    )(half_index, received, chirp_cos, chirp_sin, basis)
     return jnp.transpose(series, (1, 0, 2))
 
 
@@ -606,29 +691,39 @@
     half_index = lax.axis_index("half")
     place = lax.axis_index(GROUP)
 
-    tail = from_behind(samples[:, (frames_here - (TAPS - 1)) * length :], "tm", 1)
+    tail = from_behind(last_samples(samples, (TAPS - 1) * length), "tm", 1)
     forward = jnp.asarray(folded_forward_basis(length))
-    spectra = spectra_rows(samples, tail, filter_taps, forward)
+    half_scalar = jnp.reshape(half_index, (1,)).astype(jnp.int32)
+    spectra = spectra_rows(half_scalar, samples, tail, filter_taps, forward)
     spectra = spectra.reshape(group, channels * 2 * frames_here, feed_here)
     received = lax.all_to_all(spectra, GROUP, 0, 0, tiled=True)
     received = received.reshape(-1, feed_here)
 
     in_parity = group // 2
-    first = 2 * (place % in_parity) * channels + place // in_parity + 1
+    first = 2 * (place % in_parity) * channels + (place // in_parity ^ half_index) + 1
     first = jnp.reshape(first, (1,)).astype(jnp.int32)
-    delay = lax.dynamic_slice_in_dim(feed_delay, half_index * half_feeds, half_feeds)
-    delay = jnp.broadcast_to(delay.astype(jnp.float32)[:, None], (half_feeds, LANES))
-    cylinder = lax.dynamic_slice_in_dim(feed_cylinder, half_index * half_feeds, half_feeds)
-    cylinder = jnp.broadcast_to(cylinder[:, None], (half_feeds, LANES))
+    code = feed_cylinder * PHASES + feed_delay
+    code = lax.dynamic_slice_in_dim(code, half_index * half_feeds, half_feeds)
+    code = jnp.broadcast_to(code[:, None], (half_feeds, LANES))
     aim = jnp.transpose(pointing).astype(jnp.float32)
-    own_aim = lax.dynamic_slice_in_dim(aim, half_index * half_beams, half_beams, 1)
-    other_aim = lax.dynamic_slice_in_dim(aim, (1 - half_index) * half_beams, half_beams, 1)
-
-    other_weights = make_weights(first, delay, cylinder, other_aim, channels, 2)
-    to_send, lined = partial_beams(received, other_weights, layout, jnp.bfloat16)
-    swap = [(i, HALVES - 1 - i) for i in range(HALVES)]
-    arrived = lax.ppermute(to_send, "half", swap)
-    own = own_beams(first, lined, delay, cylinder, own_aim, 2 * cores * frames_here, 2)
+    aims = jnp.stack(
+        [
+            lax.dynamic_slice_in_dim(aim, half * half_beams, half_beams, 1)
+            for half in (1 - half_index, half_index)
+        ]
+    )
+    step = 2
+    weights = make_weights(first, code, aims, channels, step, half_feeds * 3 // 4)
+    to_send, lined = partial_beams(
+        first, code, aims, weights, received, layout, 0, step, jnp.bfloat16
+    )
+    swap = [
+        (half * near + i, (1 - half) * near + (i + near // 2) % near)
+        for half in range(HALVES)
+        for i in range(near)
+    ]
+    arrived = lax.ppermute(to_send, ("half", "near"), swap)
+    (own,) = partial_beams(first, code, aims, weights, lined, layout, 1, step, jnp.float32)
     gathered = gather_beams(own, arrived, layout, beams_here, 1.0 / math.sqrt(feeds))
     lane_channels = LANES // beams_here
     gathered = gathered.reshape(group, -1, LANES)
@@ -637,13 +732,13 @@
     kappa = jnp.arange(nchan // lane_channels, dtype=jnp.int32)[:, None]
     sub = jnp.arange(LANES, dtype=jnp.int32)[None, :] // beams_here
     side = nchan // lane_channels // 2
-    channel = 2 * (lane_channels * (kappa % side) + sub) + kappa // side
+    channel = 2 * (lane_channels * (kappa % side) + sub) + (kappa // side ^ half_index)
     position = channel.astype(jnp.float32) / nchan
     rate = jnp.tile(jnp.pi * chirp_rate, lane_channels)[None, :]
     chirp = rate * (position * position)
     inverse = jnp.asarray(folded_inverse_basis(nchan, lane_channels))
     return make_series(
-        returned, jnp.cos(chirp), jnp.sin(chirp), inverse, beams_here, frames_here
+        half_scalar, returned, jnp.cos(chirp), jnp.sin(chirp), inverse, beams_here, frames_here
     )
 
 

time: 103 us -> 92.3 us (0.90)
  Pallas kernels: 63.6 us -> 52 us
  starting transfers between devices: 14.7 us -> 22.2 us
  waiting for transfers between devices: 15.6 us -> 10.5 us
  local copies, waits for them, and re-layouts: 7.46 us -> 5.73 us
    pallas_call x5 -> x6, Pallas kernels: 60.9 us -> 50.2 us  [the longest x1 21.1 us: make_weights(): pl.pallas_call(functools.partial(weights_kernel, 32, step), grid=(sets *...]
    all_to_all x1, starting transfers between devices: 3.91 us -> 9.85 us  [halves_body(): lax.all_to_all(gathered, GROUP, 0, 0, tiled=True).reshape(-1, LANES)]
    all_to_all x1, waiting for transfers between devices: 5.73 us -> 0.01 us  [halves_body(): received = lax.all_to_all(spectra, GROUP, 0, 0, tiled=True)]
    ppermute x1, starting transfers between devices: 2.59 us -> 3.99 us  [halves_body(): arrived = lax.ppermute(to_send, ('half', 'near'), swap)]
    slice x1 -> x0, local copies, waits for them, and re-layouts: 1.18 us -> none  [halves_body(): samples[:, (frames_here - (TAPS - 1)) * length:]]
    unnamed x16 -> x24, local copies, waits for them, and re-layouts: 3.58 us -> 4.64 us
  transfers between devices with their start and end apart: 4 -> 4, of which waited for: 3 -> 2; matrix products, arithmetic and copies ran while one was open for 4% -> 2% of each run, Pallas kernels for 34% -> 33%
where the time goes in v3:
time: 92.3 us; the launch traced here: 91.9 us
  Pallas kernels  52 us (56%)
  starting transfers between devices  22.2 us (24%)
  waiting for transfers between devices  10.5 us (11%)
  local copies, waits for them, and re-layouts  5.73 us (6%)
  other arithmetic  0.96 us (1%)
    pallas_call x1, Pallas kernels, make_weights(): pl.pallas_call(functools.partial(weights_kernel, 32, step), grid=(sets *...  21.1 us
    pallas_call x2, Pallas kernels, partial_beams(): pl.pallas_call(functools.partial(beams_kernel, layout, which, step, piece...  19.7 us
    all_to_all x1, starting transfers between devices, halves_body(): lax.all_to_all(gathered, GROUP, 0, 0, tiled=True).reshape(-1, LANES)  9.85 us
    all_to_all x1, waiting for transfers between devices, halves_body(): lax.all_to_all(gathered, GROUP, 0, 0, tiled=True).reshape(-1, LANES)  8.68 us
    pallas_call x1, Pallas kernels, spectra_rows(): pl.pallas_call(functools.partial(spectra_kernel, frames_here), in_specs=[...  6.73 us
    all_to_all x1, starting transfers between devices, halves_body(): received = lax.all_to_all(spectra, GROUP, 0, 0, tiled=True)  5.84 us
    unnamed x24, local copies, waits for them, and re-layouts  4.64 us
    ppermute x1, starting transfers between devices, halves_body(): arrived = lax.ppermute(to_send, ('half', 'near'), swap)  3.99 us
  transfers between devices with their start and end apart: 4, of which 2 were waited for; matrix products, arithmetic and copies ran while one was open for 2% of the time, Pallas kernels for 33%

profile of v3, /device:TPU:0, one launch (start us, length us, event | category | flops | bytes accessed | tf_op | source)
XLA Modules:
  0.0 91.9 jit_solution(15029363050167411096)
XLA Ops:
  0.0 0.0 copy-start.1
  0.0 1.4 %copy-done.1 = bf16[128,6144]{1,0:T(8,128)(2,1)S(1)} copy-done((bf16[128,6144]{1,0:T(8,128)(2,1)S(1)}, bf16[128,6144]{1,0:T(8,128)(2,1)}, u32[]{:S(2)}) %copy-start.1) | copy-done | bytes 1572888
  1.4 0.0 copy-start.2
  1.4 0.0 copy-start.7
  1.4 0.1 tail.1
  1.5 2.5 %collective-permute-start = (bf16[128,3072]{1,0:T(8,128)(2,1)S(1)}, bf16[128,3072]{1,0:T(8,128)(2,1)S(1)}, u32[]{:S(2)}, u32[]{:S(2)}) collective-permute-start(bf16[128,3072]{1,0:T(8,128)(2,1)S(1)} %tail.1), channel_id=1, source_target_pairs={{0,1},{2,3},{4,5},{6,7},{8,9},{10,11},{12,13},{14,15},{16,17},{18,... | collective-permute-start | bytes 2359304 | tf_op jit(solution)/shard_map/ppermute | solution.py:24
  4.0 1.8 %collective-permute-done.tail_ref = bf16[128,3072]{1,0:T(8,128)(2,1)S(1)} collective-permute-done((bf16[128,3072]{1,0:T(8,128)(2,1)S(1)}, bf16[128,3072]{1,0:T(8,128)(2,1)S(1)}, u32[]{:S(2)}, u32[]{:S(2)}) %collective-permute-start) | collective-permute-done | bytes 786464 | tf_op jit(solution)/shard_map/ppermute | solution.py:24
  5.9 0.0 copy-done.2
  5.9 0.0 copy-done.7
  5.9 0.0 copy-start.3
  5.9 1.6 %copy-done.3 = bf16[2,2,512,512]{3,2,1,0:T(8,128)(2,1)S(1)} copy-done((bf16[2,2,512,512]{3,2,1,0:T(8,128)(2,1)S(1)}, bf16[2,2,512,512]{3,2,1,0:T(8,128)(2,1)}, u32[]{:S(2)}) %copy-start.3) | copy-done | bytes 2097176
  7.5 6.7 %spectra.1 = bf16[6144,128]{1,0:T(8,128)(2,1)} custom-call(s32[1]{0:T(128)} %bitcast.half_ref, bf16[128,6144]{1,0:T(8,128)(2,1)S(1)} %copy-done.2, bf16[128,3072]{1,0:T(8,128)(2,1)S(1)} %collective-permute-done.tail_ref, f32[4,1024]{1,0:T(4,128)S(1)} %copy-done.7, bf16[2,2,512,512]{3,2,1,0:T(8,128)(2,1)S(1)} %copy-done.3), custom_call_target="tpu_custom_call" | custom-call | tf_op jit(solution)/shard_map/spectra/pallas_call | solution.py:265
  14.2 0.0 copy-start.8
  14.2 0.0 copy-start.9
  14.2 0.0 copy-start.10
  14.3 5.8 %all-to-all-start = ((bf16[16,384,128]{2,1,0:T(8,128)(2,1)}), bf16[16,384,128]{2,1,0:T(8,128)(2,1)S(1)}, u32[]{:S(2)}, u32[]{:S(2)}) async-start(bf16[16,384,128]{2,1,0:T(8,128)(2,1)} %bitcast.6), calls=%async_computation | async-start | bytes 3145728 | tf_op jit(solution)/shard_map/all_to_all | solution.py:699
  20.1 0.0 copy-done.8
  20.2 0.0 copy-done.9
  20.2 0.0 copy-done.10
  20.2 0.6 pad_maximum_fusion.pointing_ref
  20.8 1.0 %broadcast_in_dim.2.code_ref = s32[1024,128]{1,0:T(8,128)} broadcast(s32[1024]{0:T(1024)S(1)} %dynamic-slice_add_fusion), dimensions={0} | broadcast | bytes 528384 | tf_op jit(solution)/shard_map/broadcast_in_dim | solution.py:707
  21.8 0.0 copy-start
  21.8 0.0 copy-start.6
  21.8 21.1 %weights.1.weights_ref = bf16[32,1536,512]{2,1,0:T(8,128)(2,1)} custom-call(s32[1]{0:T(128)} %bitcast.1.first_ref, s32[1024,128]{1,0:T(8,128)} %broadcast_in_dim.2.code_ref, f32[2,4,256]{2,1,0:T(4,128)} %pad_maximum_fusion.pointing_ref), custom_call_target="tpu_custom_call" | custom-call | flops 100663296 | bytes 50331648 | tf_op jit(solution)/shard_map/weights/pallas_call | solution.py:377
  43.0 0.0 all-to-all-done
  43.0 0.0 copy-done
  43.0 0.0 copy-done.6
  43.0 10.4 %beams.2 = (bf16[768,256]{1,0:T(8,128)(2,1)S(1)}, bf16[32,32,1024]{2,1,0:T(8,128)(2,1)}) custom-call(s32[1]{0:T(128)} %bitcast.1.first_ref, s32[1024,128]{1,0:T(8,128)S(1)} %copy-done, f32[2,4,256]{2,1,0:T(4,128)S(1)} %copy-done.6, bf16[32,1536,512]{2,1,0:T(8,128)(2,1)} %weights.1.weights_ref, bf16[6144,128]{1,0:T(8,128)(2,1)S(1)} %bitcast.15), custom_call_target="tpu_custom_call" | custom-call | flops 4294967296 | bytes 33554432 | tf_op jit(solution)/shard_map/beams/pallas_call | solution.py:518
  53.4 4.0 %collective-permute-start.1 = (bf16[768,256]{1,0:T(8,128)(2,1)S(1)}, bf16[768,256]{1,0:T(8,128)(2,1)S(1)}, u32[]{:S(2)}, u32[]{:S(2)}) collective-permute-start(bf16[768,256]{1,0:T(8,128)(2,1)S(1)} %get-tuple-element.8), channel_id=1, source_target_pairs={{0,24},{2,26},{4,28},{6,30},{8,16},{10,18},{12,20},{14,22},{16,8},... | collective-permute-start | bytes 1179656 | tf_op jit(solution)/shard_map/ppermute | solution.py:725
  57.4 0.0 copy-start.4
  57.4 1.6 %copy-done.4 = bf16[32,32,1024]{2,1,0:T(8,128)(2,1)S(1)} copy-done((bf16[32,32,1024]{2,1,0:T(8,128)(2,1)S(1)}, bf16[32,32,1024]{2,1,0:T(8,128)(2,1)}, u32[]{:S(2)}) %copy-start.4) | copy-done | bytes 2097176
  59.0 9.3 %beams.3.own_ref = f32[768,256]{1,0:T(8,128)S(1)} custom-call(s32[1]{0:T(128)} %bitcast.1.first_ref, s32[1024,128]{1,0:T(8,128)S(1)} %copy-done, f32[2,4,256]{2,1,0:T(4,128)S(1)} %copy-done.6, bf16[32,1536,512]{2,1,0:T(8,128)(2,1)} %weights.1.weights_ref, bf16[32,32,1024]{2,1,0:T(8,128)(2,1)S(1)} %copy-done.4), custom_call_target="tpu_custom_call" | custom-call | flops 4294967296 | bytes 33554432 | tf_op jit(solution)/shard_map/beams/pallas_call | solution.py:518
  68.3 0.0 copy-start.11
  68.3 0.0 copy-start.5
  68.3 0.0 collective-permute-done.1.other_ref
  68.3 1.8 %gather.1 = bf16[1536,128]{1,0:T(8,128)(2,1)} custom-call(f32[768,256]{1,0:T(8,128)S(1)} %beams.3.own_ref, bf16[768,256]{1,0:T(8,128)(2,1)S(1)} %collective-permute-done.1.other_ref), custom_call_target="tpu_custom_call" | custom-call | tf_op jit(solution)/shard_map/gather/pallas_call | solution.py:578
  70.1 9.8 %all-to-all-start.1 = ((bf16[16,96,128]{2,1,0:T(8,128)(2,1)}), bf16[16,96,128]{2,1,0:T(8,128)(2,1)S(1)}, u32[]{:S(2)}, u32[]{:S(2)}) async-start(bf16[16,96,128]{2,1,0:T(8,128)(2,1)} %bitcast.8), calls=%async_computation.1 | async-start | bytes 786432 | tf_op jit(solution)/shard_map/all_to_all | solution.py:730
  79.9 0.0 copy-done.11
  80.0 0.1 mul.67
  80.1 0.3 fusion
  80.4 8.7 %all-to-all-done.1 = bf16[16,96,128]{2,1,0:T(8,128)(2,1)S(1)} async-done(((bf16[16,96,128]{2,1,0:T(8,128)(2,1)}), bf16[16,96,128]{2,1,0:T(8,128)(2,1)S(1)}, u32[]{:S(2)}, u32[]{:S(2)}) %all-to-all-start.1) | async-done | bytes 393248 | tf_op jit(solution)/shard_map/all_to_all | solution.py:730
  89.1 0.0 copy-done.5
  89.1 2.6 %series.1 = f32[6,32,1024]{2,1,0:T(8,128)} custom-call(s32[1]{0:T(128)} %bitcast.half_ref, bf16[1536,128]{1,0:T(8,128)(2,1)S(1)} %bitcast.16, f32[128,128]{1,0:T(8,128)S(1)} %get-tuple-element.12.cos_ref, f32[128,128]{1,0:T(8,128)S(1)} %get-tuple-element.11.sin_ref, bf16[2,2,512,512]{3,2,1,0:T(8,128)(2,1)S(1)} %copy-done.5), custom_call_target="tpu_custom_call" | custom-call | tf_op jit(solution)/shard_map/series/pallas_call | solution.py:655
  (7 shorter events, 0.0 us)
Async XLA Ops:
  0.0 1.4 %copy-start.1 = (bf16[128,6144]{1,0:T(8,128)(2,1)S(1)}, bf16[128,6144]{1,0:T(8,128)(2,1)}, u32[]{:S(2)}) copy-start(bf16[128,6144]{1,0:T(8,128)(2,1)} %samples_ref.3) | copy-start | bytes 4718596
  1.4 4.5 %copy-start.2 = (bf16[128,6144]{1,0:T(8,128)(2,1)S(1)}, bf16[128,6144]{1,0:T(8,128)(2,1)}, u32[]{:S(2)}) copy-start(bf16[128,6144]{1,0:T(8,128)(2,1)} %samples_ref.3) | copy-start | bytes 4718596
  1.4 4.5 %copy-start.7 = (f32[4,1024]{1,0:T(4,128)S(1)}, f32[4,1024]{1,0:T(4,128)}, u32[]{:S(2)}) copy-start(f32[4,1024]{1,0:T(4,128)} %taps_in_ref.1) | copy-start | bytes 49156
  1.5 4.4 %collective-permute-start = (bf16[128,3072]{1,0:T(8,128)(2,1)S(1)}, bf16[128,3072]{1,0:T(8,128)(2,1)S(1)}, u32[]{:S(2)}, u32[]{:S(2)}) collective-permute-start(bf16[128,3072]{1,0:T(8,128)(2,1)S(1)} %tail.1), channel_id=1, source_target_pairs={{0,1},{2,3},{4,5},{6,7},{8,9},{10,11},{12,13},{14,15},{16,17},{18,... | collective-permute-start | bytes 2359304 | tf_op jit(solution)/shard_map/ppermute | solution.py:24
  5.9 1.6 %copy-start.3 = (bf16[2,2,512,512]{3,2,1,0:T(8,128)(2,1)S(1)}, bf16[2,2,512,512]{3,2,1,0:T(8,128)(2,1)}, u32[]{:S(2)}) copy-start(bf16[2,2,512,512]{3,2,1,0:T(8,128)(2,1)} %constant.108.clone.basis_ref) | copy-start | bytes 6291460
  14.2 5.9 %copy-start.8 = (s32[512,4]{0,1:T(4,128)S(1)}, s32[512,4]{0,1:T(4,128)}, u32[]{:S(2)}) copy-start(s32[512,4]{0,1:T(4,128)} %param.12) | copy-start | bytes 24580
  14.2 5.9 %copy-start.9 = (s32[2048]{0:T(1024)S(1)}, s32[2048]{0:T(1024)}, u32[]{:S(2)}) copy-start(s32[2048]{0:T(1024)} %param.11) | copy-start | bytes 24580
  14.2 5.9 %copy-start.10 = (s32[2048]{0:T(1024)S(1)}, s32[2048]{0:T(1024)}, u32[]{:S(2)}) copy-start(s32[2048]{0:T(1024)} %param.10) | copy-start | bytes 24580
  14.3 28.7 %all-to-all-start = ((bf16[16,384,128]{2,1,0:T(8,128)(2,1)}), bf16[16,384,128]{2,1,0:T(8,128)(2,1)S(1)}, u32[]{:S(2)}, u32[]{:S(2)}) async-start(bf16[16,384,128]{2,1,0:T(8,128)(2,1)} %bitcast.6), calls=%async_computation | async-start | bytes 3145728 | tf_op jit(solution)/shard_map/all_to_all | solution.py:699
  21.8 21.2 %copy-start = (s32[1024,128]{1,0:T(8,128)S(1)}, s32[1024,128]{1,0:T(8,128)}, u32[]{:S(2)}) copy-start(s32[1024,128]{1,0:T(8,128)} %broadcast_in_dim.2.code_ref) | copy-start | bytes 1572868
  21.8 21.2 %copy-start.6 = (f32[2,4,256]{2,1,0:T(4,128)S(1)}, f32[2,4,256]{2,1,0:T(4,128)}, u32[]{:S(2)}) copy-start(f32[2,4,256]{2,1,0:T(4,128)} %pad_maximum_fusion.pointing_ref) | copy-start | bytes 24580
  53.4 14.9 %collective-permute-start.1 = (bf16[768,256]{1,0:T(8,128)(2,1)S(1)}, bf16[768,256]{1,0:T(8,128)(2,1)S(1)}, u32[]{:S(2)}, u32[]{:S(2)}) collective-permute-start(bf16[768,256]{1,0:T(8,128)(2,1)S(1)} %get-tuple-element.8), channel_id=1, source_target_pairs={{0,24},{2,26},{4,28},{6,30},{8,16},{10,18},{12,20},{14,22},{16,8},... | collective-permute-start | bytes 1179656 | tf_op jit(solution)/shard_map/ppermute | solution.py:725
  57.4 1.6 %copy-start.4 = (bf16[32,32,1024]{2,1,0:T(8,128)(2,1)S(1)}, bf16[32,32,1024]{2,1,0:T(8,128)(2,1)}, u32[]{:S(2)}) copy-start(bf16[32,32,1024]{2,1,0:T(8,128)(2,1)} %get-tuple-element.7.spectra_ref) | copy-start | bytes 6291460
  68.3 11.7 %copy-start.11 = (f32[32]{0:T(128)S(1)}, f32[32]{0:T(128)}, u32[]{:S(2)}) copy-start(f32[32]{0:T(128)} %param.13) | copy-start | bytes 388
  68.3 20.8 %copy-start.5 = (bf16[2,2,512,512]{3,2,1,0:T(8,128)(2,1)S(1)}, bf16[2,2,512,512]{3,2,1,0:T(8,128)(2,1)}, u32[]{:S(2)}) copy-start(bf16[2,2,512,512]{3,2,1,0:T(8,128)(2,1)} %constant.109.clone.basis_ref) | copy-start | bytes 6291460
  70.1 19.0 %all-to-all-start.1 = ((bf16[16,96,128]{2,1,0:T(8,128)(2,1)}), bf16[16,96,128]{2,1,0:T(8,128)(2,1)S(1)}, u32[]{:S(2)}, u32[]{:S(2)}) async-start(bf16[16,96,128]{2,1,0:T(8,128)(2,1)} %bitcast.8), calls=%async_computation.1 | async-start | bytes 786432 | tf_op jit(solution)/shard_map/all_to_all | solution.py:730

commit v4 on v3

--- a/solution.py
+++ b/solution.py
@@ -171,8 +171,8 @@
 
 
 def spectra_kernel(
-    frames_here, half_ref, samples_ref, tail_ref, taps_in_ref, basis_ref, out_ref,
-    samples, tail, taps_ref, basis, folded, rows, packed, in_sems, out_sems,
+    frames_here, group, half_ref, samples_ref, tail_ref, taps_in_ref, basis_ref, out_ref,
+    samples, tail, taps_ref, basis, folded, packed, in_sems, out_sems,
 ):
     feed_here = samples_ref.shape[0]
     length = taps_ref.shape[1]
@@ -224,9 +224,10 @@
                     value - high.astype(jnp.float32)
                 ).astype(jnp.bfloat16)
 
-    per_channel = 2 * frames_here
+    parts = 2 * frames_here
     together = 2
     count = half // 2
+    channels = length // 2 // group
     stores = []
     for parity in range(2):
         fetch_basis[parity].wait()
@@ -238,16 +239,18 @@
                 dot_nt(basis[parity, 0], high)
                 + dot_nt(basis[parity, 1], high)
                 + dot_nt(basis[parity, 0], low)
-            )
+            ).astype(jnp.bfloat16)
             for part in range(2):
                 for ahead in range(together):
-                    start = parity * count * per_channel + part * frames_here + first + ahead
-                    rows[pl.ds(start, count, stride=per_channel), :] = result[
-                        part * count : (part + 1) * count,
-                        ahead * feed_here : (ahead + 1) * feed_here,
-                    ]
-        block = pl.ds(parity * count * per_channel, count * per_channel)
-        packed[block, :] = rows[block, :].astype(jnp.bfloat16)
+                    row = part * frames_here + first + ahead
+                    for place in range(count // channels):
+                        target = (parity * (count // channels) + place) * parts + row
+                        source = part * count + place * channels
+                        packed[pl.ds(target * channels, channels), :] = result[
+                            source : source + channels,
+                            ahead * feed_here : (ahead + 1) * feed_here,
+                        ]
+        block = pl.ds(parity * count * parts, count * parts)
         store = pltpu.make_async_copy(packed.at[block], out_ref.at[block], out_sems.at[parity])
         store.start()
         stores.append(store)
@@ -255,7 +258,7 @@
         store.wait()
 
 
-def spectra_rows(half_index, samples, tail, taps, basis):
+def spectra_rows(half_index, samples, tail, taps, basis, group):
     feed_here = samples.shape[0]
     length = taps.shape[1]
     frames_here = samples.shape[1] // length
@@ -263,7 +266,7 @@
     anywhere = pl.BlockSpec(memory_space=pl.ANY)
     in_hbm = pl.BlockSpec(memory_space=pltpu.HBM)
     return pl.pallas_call(
-        functools.partial(spectra_kernel, frames_here),
+        functools.partial(spectra_kernel, frames_here, group),
         in_specs=[pl.BlockSpec(memory_space=pltpu.SMEM), in_hbm, anywhere, in_hbm, in_hbm],
         out_specs=anywhere,
         out_shape=jax.ShapeDtypeStruct((total_rows, feed_here), jnp.bfloat16),
@@ -273,34 +276,13 @@
             pltpu.VMEM(taps.shape, taps.dtype),
             pltpu.VMEM(basis.shape, basis.dtype),
             pltpu.VMEM((2, 2, frames_here * feed_here, length // 2), jnp.bfloat16),
-            pltpu.VMEM((total_rows, feed_here), jnp.float32),
             pltpu.VMEM((total_rows, feed_here), jnp.bfloat16),
             pltpu.SemaphoreType.DMA((5,)),
             pltpu.SemaphoreType.DMA((2,)),
         ],
-        compiler_params=pltpu.CompilerParams(vmem_limit_bytes=24 * 1024 * 1024),
+        compiler_params=pltpu.CompilerParams(vmem_limit_bytes=50 * 1024 * 1024),
         name="spectra",
     )(half_index, samples, tail, taps, basis)
-
-
-def tail_kernel(samples_ref, out_ref, sem):
-    count = out_ref.shape[1]
-    where = pl.ds(samples_ref.shape[1] - count, count)
-    copy = pltpu.make_async_copy(samples_ref.at[:, where], out_ref, sem)
-    copy.start()
-    copy.wait()
-
-
-def last_samples(samples, count):
-    return pl.pallas_call(
-        tail_kernel,
-        in_specs=[pl.BlockSpec(memory_space=pltpu.HBM)],
-        out_specs=pl.BlockSpec(memory_space=pl.ANY),
-        out_shape=jax.ShapeDtypeStruct((samples.shape[0], count), samples.dtype),
-        scratch_shapes=[pltpu.SemaphoreType.DMA],
-        compiler_params=pltpu.CompilerParams(vmem_limit_bytes=4 * 1024 * 1024),
-        name="tail",
-    )(samples)
 
 
 def sine_turns(turns):
@@ -371,23 +353,23 @@
 
 
 def make_weights(first, code, pointing, channels, step, feeds):
-    sets, cylinders, beams = pointing.shape
+    _, cylinders, beams = pointing.shape
     rows = 128
-    tiles = feeds // rows
+    tiles = [count // rows for count in feeds]
     return pl.pallas_call(
         functools.partial(weights_kernel, 32, step),
-        grid=(sets * tiles,),
+        grid=(sum(tiles),),
         in_specs=[
             pl.BlockSpec(memory_space=pltpu.SMEM),
-            pl.BlockSpec((rows, LANES), lambda i: (i % tiles, 0)),
-            pl.BlockSpec((1, cylinders, beams), lambda i: (i // tiles, 0, 0)),
+            pl.BlockSpec((rows, LANES), lambda i: (jnp.where(i < tiles[0], i, i - tiles[0]), 0)),
+            pl.BlockSpec((1, cylinders, beams), lambda i: (jnp.where(i < tiles[0], 0, 1), 0, 0)),
         ],
         out_specs=pl.BlockSpec((channels, rows, 2 * beams), lambda i: (0, i, 0)),
-        out_shape=jax.ShapeDtypeStruct((channels, sets * feeds, 2 * beams), jnp.bfloat16),
+        out_shape=jax.ShapeDtypeStruct((channels, sum(feeds), 2 * beams), jnp.bfloat16),
         compiler_params=VMEM,
         cost_estimate=pl.CostEstimate(
-            flops=channels * sets * feeds * beams * 8,
-            bytes_accessed=channels * sets * feeds * beams * 4,
+            flops=channels * sum(feeds) * beams * 8,
+            bytes_accessed=channels * sum(feeds) * beams * 4,
             transcendentals=0,
         ),
         name="weights",
@@ -405,22 +387,21 @@
     return both[:, :beams] + jnp.concatenate([-by_imag[half:], by_imag[:half]], axis=0)
 
 
-def line_up(layout, arrived, wide, lined, spectra):
+def line_up(layout, arrived, lined, spectra):
     near, cores, channels, frames_here = layout
     per_source = 2 * frames_here
     per_channel = per_source * cores
     spare = spectra.shape[1] - per_channel
-    wide[...] = arrived[...].astype(jnp.float32)
     for place in range(near):
         for core in range(cores):
-            base = (place * cores + core) * channels * per_source
+            base = (place * cores + core) * per_source
             for part in range(2):
                 for index in range(frames_here):
-                    source = base + part * frames_here + index
+                    source = (base + part * frames_here + index) * channels
                     target = (part * cores + core) * frames_here + index
-                    lined[place, pl.ds(target, channels, stride=per_channel), :] = wide[
-                        pl.ds(source, channels, stride=per_source), :
-                    ]
+                    lined[place, pl.ds(target, channels, stride=per_channel), :] = arrived[
+                        pl.ds(source, channels), :
+                    ].astype(jnp.float32)
     blank = jnp.zeros((spare, arrived.shape[1]), jnp.float32)
     for channel in range(channels):
         rows = slice(channel * per_channel, (channel + 1) * per_channel)
@@ -431,14 +412,14 @@
 
 
 def beams_kernel(
-    layout, which, step, pieces, first_ref, code_ref, pointing_ref, weights_ref, spectra_ref,
+    layout, which, step, pieces, skipped, first_ref, code_ref, pointing_ref, weights_ref, spectra_ref,
     *rest,
 ):
     near, cores, channels, frames_here = layout
     per_channel = 2 * frames_here * cores
     raw = which == 0
     if raw:
-        out_ref, spectra, stored, own, total, spectra_sem, sems, arrived, wide, lined = rest
+        out_ref, spectra, stored, own, total, spectra_sem, sems, arrived, lined = rest
         fetch = pltpu.make_async_copy(spectra_ref, arrived, spectra_sem)
     else:
         out_ref, stored, own, total, spectra_sem, sems, spectra = rest
@@ -450,7 +431,7 @@
     copies = []
     for piece in range(pieces):
         place = pl.ds(piece * count, count)
-        source = weights_ref.at[place, pl.ds(which * made_feeds, made_feeds)]
+        source = weights_ref.at[place, pl.ds(skipped, made_feeds)]
         copies.append(pltpu.make_async_copy(source, stored.at[place], sems.at[piece]))
     ahead = 5
     for copy in copies[:ahead]:
@@ -468,7 +449,7 @@
     lax.fori_loop(0, own_rows // block_rows, one_block, 0)
     fetch.wait()
     if raw:
-        line_up(layout, arrived, wide, lined, spectra)
+        line_up(layout, arrived, lined, spectra)
 
     for channel in range(channels):
         rows = slice(channel * per_channel, (channel + 1) * per_channel)
@@ -489,10 +470,10 @@
             out_ref[rows, :] = turn_products(total[rows, :] + both).astype(out_ref.dtype)
 
 
-def partial_beams(first, code, pointing, weights, spectra, layout, which, step, dtype):
+def partial_beams(first, code, pointing, weights, made, spectra, layout, which, step, dtype):
     near, cores, channels, frames_here = layout
     feeds = code.shape[0]
-    made_feeds = weights.shape[1] // pointing.shape[0]
+    made_feeds = made[which]
     width = weights.shape[2]
     per_channel = 2 * cores * frames_here
     pieces = 8
@@ -510,13 +491,12 @@
         out_shape.append(jax.ShapeDtypeStruct(lined_shape, jnp.bfloat16))
         scratch += [
             pltpu.VMEM(spectra.shape, spectra.dtype),
-            pltpu.VMEM(spectra.shape, jnp.float32),
             pltpu.VMEM((near, channels * per_channel, feeds // near), jnp.float32),
         ]
     else:
         scratch.append(pltpu.VMEM(lined_shape, jnp.bfloat16))
     return pl.pallas_call(
-        functools.partial(beams_kernel, layout, which, step, pieces),
+        functools.partial(beams_kernel, layout, which, step, pieces, sum(made[:which])),
         in_specs=[
             pl.BlockSpec(memory_space=pltpu.SMEM),
             in_vmem,
@@ -691,10 +671,10 @@
     half_index = lax.axis_index("half")
     place = lax.axis_index(GROUP)
 
-    tail = from_behind(last_samples(samples, (TAPS - 1) * length), "tm", 1)
+    tail = from_behind(samples[:, (frames_here - (TAPS - 1)) * length :], "tm", 1)
     forward = jnp.asarray(folded_forward_basis(length))
     half_scalar = jnp.reshape(half_index, (1,)).astype(jnp.int32)
-    spectra = spectra_rows(half_scalar, samples, tail, filter_taps, forward)
+    spectra = spectra_rows(half_scalar, samples, tail, filter_taps, forward, group)
     spectra = spectra.reshape(group, channels * 2 * frames_here, feed_here)
     received = lax.all_to_all(spectra, GROUP, 0, 0, tiled=True)
     received = received.reshape(-1, feed_here)
@@ -713,9 +693,10 @@
         ]
     )
     step = 2
-    weights = make_weights(first, code, aims, channels, step, half_feeds * 3 // 4)
+    made = (half_feeds * 3 // 4, half_feeds // 2)
+    weights = make_weights(first, code, aims, channels, step, made)
     to_send, lined = partial_beams(
-        first, code, aims, weights, received, layout, 0, step, jnp.bfloat16
+        first, code, aims, weights, made, received, layout, 0, step, jnp.bfloat16
     )
     swap = [
         (half * near + i, (1 - half) * near + (i + near // 2) % near)
@@ -723,7 +704,9 @@
         for i in range(near)
     ]
     arrived = lax.ppermute(to_send, ("half", "near"), swap)
-    (own,) = partial_beams(first, code, aims, weights, lined, layout, 1, step, jnp.float32)
+    (own,) = partial_beams(
+        first, code, aims, weights, made, lined, layout, 1, step, jnp.float32
+    )
     gathered = gather_beams(own, arrived, layout, beams_here, 1.0 / math.sqrt(feeds))
     lane_channels = LANES // beams_here
     gathered = gathered.reshape(group, -1, LANES)

time: 92.3 us -> 89.4 us (0.969)
  starting transfers between devices: 22.2 us -> 19 us
  waiting for transfers between devices: 10.5 us -> 13.3 us
  Pallas kernels: 52 us -> 50.5 us
  local copies, waits for them, and re-layouts: 5.73 us -> 4.74 us
    pallas_call x3 -> x2, Pallas kernels: 27.9 us -> 24.8 us  [the longest x1 18.3 us: make_weights(): pl.pallas_call(functools.partial(weights_kernel, 32, step), grid=(sum(til...]
    all_to_all x1, waiting for transfers between devices: 0.01 us -> 2.77 us  [halves_body(): received = lax.all_to_all(spectra, GROUP, 0, 0, tiled=True)]
    unnamed x24 -> x20, local copies, waits for them, and re-layouts: 4.64 us -> 2.35 us
    all_to_all x1, starting transfers between devices: 9.85 us -> 8.17 us  [halves_body(): lax.all_to_all(gathered, GROUP, 0, 0, tiled=True).reshape(-1, LANES)]
    pallas_call x2, Pallas kernels: 19.7 us -> 21.3 us  [partial_beams(): pl.pallas_call(functools.partial(beams_kernel, layout, which, step, piece...]
    ppermute x1, starting transfers between devices: 3.99 us -> 2.63 us  [halves_body(): arrived = lax.ppermute(to_send, ('half', 'near'), swap)]
    slice x0 -> x1, local copies, waits for them, and re-layouts: none -> 1.3 us  [halves_body(): samples[:, (frames_here - (TAPS - 1)) * length:]]
  transfers between devices with their start and end apart: 4 -> 4, of which waited for: 2 -> 3; matrix products, arithmetic and copies ran while one was open for 2% -> 2% of each run, Pallas kernels for 33% -> 33%
where the time goes in v4:
time: 89.4 us; the launch traced here: 88.9 us
  Pallas kernels  50.5 us (56%)
  starting transfers between devices  19 us (21%)
  waiting for transfers between devices  13.3 us (15%)
  local copies, waits for them, and re-layouts  4.74 us (5%)
  other arithmetic  0.96 us (1%)
    pallas_call x2, Pallas kernels, partial_beams(): pl.pallas_call(functools.partial(beams_kernel, layout, which, step, piece...  21.3 us
    pallas_call x1, Pallas kernels, make_weights(): pl.pallas_call(functools.partial(weights_kernel, 32, step), grid=(sum(til...  18.3 us
    all_to_all x1, waiting for transfers between devices, halves_body(): lax.all_to_all(gathered, GROUP, 0, 0, tiled=True).reshape(-1, LANES)  8.68 us
    all_to_all x1, starting transfers between devices, halves_body(): lax.all_to_all(gathered, GROUP, 0, 0, tiled=True).reshape(-1, LANES)  8.17 us
    pallas_call x1, Pallas kernels, spectra_rows(): pl.pallas_call(functools.partial(spectra_kernel, frames_here, group), in_...  6.52 us
    all_to_all x1, starting transfers between devices, halves_body(): received = lax.all_to_all(spectra, GROUP, 0, 0, tiled=True)  5.84 us
    all_to_all x1, waiting for transfers between devices, halves_body(): received = lax.all_to_all(spectra, GROUP, 0, 0, tiled=True)  2.77 us
    ppermute x1, starting transfers between devices, halves_body(): arrived = lax.ppermute(to_send, ('half', 'near'), swap)  2.63 us
  transfers between devices with their start and end apart: 4, of which 3 were waited for; matrix products, arithmetic and copies ran while one was open for 2% of the time, Pallas kernels for 33%

profile of v4, /device:TPU:0, one launch (start us, length us, event | category | flops | bytes accessed | tf_op | source)
XLA Modules:
  0.0 88.9 jit_solution(14031216143662893300)
XLA Ops:
  0.0 0.0 copy-start.1
  0.0 1.3 %slice.3 = bf16[128,3072]{1,0:T(8,128)(2,1)S(1)} slice(bf16[128,6144]{1,0:T(8,128)(2,1)} %samples_ref.1), slice={[0:128], [3072:6144]} | slice | bytes 1572864 | tf_op jit(solution)/shard_map/slice | solution.py:674
  1.3 2.4 %collective-permute-start = (bf16[128,3072]{1,0:T(8,128)(2,1)S(1)}, bf16[128,3072]{1,0:T(8,128)(2,1)S(1)}, u32[]{:S(2)}, u32[]{:S(2)}) collective-permute-start(bf16[128,3072]{1,0:T(8,128)(2,1)S(1)} %slice.3), channel_id=1, source_target_pairs={{0,1},{2,3},{4,5},{6,7},{8,9},{10,11},{12,13},{14,15},{16,17},{18,... | collective-permute-start | bytes 2359304 | tf_op jit(solution)/shard_map/ppermute | solution.py:24
  3.7 1.8 %collective-permute-done.tail_ref = bf16[128,3072]{1,0:T(8,128)(2,1)S(1)} collective-permute-done((bf16[128,3072]{1,0:T(8,128)(2,1)S(1)}, bf16[128,3072]{1,0:T(8,128)(2,1)S(1)}, u32[]{:S(2)}, u32[]{:S(2)}) %collective-permute-start) | collective-permute-done | bytes 786464 | tf_op jit(solution)/shard_map/ppermute | solution.py:24
  5.6 0.0 copy-done.1
  5.6 0.0 copy-start.5
  5.6 0.7 copy-done.5
  6.3 6.5 %spectra.1 = bf16[6144,128]{1,0:T(8,128)(2,1)} custom-call(s32[1]{0:T(128)} %bitcast.half_ref, bf16[128,6144]{1,0:T(8,128)(2,1)S(1)} %copy-done.1, bf16[128,3072]{1,0:T(8,128)(2,1)S(1)} %collective-permute-done.tail_ref, f32[4,1024]{1,0:T(4,128)S(1)} %copy-done.5, bf16[2,2,512,512]{3,2,1,0:T(8,128)(2,1)} %constant.108.clone.basis_ref), custom_call_target="tpu_custom_call" | custom-call | tf_op jit(solution)/shard_map/spectra/pallas_call | solution.py:268
  12.8 0.0 copy-start.6
  12.8 0.0 copy-start.7
  12.8 0.0 copy-start.8
  12.9 5.8 %all-to-all-start = ((bf16[16,384,128]{2,1,0:T(8,128)(2,1)}), bf16[16,384,128]{2,1,0:T(8,128)(2,1)S(1)}, u32[]{:S(2)}, u32[]{:S(2)}) async-start(bf16[16,384,128]{2,1,0:T(8,128)(2,1)} %bitcast.6), calls=%async_computation | async-start | bytes 3145728 | tf_op jit(solution)/shard_map/all_to_all | solution.py:679
  18.7 0.0 copy-done.6
  18.8 0.0 copy-done.7
  18.8 0.0 copy-done.8
  18.8 0.6 pad_maximum_fusion.pointing_ref
  19.4 1.0 %broadcast_in_dim.2.code_ref = s32[1024,128]{1,0:T(8,128)} broadcast(s32[1024]{0:T(1024)S(1)} %dynamic-slice_add_fusion), dimensions={0} | broadcast | bytes 528384 | tf_op jit(solution)/shard_map/broadcast_in_dim | solution.py:687
  20.4 0.0 copy-start
  20.4 0.0 copy-start.4
  20.4 18.3 %weights.1.weights_ref = bf16[32,1280,512]{2,1,0:T(8,128)(2,1)} custom-call(s32[1]{0:T(128)} %bitcast.1.first_ref, s32[1024,128]{1,0:T(8,128)} %broadcast_in_dim.2.code_ref, f32[2,4,256]{2,1,0:T(4,128)} %pad_maximum_fusion.pointing_ref), custom_call_target="tpu_custom_call" | custom-call | flops 83886080 | bytes 41943040 | tf_op jit(solution)/shard_map/weights/pallas_call | solution.py:359
  38.7 2.8 %all-to-all-done = bf16[16,384,128]{2,1,0:T(8,128)(2,1)S(1)} async-done(((bf16[16,384,128]{2,1,0:T(8,128)(2,1)}), bf16[16,384,128]{2,1,0:T(8,128)(2,1)S(1)}, u32[]{:S(2)}, u32[]{:S(2)}) %all-to-all-start) | async-done | bytes 1572896 | tf_op jit(solution)/shard_map/all_to_all | solution.py:679
  41.5 0.0 copy-done
  41.5 0.0 copy-done.4
  41.5 10.3 %beams.2 = (bf16[768,256]{1,0:T(8,128)(2,1)S(1)}, bf16[32,32,1024]{2,1,0:T(8,128)(2,1)}) custom-call(s32[1]{0:T(128)} %bitcast.1.first_ref, s32[1024,128]{1,0:T(8,128)S(1)} %copy-done, f32[2,4,256]{2,1,0:T(4,128)S(1)} %copy-done.4, bf16[32,1280,512]{2,1,0:T(8,128)(2,1)} %weights.1.weights_ref, bf16[6144,128]{1,0:T(8,128)(2,1)S(1)} %bitcast.15), custom_call_target="tpu_custom_call" | custom-call | flops 4294967296 | bytes 33554432 | tf_op jit(solution)/shard_map/beams/pallas_call | solution.py:498
  51.7 2.6 %collective-permute-start.1 = (bf16[768,256]{1,0:T(8,128)(2,1)S(1)}, bf16[768,256]{1,0:T(8,128)(2,1)S(1)}, u32[]{:S(2)}, u32[]{:S(2)}) collective-permute-start(bf16[768,256]{1,0:T(8,128)(2,1)S(1)} %get-tuple-element.8), channel_id=1, source_target_pairs={{0,24},{2,26},{4,28},{6,30},{8,16},{10,18},{12,20},{14,22},{16,8},... | collective-permute-start | bytes 1179656 | tf_op jit(solution)/shard_map/ppermute | solution.py:706
  54.4 0.0 copy-start.2
  54.4 1.6 %copy-done.2 = bf16[32,32,1024]{2,1,0:T(8,128)(2,1)S(1)} copy-done((bf16[32,32,1024]{2,1,0:T(8,128)(2,1)S(1)}, bf16[32,32,1024]{2,1,0:T(8,128)(2,1)}, u32[]{:S(2)}) %copy-start.2) | copy-done | bytes 2097176
  56.0 11.1 %beams.3.own_ref = f32[768,256]{1,0:T(8,128)S(1)} custom-call(s32[1]{0:T(128)} %bitcast.1.first_ref, s32[1024,128]{1,0:T(8,128)S(1)} %copy-done, f32[2,4,256]{2,1,0:T(4,128)S(1)} %copy-done.4, bf16[32,1280,512]{2,1,0:T(8,128)(2,1)} %weights.1.weights_ref, bf16[32,32,1024]{2,1,0:T(8,128)(2,1)S(1)} %copy-done.2), custom_call_target="tpu_custom_call" | custom-call | flops 4294967296 | bytes 33554432 | tf_op jit(solution)/shard_map/beams/pallas_call | solution.py:498
  67.0 0.0 copy-start.9
  67.0 0.0 copy-start.3
  67.0 0.0 collective-permute-done.1.other_ref
  67.1 1.8 %gather.1 = bf16[1536,128]{1,0:T(8,128)(2,1)} custom-call(f32[768,256]{1,0:T(8,128)S(1)} %beams.3.own_ref, bf16[768,256]{1,0:T(8,128)(2,1)S(1)} %collective-permute-done.1.other_ref), custom_call_target="tpu_custom_call" | custom-call | tf_op jit(solution)/shard_map/gather/pallas_call | solution.py:558
  68.8 8.2 %all-to-all-start.1 = ((bf16[16,96,128]{2,1,0:T(8,128)(2,1)}), bf16[16,96,128]{2,1,0:T(8,128)(2,1)S(1)}, u32[]{:S(2)}, u32[]{:S(2)}) async-start(bf16[16,96,128]{2,1,0:T(8,128)(2,1)} %bitcast.8), calls=%async_computation.1 | async-start | bytes 786432 | tf_op jit(solution)/shard_map/all_to_all | solution.py:713
  77.0 0.0 copy-done.9
  77.0 0.1 mul.67
  77.1 0.3 fusion
  77.5 8.7 %all-to-all-done.1 = bf16[16,96,128]{2,1,0:T(8,128)(2,1)S(1)} async-done(((bf16[16,96,128]{2,1,0:T(8,128)(2,1)}), bf16[16,96,128]{2,1,0:T(8,128)(2,1)S(1)}, u32[]{:S(2)}, u32[]{:S(2)}) %all-to-all-start.1) | async-done | bytes 393248 | tf_op jit(solution)/shard_map/all_to_all | solution.py:713
  86.1 0.0 copy-done.3
  86.1 2.6 %series.1 = f32[6,32,1024]{2,1,0:T(8,128)} custom-call(s32[1]{0:T(128)} %bitcast.half_ref, bf16[1536,128]{1,0:T(8,128)(2,1)S(1)} %bitcast.16, f32[128,128]{1,0:T(8,128)S(1)} %get-tuple-element.12.cos_ref, f32[128,128]{1,0:T(8,128)S(1)} %get-tuple-element.11.sin_ref, bf16[2,2,512,512]{3,2,1,0:T(8,128)(2,1)S(1)} %copy-done.3), custom_call_target="tpu_custom_call" | custom-call | tf_op jit(solution)/shard_map/series/pallas_call | solution.py:635
  (7 shorter events, 0.0 us)
Async XLA Ops:
  0.0 5.6 %copy-start.1 = (bf16[128,6144]{1,0:T(8,128)(2,1)S(1)}, bf16[128,6144]{1,0:T(8,128)(2,1)}, u32[]{:S(2)}) copy-start(bf16[128,6144]{1,0:T(8,128)(2,1)} %samples_ref.1) | copy-start | bytes 4718596
  1.3 4.3 %collective-permute-start = (bf16[128,3072]{1,0:T(8,128)(2,1)S(1)}, bf16[128,3072]{1,0:T(8,128)(2,1)S(1)}, u32[]{:S(2)}, u32[]{:S(2)}) collective-permute-start(bf16[128,3072]{1,0:T(8,128)(2,1)S(1)} %slice.3), channel_id=1, source_target_pairs={{0,1},{2,3},{4,5},{6,7},{8,9},{10,11},{12,13},{14,15},{16,17},{18,... | collective-permute-start | bytes 2359304 | tf_op jit(solution)/shard_map/ppermute | solution.py:24
  5.6 0.7 copy-start.5
  12.8 5.9 %copy-start.6 = (s32[512,4]{0,1:T(4,128)S(1)}, s32[512,4]{0,1:T(4,128)}, u32[]{:S(2)}) copy-start(s32[512,4]{0,1:T(4,128)} %param.12) | copy-start | bytes 24580
  12.8 6.0 %copy-start.7 = (s32[2048]{0:T(1024)S(1)}, s32[2048]{0:T(1024)}, u32[]{:S(2)}) copy-start(s32[2048]{0:T(1024)} %param.11) | copy-start | bytes 24580
  12.8 5.9 %copy-start.8 = (s32[2048]{0:T(1024)S(1)}, s32[2048]{0:T(1024)}, u32[]{:S(2)}) copy-start(s32[2048]{0:T(1024)} %param.10) | copy-start | bytes 24580
  12.9 28.6 %all-to-all-start = ((bf16[16,384,128]{2,1,0:T(8,128)(2,1)}), bf16[16,384,128]{2,1,0:T(8,128)(2,1)S(1)}, u32[]{:S(2)}, u32[]{:S(2)}) async-start(bf16[16,384,128]{2,1,0:T(8,128)(2,1)} %bitcast.6), calls=%async_computation | async-start | bytes 3145728 | tf_op jit(solution)/shard_map/all_to_all | solution.py:679
  20.4 21.0 %copy-start = (s32[1024,128]{1,0:T(8,128)S(1)}, s32[1024,128]{1,0:T(8,128)}, u32[]{:S(2)}) copy-start(s32[1024,128]{1,0:T(8,128)} %broadcast_in_dim.2.code_ref) | copy-start | bytes 1572868
  20.4 21.0 %copy-start.4 = (f32[2,4,256]{2,1,0:T(4,128)S(1)}, f32[2,4,256]{2,1,0:T(4,128)}, u32[]{:S(2)}) copy-start(f32[2,4,256]{2,1,0:T(4,128)} %pad_maximum_fusion.pointing_ref) | copy-start | bytes 24580
  51.7 15.3 %collective-permute-start.1 = (bf16[768,256]{1,0:T(8,128)(2,1)S(1)}, bf16[768,256]{1,0:T(8,128)(2,1)S(1)}, u32[]{:S(2)}, u32[]{:S(2)}) collective-permute-start(bf16[768,256]{1,0:T(8,128)(2,1)S(1)} %get-tuple-element.8), channel_id=1, source_target_pairs={{0,24},{2,26},{4,28},{6,30},{8,16},{10,18},{12,20},{14,22},{16,8},... | collective-permute-start | bytes 1179656 | tf_op jit(solution)/shard_map/ppermute | solution.py:706
  54.4 1.6 %copy-start.2 = (bf16[32,32,1024]{2,1,0:T(8,128)(2,1)S(1)}, bf16[32,32,1024]{2,1,0:T(8,128)(2,1)}, u32[]{:S(2)}) copy-start(bf16[32,32,1024]{2,1,0:T(8,128)(2,1)} %get-tuple-element.7.spectra_ref) | copy-start | bytes 6291460
  67.0 10.0 %copy-start.9 = (f32[32]{0:T(128)S(1)}, f32[32]{0:T(128)}, u32[]{:S(2)}) copy-start(f32[32]{0:T(128)} %param.13) | copy-start | bytes 388
  67.0 19.1 %copy-start.3 = (bf16[2,2,512,512]{3,2,1,0:T(8,128)(2,1)S(1)}, bf16[2,2,512,512]{3,2,1,0:T(8,128)(2,1)}, u32[]{:S(2)}) copy-start(bf16[2,2,512,512]{3,2,1,0:T(8,128)(2,1)} %constant.109.clone.basis_ref) | copy-start | bytes 6291460
  68.8 17.3 %all-to-all-start.1 = ((bf16[16,96,128]{2,1,0:T(8,128)(2,1)}), bf16[16,96,128]{2,1,0:T(8,128)(2,1)S(1)}, u32[]{:S(2)}, u32[]{:S(2)}) async-start(bf16[16,96,128]{2,1,0:T(8,128)(2,1)} %bitcast.8), calls=%async_computation.1 | async-start | bytes 786432 | tf_op jit(solution)/shard_map/all_to_all | solution.py:713

commit v5 on v4

--- a/solution.py
+++ b/solution.py
@@ -354,7 +354,7 @@
 
 def make_weights(first, code, pointing, channels, step, feeds):
     _, cylinders, beams = pointing.shape
-    rows = 128
+    rows = 256
     tiles = [count // rows for count in feeds]
     return pl.pallas_call(
         functools.partial(weights_kernel, 32, step),
@@ -412,44 +412,60 @@
 
 
 def beams_kernel(
-    layout, which, step, pieces, skipped, first_ref, code_ref, pointing_ref, weights_ref, spectra_ref,
+    layout, which, step, pieces, skipped, base, first_ref, code_ref, pointing_ref, weights_ref, spectra_ref,
     *rest,
 ):
-    near, cores, channels, frames_here = layout
+    _, cores, _, frames_here = layout
     per_channel = 2 * frames_here * cores
-    raw = which == 0
+    raw = base is None
     if raw:
-        out_ref, spectra, stored, own, total, spectra_sem, sems, arrived, lined = rest
-        fetch = pltpu.make_async_copy(spectra_ref, arrived, spectra_sem)
+        out_ref, spectra_out_ref, *rest = rest
     else:
-        out_ref, stored, own, total, spectra_sem, sems, spectra = rest
-        fetch = pltpu.make_async_copy(spectra_ref, spectra, spectra_sem)
+        out_ref, *rest = rest
+    stored, own, total, code, spectra, extra_sems, sems, *rest = rest
+    if raw:
+        arrived, lined = rest
+    channels, made_feeds, _ = stored.shape
+    here = pl.ds(base or 0, channels)
+    if raw:
+        fetch = pltpu.make_async_copy(spectra_ref, arrived, extra_sems.at[0])
+    else:
+        fetch = pltpu.make_async_copy(spectra_ref.at[here], spectra, extra_sems.at[0])
+    own_rows = own.shape[1]
+    fetch_code = pltpu.make_async_copy(
+        code_ref.at[pl.ds(made_feeds, own_rows)], code, extra_sems.at[1]
+    )
+    fetch_code.start()
     fetch.start()
-    made_feeds = stored.shape[1]
-    own_rows = own.shape[1]
     count = channels // pieces
     copies = []
     for piece in range(pieces):
         place = pl.ds(piece * count, count)
-        source = weights_ref.at[place, pl.ds(skipped, made_feeds)]
+        there = pl.ds((base or 0) + piece * count, count)
+        source = weights_ref.at[there, pl.ds(skipped, made_feeds)]
         copies.append(pltpu.make_async_copy(source, stored.at[place], sems.at[piece]))
-    ahead = 5
-    for copy in copies[:ahead]:
+    ahead = min(5, pieces)
+    soon = ahead if raw else 2
+    for copy in copies[:soon]:
         copy.start()
 
     block_rows = 32
-    first = chain_start(first_ref[0], channels, step)
+    first = chain_start(first_ref[0] + step * (base or 0), channels, step)
 
     def one_block(index, carry):
         target = pl.ds(pl.multiple_of(index * block_rows, block_rows), block_rows)
-        source = pl.ds(pl.multiple_of(made_feeds + index * block_rows, block_rows), block_rows)
-        chain_of_weights(first, step, code_ref[source], pointing_ref.at[which], own, target)
+        chain_of_weights(first, step, code[target], pointing_ref.at[which], own, target)
         return carry
 
+    fetch_code.wait()
     lax.fori_loop(0, own_rows // block_rows, one_block, 0)
     fetch.wait()
+    for copy in copies[soon:ahead]:
+        copy.start()
     if raw:
         line_up(layout, arrived, lined, spectra)
+        keep = pltpu.make_async_copy(spectra, spectra_out_ref, extra_sems.at[2])
+        keep.start()
 
     for channel in range(channels):
         rows = slice(channel * per_channel, (channel + 1) * per_channel)
@@ -468,49 +484,55 @@
                 preferred_element_type=jnp.float32,
             )[:per_channel]
             out_ref[rows, :] = turn_products(total[rows, :] + both).astype(out_ref.dtype)
-
-
-def partial_beams(first, code, pointing, weights, made, spectra, layout, which, step, dtype):
-    near, cores, channels, frames_here = layout
+    if raw:
+        keep.wait()
+
+
+def partial_beams(
+    first, code, pointing, weights, made, spectra, layout, which, channels, base, step, dtype
+):
+    near, cores, all_channels, frames_here = layout
     feeds = code.shape[0]
     made_feeds = made[which]
     width = weights.shape[2]
     per_channel = 2 * cores * frames_here
-    pieces = 8
+    pieces = channels // 4
+    raw = base is None
+    lined_channels = all_channels if raw else channels
     in_vmem = pl.BlockSpec(memory_space=pltpu.VMEM)
-    lined_shape = (channels, padded_rows(per_channel), feeds)
+    lined_shape = (lined_channels, padded_rows(per_channel), feeds)
     out_shape = [jax.ShapeDtypeStruct((channels * per_channel, width // 2), dtype)]
     scratch = [
         pltpu.VMEM((channels, made_feeds, width), weights.dtype),
         pltpu.VMEM((channels, feeds - made_feeds, width), weights.dtype),
         pltpu.VMEM((channels * per_channel, width), jnp.float32),
-        pltpu.SemaphoreType.DMA,
+        pltpu.VMEM((feeds - made_feeds, LANES), code.dtype),
+        pltpu.VMEM(lined_shape, jnp.bfloat16),
+        pltpu.SemaphoreType.DMA((3,)),
         pltpu.SemaphoreType.DMA((pieces,)),
     ]
-    if which == 0:
+    if raw:
         out_shape.append(jax.ShapeDtypeStruct(lined_shape, jnp.bfloat16))
         scratch += [
             pltpu.VMEM(spectra.shape, spectra.dtype),
-            pltpu.VMEM((near, channels * per_channel, feeds // near), jnp.float32),
+            pltpu.VMEM((near, all_channels * per_channel, feeds // near), jnp.float32),
         ]
-    else:
-        scratch.append(pltpu.VMEM(lined_shape, jnp.bfloat16))
     return pl.pallas_call(
-        functools.partial(beams_kernel, layout, which, step, pieces, sum(made[:which])),
+        functools.partial(beams_kernel, layout, which, step, pieces, sum(made[:which]), base),
         in_specs=[
             pl.BlockSpec(memory_space=pltpu.SMEM),
-            in_vmem,
+            pl.BlockSpec(memory_space=pltpu.HBM),
             in_vmem,
             pl.BlockSpec(memory_space=pltpu.HBM),
-            pl.BlockSpec(memory_space=pl.ANY if which == 0 else pltpu.HBM),
+            pl.BlockSpec(memory_space=pl.ANY if raw else pltpu.HBM),
         ],
-        out_specs=[in_vmem] * len(out_shape),
+        out_specs=[in_vmem, pl.BlockSpec(memory_space=pltpu.HBM)][: len(out_shape)],
         out_shape=out_shape,
         scratch_shapes=scratch,
         compiler_params=pltpu.CompilerParams(vmem_limit_bytes=50 * 1024 * 1024),
         cost_estimate=pl.CostEstimate(
-            flops=channels * feeds * width * 2 * 128,
-            bytes_accessed=channels * feeds * width * 2,
+            flops=(1 - which) * channels * feeds * width * 2 * 128 + 1,
+            bytes_accessed=(1 - which) * channels * feeds * width * 2 + 1,
             transcendentals=0,
         ),
         name="beams",
@@ -518,7 +540,7 @@
 
 
 def gather_kernel(
-    layout, beams_here, scale, own_ref, other_ref, out_ref, own, other, total, rows, sems
+    layout, beams_here, scale, own_ref, early_ref, late_ref, out_ref, own, other, total, rows, sems
 ):
     near, cores, channels, frames_here = layout
     lane_channels = LANES // beams_here
@@ -527,7 +549,10 @@
     groups = channels // lane_channels
     fetches = [
         pltpu.make_async_copy(own_ref, own, sems.at[0]),
-        pltpu.make_async_copy(other_ref, other, sems.at[1]),
+        pltpu.make_async_copy(early_ref, other.at[pl.ds(0, early_ref.shape[0])], sems.at[1]),
+        pltpu.make_async_copy(
+            late_ref, other.at[pl.ds(early_ref.shape[0], late_ref.shape[0])], sems.at[2]
+        ),
     ]
     for fetch in fetches:
         fetch.start()
@@ -552,23 +577,23 @@
     out_ref[...] = rows[...].astype(jnp.bfloat16)
 
 
-def gather_beams(own, other, layout, beams_here, scale):
+def gather_beams(own, early, late, layout, beams_here, scale):
     near, cores, channels, frames_here = layout
     total_rows = near * cores * channels // (LANES // beams_here) * 2 * frames_here
     return pl.pallas_call(
         functools.partial(gather_kernel, layout, beams_here, scale),
-        in_specs=[pl.BlockSpec(memory_space=pltpu.HBM), pl.BlockSpec(memory_space=pl.ANY)],
+        in_specs=[pl.BlockSpec(memory_space=pltpu.HBM)] + [pl.BlockSpec(memory_space=pl.ANY)] * 2,
         out_shape=jax.ShapeDtypeStruct((total_rows, LANES), jnp.bfloat16),
         scratch_shapes=[
             pltpu.VMEM(own.shape, own.dtype),
-            pltpu.VMEM(other.shape, other.dtype),
+            pltpu.VMEM(own.shape, early.dtype),
             pltpu.VMEM(own.shape, jnp.float32),
             pltpu.VMEM((total_rows, LANES), jnp.float32),
-            pltpu.SemaphoreType.DMA((2,)),
+            pltpu.SemaphoreType.DMA((3,)),
         ],
         compiler_params=pltpu.CompilerParams(vmem_limit_bytes=16 * 1024 * 1024),
         name="gather",
-    )(own, other)
+    )(own, early, late)
 
 
 def series_kernel(
@@ -693,21 +718,25 @@
         ]
     )
     step = 2
-    made = (half_feeds * 3 // 4, half_feeds // 2)
+    made = (half_feeds * 3 // 4, half_feeds * 3 // 4)
     weights = make_weights(first, code, aims, channels, step, made)
-    to_send, lined = partial_beams(
-        first, code, aims, weights, made, received, layout, 0, step, jnp.bfloat16
-    )
     swap = [
         (half * near + i, (1 - half) * near + (i + near // 2) % near)
         for half in range(HALVES)
         for i in range(near)
     ]
-    arrived = lax.ppermute(to_send, ("half", "near"), swap)
-    (own,) = partial_beams(
-        first, code, aims, weights, made, lined, layout, 1, step, jnp.float32
-    )
-    gathered = gather_beams(own, arrived, layout, beams_here, 1.0 / math.sqrt(feeds))
+    common = (first, code, aims, weights, made)
+    piece = channels * 5 // 8
+    early, lined = partial_beams(
+        *common, received, layout, 0, piece, None, step, jnp.bfloat16
+    )
+    early = lax.ppermute(early, ("half", "near"), swap)
+    (late,) = partial_beams(
+        *common, lined, layout, 0, channels - piece, piece, step, jnp.bfloat16
+    )
+    late = lax.ppermute(late, ("half", "near"), swap)
+    (own,) = partial_beams(*common, lined, layout, 1, channels, 0, step, jnp.float32)
+    gathered = gather_beams(own, early, late, layout, beams_here, 1.0 / math.sqrt(feeds))
     lane_channels = LANES // beams_here
     gathered = gathered.reshape(group, -1, LANES)
     returned = lax.all_to_all(gathered, GROUP, 0, 0, tiled=True).reshape(-1, LANES)

time: 89.4 us -> 87.3 us (0.977)
  starting transfers between devices: 19 us -> 15.8 us
  Pallas kernels: 50.5 us -> 53.6 us
  waiting for transfers between devices: 13.3 us -> 11.3 us
    all_to_all x1, starting transfers between devices: 8.17 us -> 3.65 us  [halves_body(): lax.all_to_all(gathered, GROUP, 0, 0, tiled=True).reshape(-1, LANES)]
    pallas_call x1, Pallas kernels: 18.3 us -> 20.3 us  [make_weights(): pl.pallas_call(functools.partial(weights_kernel, 32, step), grid=(sum(til...]
    all_to_all x1, waiting for transfers between devices: 2.77 us -> 0.76 us  [halves_body(): received = lax.all_to_all(spectra, GROUP, 0, 0, tiled=True)]
    ppermute x1 -> x2, starting transfers between devices: 2.63 us -> 3.95 us  [the longest x1 3.25 us: halves_body(): early = lax.ppermute(early, ('half', 'near'), swap)]
    pallas_call x2 -> x3, Pallas kernels: 21.3 us -> 22 us  [partial_beams(): pl.pallas_call(functools.partial(beams_kernel, layout, which, step, piece...]
  transfers between devices with their start and end apart: 4 -> 5, of which waited for: 3 -> 3; matrix products, arithmetic and copies ran while one was open for 2% -> 2% of each run, Pallas kernels for 33% -> 40%
where the time goes in v5:
time: 87.3 us; the launch traced here: 86.8 us
  Pallas kernels  53.6 us (61%)
  starting transfers between devices  15.8 us (18%)
  waiting for transfers between devices  11.3 us (13%)
  local copies, waits for them, and re-layouts  4.74 us (5%)
  other arithmetic  0.97 us (1%)
    pallas_call x3, Pallas kernels, partial_beams(): pl.pallas_call(functools.partial(beams_kernel, layout, which, step, piece...  22 us
    pallas_call x1, Pallas kernels, make_weights(): pl.pallas_call(functools.partial(weights_kernel, 32, step), grid=(sum(til...  20.3 us
    all_to_all x1, waiting for transfers between devices, halves_body(): lax.all_to_all(gathered, GROUP, 0, 0, tiled=True).reshape(-1, LANES)  8.68 us
    pallas_call x1, Pallas kernels, spectra_rows(): pl.pallas_call(functools.partial(spectra_kernel, frames_here, group), in_...  6.51 us
    all_to_all x1, starting transfers between devices, halves_body(): received = lax.all_to_all(spectra, GROUP, 0, 0, tiled=True)  5.84 us
    all_to_all x1, starting transfers between devices, halves_body(): lax.all_to_all(gathered, GROUP, 0, 0, tiled=True).reshape(-1, LANES)  3.65 us
    ppermute x1, starting transfers between devices, halves_body(): early = lax.ppermute(early, ('half', 'near'), swap)  3.25 us
    pallas_call x1, Pallas kernels, make_series(): pl.pallas_call(functools.partial(series_kernel, beams_here), in_specs=[pl...  2.62 us
  transfers between devices with their start and end apart: 5, of which 3 were waited for; matrix products, arithmetic and copies ran while one was open for 2% of the time, Pallas kernels for 40%

profile of v5, /device:TPU:0, one launch (start us, length us, event | category | flops | bytes accessed | tf_op | source)
XLA Modules:
  0.0 86.8 jit_solution(3334815443396776315)
XLA Ops:
  0.0 0.0 copy-start.2
  0.0 1.3 %slice.3 = bf16[128,3072]{1,0:T(8,128)(2,1)S(1)} slice(bf16[128,6144]{1,0:T(8,128)(2,1)} %samples_ref.1), slice={[0:128], [3072:6144]} | slice | bytes 1572864 | tf_op jit(solution)/shard_map/slice | solution.py:699
  1.3 2.4 %collective-permute-start = (bf16[128,3072]{1,0:T(8,128)(2,1)S(1)}, bf16[128,3072]{1,0:T(8,128)(2,1)S(1)}, u32[]{:S(2)}, u32[]{:S(2)}) collective-permute-start(bf16[128,3072]{1,0:T(8,128)(2,1)S(1)} %slice.3), channel_id=1, source_target_pairs={{0,1},{2,3},{4,5},{6,7},{8,9},{10,11},{12,13},{14,15},{16,17},{18,... | collective-permute-start | bytes 2359304 | tf_op jit(solution)/shard_map/ppermute | solution.py:24
  3.7 1.8 %collective-permute-done.tail_ref = bf16[128,3072]{1,0:T(8,128)(2,1)S(1)} collective-permute-done((bf16[128,3072]{1,0:T(8,128)(2,1)S(1)}, bf16[128,3072]{1,0:T(8,128)(2,1)S(1)}, u32[]{:S(2)}, u32[]{:S(2)}) %collective-permute-start) | collective-permute-done | bytes 786464 | tf_op jit(solution)/shard_map/ppermute | solution.py:24
  5.6 0.0 copy-done.2
  5.6 0.0 copy-start.5
  5.6 0.7 copy-done.5
  6.3 6.5 %spectra.1 = bf16[6144,128]{1,0:T(8,128)(2,1)} custom-call(s32[1]{0:T(128)} %bitcast.half_ref, bf16[128,6144]{1,0:T(8,128)(2,1)S(1)} %copy-done.2, bf16[128,3072]{1,0:T(8,128)(2,1)S(1)} %collective-permute-done.tail_ref, f32[4,1024]{1,0:T(4,128)S(1)} %copy-done.5, bf16[2,2,512,512]{3,2,1,0:T(8,128)(2,1)} %constant.108.clone.basis_ref), custom_call_target="tpu_custom_call" | custom-call | tf_op jit(solution)/shard_map/spectra/pallas_call | solution.py:268
  12.8 0.0 copy-start.6
  12.8 0.0 copy-start.7
  12.8 0.0 copy-start.8
  12.8 5.8 %all-to-all-start = ((bf16[16,384,128]{2,1,0:T(8,128)(2,1)}), bf16[16,384,128]{2,1,0:T(8,128)(2,1)S(1)}, u32[]{:S(2)}, u32[]{:S(2)}) async-start(bf16[16,384,128]{2,1,0:T(8,128)(2,1)} %bitcast.6), calls=%async_computation | async-start | bytes 3145728 | tf_op jit(solution)/shard_map/all_to_all | solution.py:704
  18.7 0.0 copy-done.6
  18.7 0.0 copy-done.7
  18.8 0.0 copy-done.8
  18.8 0.6 pad_maximum_fusion.pointing_ref
  19.4 1.0 %broadcast_in_dim.2.code_ref = s32[1024,128]{1,0:T(8,128)} broadcast(s32[1024]{0:T(1024)S(1)} %dynamic-slice_add_fusion), dimensions={0} | broadcast | bytes 528384 | tf_op jit(solution)/shard_map/broadcast_in_dim | solution.py:712
  20.4 0.0 copy-start
  20.4 0.0 copy-start.4
  20.4 20.3 %weights.1.weights_ref = bf16[32,1536,512]{2,1,0:T(8,128)(2,1)} custom-call(s32[1]{0:T(128)} %bitcast.1.first_ref, s32[1024,128]{1,0:T(8,128)} %broadcast_in_dim.2.code_ref, f32[2,4,256]{2,1,0:T(4,128)} %pad_maximum_fusion.pointing_ref), custom_call_target="tpu_custom_call" | custom-call | flops 100663296 | bytes 50331648 | tf_op jit(solution)/shard_map/weights/pallas_call | solution.py:359
  40.7 0.8 all-to-all-done
  41.4 0.0 copy-done
  41.5 0.0 copy-done.4
  41.5 7.3 %beams.3 = (bf16[480,256]{1,0:T(8,128)(2,1)S(1)}, bf16[32,32,1024]{2,1,0:T(8,128)(2,1)}) custom-call(s32[1]{0:T(128)} %bitcast.1.first_ref, s32[1024,128]{1,0:T(8,128)S(1)} %copy-done, f32[2,4,256]{2,1,0:T(4,128)S(1)} %copy-done.4, bf16[32,1536,512]{2,1,0:T(8,128)(2,1)} %weights.1.weights_ref, bf16[6144,128]{1,0:T(8,128)(2,1)S(1)} %bitcast.15), custom_call_target="tpu_custom_call" | custom-call | flops 2684354560 | bytes 20971520 | tf_op jit(solution)/shard_map/beams/pallas_call | solution.py:520
  48.7 3.2 %collective-permute-start.1 = (bf16[480,256]{1,0:T(8,128)(2,1)S(1)}, bf16[480,256]{1,0:T(8,128)(2,1)S(1)}, u32[]{:S(2)}, u32[]{:S(2)}) collective-permute-start(bf16[480,256]{1,0:T(8,128)(2,1)S(1)} %get-tuple-element.8), channel_id=1, source_target_pairs={{0,24},{2,26},{4,28},{6,30},{8,16},{10,18},{12,20},{14,22},{16,8},... | collective-permute-start | bytes 737288 | tf_op jit(solution)/shard_map/ppermute | solution.py:733
  52.0 0.0 copy-start.1
  52.0 1.6 %copy-done.1 = bf16[32,32,1024]{2,1,0:T(8,128)(2,1)S(1)} copy-done((bf16[32,32,1024]{2,1,0:T(8,128)(2,1)S(1)}, bf16[32,32,1024]{2,1,0:T(8,128)(2,1)}, u32[]{:S(2)}) %copy-start.1) | copy-done | bytes 2097176
  53.6 4.9 %beams.5 = bf16[288,256]{1,0:T(8,128)(2,1)S(1)} custom-call(s32[1]{0:T(128)} %bitcast.1.first_ref, s32[1024,128]{1,0:T(8,128)S(1)} %copy-done, f32[2,4,256]{2,1,0:T(4,128)S(1)} %copy-done.4, bf16[32,1536,512]{2,1,0:T(8,128)(2,1)} %weights.1.weights_ref, bf16[32,32,1024]{2,1,0:T(8,128)(2,1)S(1)} %copy-done.1), custom_call_target="tpu_custom_call" | custom-call | flops 1610612736 | bytes 12582913 | tf_op jit(solution)/shard_map/beams/pallas_call | solution.py:520
  58.5 0.7 collective-permute-start.2
  59.2 9.9 %beams.4.own_ref = f32[768,256]{1,0:T(8,128)S(1)} custom-call(s32[1]{0:T(128)} %bitcast.1.first_ref, s32[1024,128]{1,0:T(8,128)S(1)} %copy-done, f32[2,4,256]{2,1,0:T(4,128)S(1)} %copy-done.4, bf16[32,1536,512]{2,1,0:T(8,128)(2,1)} %weights.1.weights_ref, bf16[32,32,1024]{2,1,0:T(8,128)(2,1)S(1)} %copy-done.1), custom_call_target="tpu_custom_call" | custom-call | flops 1 | bytes 1 | tf_op jit(solution)/shard_map/beams/pallas_call | solution.py:520
  69.1 0.0 copy-start.9
  69.1 0.0 copy-start.3
  69.1 0.0 collective-permute-done.2.late_ref
  69.1 0.0 collective-permute-done.1.early_ref
  69.1 2.1 %gather.1 = bf16[1536,128]{1,0:T(8,128)(2,1)} custom-call(f32[768,256]{1,0:T(8,128)S(1)} %beams.4.own_ref, bf16[480,256]{1,0:T(8,128)(2,1)S(1)} %collective-permute-done.1.early_ref, bf16[288,256]{1,0:T(8,128)(2,1)S(1)} %collective-permute-done.2.late_ref), custom_call_target="tpu_custom_call" | custom-call | tf_op jit(solution)/shard_map/gather/pallas_call | solution.py:583
  71.2 3.6 %all-to-all-start.1 = ((bf16[16,96,128]{2,1,0:T(8,128)(2,1)}), bf16[16,96,128]{2,1,0:T(8,128)(2,1)S(1)}, u32[]{:S(2)}, u32[]{:S(2)}) async-start(bf16[16,96,128]{2,1,0:T(8,128)(2,1)} %bitcast.8), calls=%async_computation.1 | async-start | bytes 786432 | tf_op jit(solution)/shard_map/all_to_all | solution.py:742
  74.9 0.0 copy-done.9
  74.9 0.1 mul.67
  75.0 0.3 fusion
  75.3 8.7 %all-to-all-done.1 = bf16[16,96,128]{2,1,0:T(8,128)(2,1)S(1)} async-done(((bf16[16,96,128]{2,1,0:T(8,128)(2,1)}), bf16[16,96,128]{2,1,0:T(8,128)(2,1)S(1)}, u32[]{:S(2)}, u32[]{:S(2)}) %all-to-all-start.1) | async-done | bytes 393248 | tf_op jit(solution)/shard_map/all_to_all | solution.py:742
  84.0 0.0 copy-done.3
  84.0 2.6 %series.1 = f32[6,32,1024]{2,1,0:T(8,128)} custom-call(s32[1]{0:T(128)} %bitcast.half_ref, bf16[1536,128]{1,0:T(8,128)(2,1)S(1)} %bitcast.16, f32[128,128]{1,0:T(8,128)S(1)} %get-tuple-element.12.cos_ref, f32[128,128]{1,0:T(8,128)S(1)} %get-tuple-element.11.sin_ref, bf16[2,2,512,512]{3,2,1,0:T(8,128)(2,1)S(1)} %copy-done.3), custom_call_target="tpu_custom_call" | custom-call | tf_op jit(solution)/shard_map/series/pallas_call | solution.py:660
  (7 shorter events, 0.0 us)
Async XLA Ops:
  0.0 5.6 %copy-start.2 = (bf16[128,6144]{1,0:T(8,128)(2,1)S(1)}, bf16[128,6144]{1,0:T(8,128)(2,1)}, u32[]{:S(2)}) copy-start(bf16[128,6144]{1,0:T(8,128)(2,1)} %samples_ref.1) | copy-start | bytes 4718596
  1.3 4.3 %collective-permute-start = (bf16[128,3072]{1,0:T(8,128)(2,1)S(1)}, bf16[128,3072]{1,0:T(8,128)(2,1)S(1)}, u32[]{:S(2)}, u32[]{:S(2)}) collective-permute-start(bf16[128,3072]{1,0:T(8,128)(2,1)S(1)} %slice.3), channel_id=1, source_target_pairs={{0,1},{2,3},{4,5},{6,7},{8,9},{10,11},{12,13},{14,15},{16,17},{18,... | collective-permute-start | bytes 2359304 | tf_op jit(solution)/shard_map/ppermute | solution.py:24
  5.6 0.7 copy-start.5
  12.8 5.9 %copy-start.6 = (s32[512,4]{0,1:T(4,128)S(1)}, s32[512,4]{0,1:T(4,128)}, u32[]{:S(2)}) copy-start(s32[512,4]{0,1:T(4,128)} %param.12) | copy-start | bytes 24580
  12.8 5.9 %copy-start.7 = (s32[2048]{0:T(1024)S(1)}, s32[2048]{0:T(1024)}, u32[]{:S(2)}) copy-start(s32[2048]{0:T(1024)} %param.11) | copy-start | bytes 24580
  12.8 5.9 %copy-start.8 = (s32[2048]{0:T(1024)S(1)}, s32[2048]{0:T(1024)}, u32[]{:S(2)}) copy-start(s32[2048]{0:T(1024)} %param.10) | copy-start | bytes 24580
  12.8 28.6 %all-to-all-start = ((bf16[16,384,128]{2,1,0:T(8,128)(2,1)}), bf16[16,384,128]{2,1,0:T(8,128)(2,1)S(1)}, u32[]{:S(2)}, u32[]{:S(2)}) async-start(bf16[16,384,128]{2,1,0:T(8,128)(2,1)} %bitcast.6), calls=%async_computation | async-start | bytes 3145728 | tf_op jit(solution)/shard_map/all_to_all | solution.py:704
  20.4 21.0 %copy-start = (s32[1024,128]{1,0:T(8,128)S(1)}, s32[1024,128]{1,0:T(8,128)}, u32[]{:S(2)}) copy-start(s32[1024,128]{1,0:T(8,128)} %broadcast_in_dim.2.code_ref) | copy-start | bytes 1572868
  20.4 21.1 %copy-start.4 = (f32[2,4,256]{2,1,0:T(4,128)S(1)}, f32[2,4,256]{2,1,0:T(4,128)}, u32[]{:S(2)}) copy-start(f32[2,4,256]{2,1,0:T(4,128)} %pad_maximum_fusion.pointing_ref) | copy-start | bytes 24580
  48.7 20.4 %collective-permute-start.1 = (bf16[480,256]{1,0:T(8,128)(2,1)S(1)}, bf16[480,256]{1,0:T(8,128)(2,1)S(1)}, u32[]{:S(2)}, u32[]{:S(2)}) collective-permute-start(bf16[480,256]{1,0:T(8,128)(2,1)S(1)} %get-tuple-element.8), channel_id=1, source_target_pairs={{0,24},{2,26},{4,28},{6,30},{8,16},{10,18},{12,20},{14,22},{16,8},... | collective-permute-start | bytes 737288 | tf_op jit(solution)/shard_map/ppermute | solution.py:733
  52.0 1.6 %copy-start.1 = (bf16[32,32,1024]{2,1,0:T(8,128)(2,1)S(1)}, bf16[32,32,1024]{2,1,0:T(8,128)(2,1)}, u32[]{:S(2)}) copy-start(bf16[32,32,1024]{2,1,0:T(8,128)(2,1)} %get-tuple-element.7.spectra_ref) | copy-start | bytes 6291460
  58.5 10.6 %collective-permute-start.2 = (bf16[288,256]{1,0:T(8,128)(2,1)S(1)}, bf16[288,256]{1,0:T(8,128)(2,1)S(1)}, u32[]{:S(2)}, u32[]{:S(2)}) collective-permute-start(bf16[288,256]{1,0:T(8,128)(2,1)S(1)} %beams.5), channel_id=1, source_target_pairs={{0,24},{2,26},{4,28},{6,30},{8,16},{10,18},{12,20},{14,22},{16,8},... | collective-permute-start | bytes 442376 | tf_op jit(solution)/shard_map/ppermute | solution.py:737
  69.1 5.8 %copy-start.9 = (f32[32]{0:T(128)S(1)}, f32[32]{0:T(128)}, u32[]{:S(2)}) copy-start(f32[32]{0:T(128)} %param.13) | copy-start | bytes 388
  69.1 14.9 %copy-start.3 = (bf16[2,2,512,512]{3,2,1,0:T(8,128)(2,1)S(1)}, bf16[2,2,512,512]{3,2,1,0:T(8,128)(2,1)}, u32[]{:S(2)}) copy-start(bf16[2,2,512,512]{3,2,1,0:T(8,128)(2,1)} %constant.109.clone.basis_ref) | copy-start | bytes 6291460
  71.2 12.8 %all-to-all-start.1 = ((bf16[16,96,128]{2,1,0:T(8,128)(2,1)}), bf16[16,96,128]{2,1,0:T(8,128)(2,1)S(1)}, u32[]{:S(2)}, u32[]{:S(2)}) async-start(bf16[16,96,128]{2,1,0:T(8,128)(2,1)} %bitcast.8), calls=%async_computation.1 | async-start | bytes 786432 | tf_op jit(solution)/shard_map/all_to_all | solution.py:742

commit v6 on v5

--- a/solution.py
+++ b/solution.py
@@ -699,7 +699,8 @@
     tail = from_behind(samples[:, (frames_here - (TAPS - 1)) * length :], "tm", 1)
     forward = jnp.asarray(folded_forward_basis(length))
     half_scalar = jnp.reshape(half_index, (1,)).astype(jnp.int32)
-    spectra = spectra_rows(half_scalar, samples, tail, filter_taps, forward, group)
+    taps = jnp.concatenate([filter_taps, filter_taps])
+    spectra = spectra_rows(half_scalar, samples, tail, taps, forward, group)
     spectra = spectra.reshape(group, channels * 2 * frames_here, feed_here)
     received = lax.all_to_all(spectra, GROUP, 0, 0, tiled=True)
     received = received.reshape(-1, feed_here)

time: 87.3 us -> 86.6 us (level)
    unnamed x20 -> x18, local copies, waits for them, and re-layouts: 2.35 us -> 1.63 us
  transfers between devices with their start and end apart: 5 -> 5, of which waited for: 3 -> 3; matrix products, arithmetic and copies ran while one was open for 2% -> 3% of each run, Pallas kernels for 40% -> 41%
where the time goes in v6:
time: 86.6 us; the launch traced here: 86.1 us
  Pallas kernels  53.6 us (62%)
  starting transfers between devices  15.9 us (18%)
  waiting for transfers between devices  10.5 us (12%)
  local copies, waits for them, and re-layouts  4.03 us (5%)
  other arithmetic  1.77 us (2%)
    pallas_call x3, Pallas kernels, partial_beams(): pl.pallas_call(functools.partial(beams_kernel, layout, which, step, piece...  22 us
    pallas_call x1, Pallas kernels, make_weights(): pl.pallas_call(functools.partial(weights_kernel, 32, step), grid=(sum(til...  20.3 us
    all_to_all x1, waiting for transfers between devices, halves_body(): lax.all_to_all(gathered, GROUP, 0, 0, tiled=True).reshape(-1, LANES)  8.68 us
    pallas_call x1, Pallas kernels, spectra_rows(): pl.pallas_call(functools.partial(spectra_kernel, frames_here, group), in_...  6.52 us
    all_to_all x1, starting transfers between devices, halves_body(): received = lax.all_to_all(spectra, GROUP, 0, 0, tiled=True)  5.84 us
    all_to_all x1, starting transfers between devices, halves_body(): lax.all_to_all(gathered, GROUP, 0, 0, tiled=True).reshape(-1, LANES)  3.66 us
    ppermute x1, starting transfers between devices, halves_body(): early = lax.ppermute(early, ('half', 'near'), swap)  3.25 us
    pallas_call x1, Pallas kernels, make_series(): pl.pallas_call(functools.partial(series_kernel, beams_here), in_specs=[pl...  2.61 us
  transfers between devices with their start and end apart: 5, of which 3 were waited for; matrix products, arithmetic and copies ran while one was open for 3% of the time, Pallas kernels for 41%

profile of v6, /device:TPU:0, one launch (start us, length us, event | category | flops | bytes accessed | tf_op | source)
XLA Modules:
  0.0 86.1 jit_solution(15978006541653847372)
XLA Ops:
  0.0 0.0 copy-start.2
  0.0 1.3 %slice.3 = bf16[128,3072]{1,0:T(8,128)(2,1)S(1)} slice(bf16[128,6144]{1,0:T(8,128)(2,1)} %samples_ref.1), slice={[0:128], [3072:6144]} | slice | bytes 1572864 | tf_op jit(solution)/shard_map/slice | solution.py:699
  1.3 2.4 %collective-permute-start = (bf16[128,3072]{1,0:T(8,128)(2,1)S(1)}, bf16[128,3072]{1,0:T(8,128)(2,1)S(1)}, u32[]{:S(2)}, u32[]{:S(2)}) collective-permute-start(bf16[128,3072]{1,0:T(8,128)(2,1)S(1)} %slice.3), channel_id=1, source_target_pairs={{0,1},{2,3},{4,5},{6,7},{8,9},{10,11},{12,13},{14,15},{16,17},{18,... | collective-permute-start | bytes 2359304 | tf_op jit(solution)/shard_map/ppermute | solution.py:24
  3.7 0.8 pad_maximum_fusion.taps_in_ref
  4.5 1.0 %collective-permute-done.tail_ref = bf16[128,3072]{1,0:T(8,128)(2,1)S(1)} collective-permute-done((bf16[128,3072]{1,0:T(8,128)(2,1)S(1)}, bf16[128,3072]{1,0:T(8,128)(2,1)S(1)}, u32[]{:S(2)}, u32[]{:S(2)}) %collective-permute-start) | collective-permute-done | bytes 786464 | tf_op jit(solution)/shard_map/ppermute | solution.py:24
  5.6 0.0 copy-done.2
  5.6 6.5 %spectra.1 = bf16[6144,128]{1,0:T(8,128)(2,1)} custom-call(s32[1]{0:T(128)} %bitcast.half_ref, bf16[128,6144]{1,0:T(8,128)(2,1)S(1)} %copy-done.2, bf16[128,3072]{1,0:T(8,128)(2,1)S(1)} %collective-permute-done.tail_ref, f32[8,1024]{1,0:T(8,128)S(1)} %pad_maximum_fusion.taps_in_ref, bf16[2,2,512,512]{3,2,1,0:T(8,128)(2,1)} %constant.108.clone.basis_ref), custom_call_target="tpu_custom_call" | custom-call | tf_op jit(solution)/shard_map/spectra/pallas_call | solution.py:268
  12.1 0.0 copy-start.5
  12.1 0.0 copy-start.6
  12.1 0.0 copy-start.7
  12.1 5.8 %all-to-all-start = ((bf16[16,384,128]{2,1,0:T(8,128)(2,1)}), bf16[16,384,128]{2,1,0:T(8,128)(2,1)S(1)}, u32[]{:S(2)}, u32[]{:S(2)}) async-start(bf16[16,384,128]{2,1,0:T(8,128)(2,1)} %bitcast.6), calls=%async_computation | async-start | bytes 3145728 | tf_op jit(solution)/shard_map/all_to_all | solution.py:705
  18.0 0.0 copy-done.5
  18.0 0.0 copy-done.6
  18.0 0.0 copy-done.7
  18.1 0.6 pad_maximum_fusion.1.pointing_ref
  18.7 1.0 %broadcast_in_dim.2.code_ref = s32[1024,128]{1,0:T(8,128)} broadcast(s32[1024]{0:T(1024)S(1)} %dynamic-slice_add_fusion), dimensions={0} | broadcast | bytes 528384 | tf_op jit(solution)/shard_map/broadcast_in_dim | solution.py:713
  19.7 0.0 copy-start
  19.7 0.0 copy-start.4
  19.7 20.3 %weights.1.weights_ref = bf16[32,1536,512]{2,1,0:T(8,128)(2,1)} custom-call(s32[1]{0:T(128)} %bitcast.1.first_ref, s32[1024,128]{1,0:T(8,128)} %broadcast_in_dim.2.code_ref, f32[2,4,256]{2,1,0:T(4,128)} %pad_maximum_fusion.1.pointing_ref), custom_call_target="tpu_custom_call" | custom-call | flops 100663296 | bytes 50331648 | tf_op jit(solution)/shard_map/weights/pallas_call | solution.py:359
  40.0 0.7 all-to-all-done
  40.7 0.0 copy-done
  40.7 0.0 copy-done.4
  40.7 7.3 %beams.3 = (bf16[480,256]{1,0:T(8,128)(2,1)S(1)}, bf16[32,32,1024]{2,1,0:T(8,128)(2,1)}) custom-call(s32[1]{0:T(128)} %bitcast.1.first_ref, s32[1024,128]{1,0:T(8,128)S(1)} %copy-done, f32[2,4,256]{2,1,0:T(4,128)S(1)} %copy-done.4, bf16[32,1536,512]{2,1,0:T(8,128)(2,1)} %weights.1.weights_ref, bf16[6144,128]{1,0:T(8,128)(2,1)S(1)} %bitcast.15), custom_call_target="tpu_custom_call" | custom-call | flops 2684354560 | bytes 20971520 | tf_op jit(solution)/shard_map/beams/pallas_call | solution.py:520
  48.0 3.3 %collective-permute-start.1 = (bf16[480,256]{1,0:T(8,128)(2,1)S(1)}, bf16[480,256]{1,0:T(8,128)(2,1)S(1)}, u32[]{:S(2)}, u32[]{:S(2)}) collective-permute-start(bf16[480,256]{1,0:T(8,128)(2,1)S(1)} %get-tuple-element.8), channel_id=1, source_target_pairs={{0,24},{2,26},{4,28},{6,30},{8,16},{10,18},{12,20},{14,22},{16,8},... | collective-permute-start | bytes 737288 | tf_op jit(solution)/shard_map/ppermute | solution.py:734
  51.3 0.0 copy-start.1
  51.3 1.6 %copy-done.1 = bf16[32,32,1024]{2,1,0:T(8,128)(2,1)S(1)} copy-done((bf16[32,32,1024]{2,1,0:T(8,128)(2,1)S(1)}, bf16[32,32,1024]{2,1,0:T(8,128)(2,1)}, u32[]{:S(2)}) %copy-start.1) | copy-done | bytes 2097176
  52.9 4.9 %beams.5 = bf16[288,256]{1,0:T(8,128)(2,1)S(1)} custom-call(s32[1]{0:T(128)} %bitcast.1.first_ref, s32[1024,128]{1,0:T(8,128)S(1)} %copy-done, f32[2,4,256]{2,1,0:T(4,128)S(1)} %copy-done.4, bf16[32,1536,512]{2,1,0:T(8,128)(2,1)} %weights.1.weights_ref, bf16[32,32,1024]{2,1,0:T(8,128)(2,1)S(1)} %copy-done.1), custom_call_target="tpu_custom_call" | custom-call | flops 1610612736 | bytes 12582913 | tf_op jit(solution)/shard_map/beams/pallas_call | solution.py:520
  57.8 0.7 collective-permute-start.2
  58.5 9.9 %beams.4.own_ref = f32[768,256]{1,0:T(8,128)S(1)} custom-call(s32[1]{0:T(128)} %bitcast.1.first_ref, s32[1024,128]{1,0:T(8,128)S(1)} %copy-done, f32[2,4,256]{2,1,0:T(4,128)S(1)} %copy-done.4, bf16[32,1536,512]{2,1,0:T(8,128)(2,1)} %weights.1.weights_ref, bf16[32,32,1024]{2,1,0:T(8,128)(2,1)S(1)} %copy-done.1), custom_call_target="tpu_custom_call" | custom-call | flops 1 | bytes 1 | tf_op jit(solution)/shard_map/beams/pallas_call | solution.py:520
  68.4 0.0 copy-start.8
  68.4 0.0 copy-start.3
  68.4 0.0 collective-permute-done.2.late_ref
  68.4 0.0 collective-permute-done.1.early_ref
  68.4 2.1 %gather.1 = bf16[1536,128]{1,0:T(8,128)(2,1)} custom-call(f32[768,256]{1,0:T(8,128)S(1)} %beams.4.own_ref, bf16[480,256]{1,0:T(8,128)(2,1)S(1)} %collective-permute-done.1.early_ref, bf16[288,256]{1,0:T(8,128)(2,1)S(1)} %collective-permute-done.2.late_ref), custom_call_target="tpu_custom_call" | custom-call | tf_op jit(solution)/shard_map/gather/pallas_call | solution.py:583
  70.5 3.7 %all-to-all-start.1 = ((bf16[16,96,128]{2,1,0:T(8,128)(2,1)}), bf16[16,96,128]{2,1,0:T(8,128)(2,1)S(1)}, u32[]{:S(2)}, u32[]{:S(2)}) async-start(bf16[16,96,128]{2,1,0:T(8,128)(2,1)} %bitcast.8), calls=%async_computation.1 | async-start | bytes 786432 | tf_op jit(solution)/shard_map/all_to_all | solution.py:743
  74.2 0.0 copy-done.8
  74.2 0.1 mul.67
  74.3 0.3 fusion
  74.6 8.7 %all-to-all-done.1 = bf16[16,96,128]{2,1,0:T(8,128)(2,1)S(1)} async-done(((bf16[16,96,128]{2,1,0:T(8,128)(2,1)}), bf16[16,96,128]{2,1,0:T(8,128)(2,1)S(1)}, u32[]{:S(2)}, u32[]{:S(2)}) %all-to-all-start.1) | async-done | bytes 393248 | tf_op jit(solution)/shard_map/all_to_all | solution.py:743
  83.3 0.0 copy-done.3
  83.3 2.6 %series.1 = f32[6,32,1024]{2,1,0:T(8,128)} custom-call(s32[1]{0:T(128)} %bitcast.half_ref, bf16[1536,128]{1,0:T(8,128)(2,1)S(1)} %bitcast.16, f32[128,128]{1,0:T(8,128)S(1)} %get-tuple-element.12.cos_ref, f32[128,128]{1,0:T(8,128)S(1)} %get-tuple-element.11.sin_ref, bf16[2,2,512,512]{3,2,1,0:T(8,128)(2,1)S(1)} %copy-done.3), custom_call_target="tpu_custom_call" | custom-call | tf_op jit(solution)/shard_map/series/pallas_call | solution.py:660
  (7 shorter events, 0.0 us)
Async XLA Ops:
  0.0 5.6 %copy-start.2 = (bf16[128,6144]{1,0:T(8,128)(2,1)S(1)}, bf16[128,6144]{1,0:T(8,128)(2,1)}, u32[]{:S(2)}) copy-start(bf16[128,6144]{1,0:T(8,128)(2,1)} %samples_ref.1) | copy-start | bytes 4718596
  1.3 4.3 %collective-permute-start = (bf16[128,3072]{1,0:T(8,128)(2,1)S(1)}, bf16[128,3072]{1,0:T(8,128)(2,1)S(1)}, u32[]{:S(2)}, u32[]{:S(2)}) collective-permute-start(bf16[128,3072]{1,0:T(8,128)(2,1)S(1)} %slice.3), channel_id=1, source_target_pairs={{0,1},{2,3},{4,5},{6,7},{8,9},{10,11},{12,13},{14,15},{16,17},{18,... | collective-permute-start | bytes 2359304 | tf_op jit(solution)/shard_map/ppermute | solution.py:24
  12.1 5.9 %copy-start.5 = (s32[512,4]{0,1:T(4,128)S(1)}, s32[512,4]{0,1:T(4,128)}, u32[]{:S(2)}) copy-start(s32[512,4]{0,1:T(4,128)} %param.12) | copy-start | bytes 24580
  12.1 5.9 %copy-start.6 = (s32[2048]{0:T(1024)S(1)}, s32[2048]{0:T(1024)}, u32[]{:S(2)}) copy-start(s32[2048]{0:T(1024)} %param.11) | copy-start | bytes 24580
  12.1 5.9 %copy-start.7 = (s32[2048]{0:T(1024)S(1)}, s32[2048]{0:T(1024)}, u32[]{:S(2)}) copy-start(s32[2048]{0:T(1024)} %param.10) | copy-start | bytes 24580
  12.1 28.6 %all-to-all-start = ((bf16[16,384,128]{2,1,0:T(8,128)(2,1)}), bf16[16,384,128]{2,1,0:T(8,128)(2,1)S(1)}, u32[]{:S(2)}, u32[]{:S(2)}) async-start(bf16[16,384,128]{2,1,0:T(8,128)(2,1)} %bitcast.6), calls=%async_computation | async-start | bytes 3145728 | tf_op jit(solution)/shard_map/all_to_all | solution.py:705
  19.7 21.1 %copy-start = (s32[1024,128]{1,0:T(8,128)S(1)}, s32[1024,128]{1,0:T(8,128)}, u32[]{:S(2)}) copy-start(s32[1024,128]{1,0:T(8,128)} %broadcast_in_dim.2.code_ref) | copy-start | bytes 1572868
  19.7 21.1 %copy-start.4 = (f32[2,4,256]{2,1,0:T(4,128)S(1)}, f32[2,4,256]{2,1,0:T(4,128)}, u32[]{:S(2)}) copy-start(f32[2,4,256]{2,1,0:T(4,128)} %pad_maximum_fusion.1.pointing_ref) | copy-start | bytes 24580
  48.0 20.4 %collective-permute-start.1 = (bf16[480,256]{1,0:T(8,128)(2,1)S(1)}, bf16[480,256]{1,0:T(8,128)(2,1)S(1)}, u32[]{:S(2)}, u32[]{:S(2)}) collective-permute-start(bf16[480,256]{1,0:T(8,128)(2,1)S(1)} %get-tuple-element.8), channel_id=1, source_target_pairs={{0,24},{2,26},{4,28},{6,30},{8,16},{10,18},{12,20},{14,22},{16,8},... | collective-permute-start | bytes 737288 | tf_op jit(solution)/shard_map/ppermute | solution.py:734
  51.3 1.6 %copy-start.1 = (bf16[32,32,1024]{2,1,0:T(8,128)(2,1)S(1)}, bf16[32,32,1024]{2,1,0:T(8,128)(2,1)}, u32[]{:S(2)}) copy-start(bf16[32,32,1024]{2,1,0:T(8,128)(2,1)} %get-tuple-element.7.spectra_ref) | copy-start | bytes 6291460
  57.8 10.6 %collective-permute-start.2 = (bf16[288,256]{1,0:T(8,128)(2,1)S(1)}, bf16[288,256]{1,0:T(8,128)(2,1)S(1)}, u32[]{:S(2)}, u32[]{:S(2)}) collective-permute-start(bf16[288,256]{1,0:T(8,128)(2,1)S(1)} %beams.5), channel_id=1, source_target_pairs={{0,24},{2,26},{4,28},{6,30},{8,16},{10,18},{12,20},{14,22},{16,8},... | collective-permute-start | bytes 442376 | tf_op jit(solution)/shard_map/ppermute | solution.py:738
  68.4 5.8 %copy-start.8 = (f32[32]{0:T(128)S(1)}, f32[32]{0:T(128)}, u32[]{:S(2)}) copy-start(f32[32]{0:T(128)} %param.13) | copy-start | bytes 388
  68.4 14.9 %copy-start.3 = (bf16[2,2,512,512]{3,2,1,0:T(8,128)(2,1)S(1)}, bf16[2,2,512,512]{3,2,1,0:T(8,128)(2,1)}, u32[]{:S(2)}) copy-start(bf16[2,2,512,512]{3,2,1,0:T(8,128)(2,1)} %constant.109.clone.basis_ref) | copy-start | bytes 6291460
  70.5 12.8 %all-to-all-start.1 = ((bf16[16,96,128]{2,1,0:T(8,128)(2,1)}), bf16[16,96,128]{2,1,0:T(8,128)(2,1)S(1)}, u32[]{:S(2)}, u32[]{:S(2)}) async-start(bf16[16,96,128]{2,1,0:T(8,128)(2,1)} %bitcast.8), calls=%async_computation.1 | async-start | bytes 786432 | tf_op jit(solution)/shard_map/all_to_all | solution.py:743

commit v7 on v6

--- a/solution.py
+++ b/solution.py
@@ -237,7 +237,6 @@
             low = folded[parity, 1, where, :]
             result = (
                 dot_nt(basis[parity, 0], high)
-                + dot_nt(basis[parity, 1], high)
                 + dot_nt(basis[parity, 0], low)
             ).astype(jnp.bfloat16)
             for part in range(2):

time: 86.6 us -> 85.5 us (0.987)
  Pallas kernels: 53.6 us -> 52.5 us
    pallas_call x1, Pallas kernels: 6.52 us -> 5.44 us  [spectra_rows(): pl.pallas_call(functools.partial(spectra_kernel, frames_here, group), in_...]
where the time goes in v7:
time: 85.5 us; the launch traced here: 85 us
  Pallas kernels  52.5 us (61%)
  starting transfers between devices  15.8 us (18%)
  waiting for transfers between devices  10.5 us (12%)
  local copies, waits for them, and re-layouts  4.03 us (5%)
  other arithmetic  1.77 us (2%)
    pallas_call x3, Pallas kernels, partial_beams(): pl.pallas_call(functools.partial(beams_kernel, layout, which, step, piece...  22 us
    pallas_call x1, Pallas kernels, make_weights(): pl.pallas_call(functools.partial(weights_kernel, 32, step), grid=(sum(til...  20.3 us
    all_to_all x1, waiting for transfers between devices, halves_body(): lax.all_to_all(gathered, GROUP, 0, 0, tiled=True).reshape(-1, LANES)  8.68 us
    all_to_all x1, starting transfers between devices, halves_body(): received = lax.all_to_all(spectra, GROUP, 0, 0, tiled=True)  5.84 us
    pallas_call x1, Pallas kernels, spectra_rows(): pl.pallas_call(functools.partial(spectra_kernel, frames_here, group), in_...  5.44 us
    all_to_all x1, starting transfers between devices, halves_body(): lax.all_to_all(gathered, GROUP, 0, 0, tiled=True).reshape(-1, LANES)  3.65 us
    ppermute x1, starting transfers between devices, halves_body(): early = lax.ppermute(early, ('half', 'near'), swap)  3.25 us
    pallas_call x1, Pallas kernels, make_series(): pl.pallas_call(functools.partial(series_kernel, beams_here), in_specs=[pl...  2.62 us
  transfers between devices with their start and end apart: 5, of which 3 were waited for; matrix products, arithmetic and copies ran while one was open for 3% of the time, Pallas kernels for 41%

profile of v7, /device:TPU:0, one launch (start us, length us, event | category | flops | bytes accessed | tf_op | source)
XLA Modules:
  0.0 85.0 jit_solution(11870964512737539937)
XLA Ops:
  0.0 0.0 copy-start.2
  0.0 1.3 %slice.3 = bf16[128,3072]{1,0:T(8,128)(2,1)S(1)} slice(bf16[128,6144]{1,0:T(8,128)(2,1)} %samples_ref.1), slice={[0:128], [3072:6144]} | slice | bytes 1572864 | tf_op jit(solution)/shard_map/slice | solution.py:698
  1.3 2.4 %collective-permute-start = (bf16[128,3072]{1,0:T(8,128)(2,1)S(1)}, bf16[128,3072]{1,0:T(8,128)(2,1)S(1)}, u32[]{:S(2)}, u32[]{:S(2)}) collective-permute-start(bf16[128,3072]{1,0:T(8,128)(2,1)S(1)} %slice.3), channel_id=1, source_target_pairs={{0,1},{2,3},{4,5},{6,7},{8,9},{10,11},{12,13},{14,15},{16,17},{18,... | collective-permute-start | bytes 2359304 | tf_op jit(solution)/shard_map/ppermute | solution.py:24
  3.7 0.8 pad_maximum_fusion.taps_in_ref
  4.5 1.0 %collective-permute-done.tail_ref = bf16[128,3072]{1,0:T(8,128)(2,1)S(1)} collective-permute-done((bf16[128,3072]{1,0:T(8,128)(2,1)S(1)}, bf16[128,3072]{1,0:T(8,128)(2,1)S(1)}, u32[]{:S(2)}, u32[]{:S(2)}) %collective-permute-start) | collective-permute-done | bytes 786464 | tf_op jit(solution)/shard_map/ppermute | solution.py:24
  5.6 0.0 copy-done.2
  5.6 5.4 %spectra.1 = bf16[6144,128]{1,0:T(8,128)(2,1)} custom-call(s32[1]{0:T(128)} %bitcast.half_ref, bf16[128,6144]{1,0:T(8,128)(2,1)S(1)} %copy-done.2, bf16[128,3072]{1,0:T(8,128)(2,1)S(1)} %collective-permute-done.tail_ref, f32[8,1024]{1,0:T(8,128)S(1)} %pad_maximum_fusion.taps_in_ref, bf16[2,2,512,512]{3,2,1,0:T(8,128)(2,1)} %constant.108.clone.basis_ref), custom_call_target="tpu_custom_call" | custom-call | tf_op jit(solution)/shard_map/spectra/pallas_call | solution.py:267
  11.0 0.0 copy-start.5
  11.0 0.0 copy-start.6
  11.0 0.0 copy-start.7
  11.1 5.8 %all-to-all-start = ((bf16[16,384,128]{2,1,0:T(8,128)(2,1)}), bf16[16,384,128]{2,1,0:T(8,128)(2,1)S(1)}, u32[]{:S(2)}, u32[]{:S(2)}) async-start(bf16[16,384,128]{2,1,0:T(8,128)(2,1)} %bitcast.6), calls=%async_computation | async-start | bytes 3145728 | tf_op jit(solution)/shard_map/all_to_all | solution.py:704
  16.9 0.0 copy-done.5
  17.0 0.0 copy-done.6
  17.0 0.0 copy-done.7
  17.0 0.6 pad_maximum_fusion.1.pointing_ref
  17.6 1.0 %broadcast_in_dim.2.code_ref = s32[1024,128]{1,0:T(8,128)} broadcast(s32[1024]{0:T(1024)S(1)} %dynamic-slice_add_fusion), dimensions={0} | broadcast | bytes 528384 | tf_op jit(solution)/shard_map/broadcast_in_dim | solution.py:712
  18.6 0.0 copy-start
  18.6 0.0 copy-start.4
  18.6 20.3 %weights.1.weights_ref = bf16[32,1536,512]{2,1,0:T(8,128)(2,1)} custom-call(s32[1]{0:T(128)} %bitcast.1.first_ref, s32[1024,128]{1,0:T(8,128)} %broadcast_in_dim.2.code_ref, f32[2,4,256]{2,1,0:T(4,128)} %pad_maximum_fusion.1.pointing_ref), custom_call_target="tpu_custom_call" | custom-call | flops 100663296 | bytes 50331648 | tf_op jit(solution)/shard_map/weights/pallas_call | solution.py:358
  38.9 0.7 all-to-all-done
  39.7 0.0 copy-done
  39.7 0.0 copy-done.4
  39.7 7.3 %beams.3 = (bf16[480,256]{1,0:T(8,128)(2,1)S(1)}, bf16[32,32,1024]{2,1,0:T(8,128)(2,1)}) custom-call(s32[1]{0:T(128)} %bitcast.1.first_ref, s32[1024,128]{1,0:T(8,128)S(1)} %copy-done, f32[2,4,256]{2,1,0:T(4,128)S(1)} %copy-done.4, bf16[32,1536,512]{2,1,0:T(8,128)(2,1)} %weights.1.weights_ref, bf16[6144,128]{1,0:T(8,128)(2,1)S(1)} %bitcast.15), custom_call_target="tpu_custom_call" | custom-call | flops 2684354560 | bytes 20971520 | tf_op jit(solution)/shard_map/beams/pallas_call | solution.py:519
  47.0 3.3 %collective-permute-start.1 = (bf16[480,256]{1,0:T(8,128)(2,1)S(1)}, bf16[480,256]{1,0:T(8,128)(2,1)S(1)}, u32[]{:S(2)}, u32[]{:S(2)}) collective-permute-start(bf16[480,256]{1,0:T(8,128)(2,1)S(1)} %get-tuple-element.8), channel_id=1, source_target_pairs={{0,24},{2,26},{4,28},{6,30},{8,16},{10,18},{12,20},{14,22},{16,8},... | collective-permute-start | bytes 737288 | tf_op jit(solution)/shard_map/ppermute | solution.py:733
  50.2 0.0 copy-start.1
  50.2 1.6 %copy-done.1 = bf16[32,32,1024]{2,1,0:T(8,128)(2,1)S(1)} copy-done((bf16[32,32,1024]{2,1,0:T(8,128)(2,1)S(1)}, bf16[32,32,1024]{2,1,0:T(8,128)(2,1)}, u32[]{:S(2)}) %copy-start.1) | copy-done | bytes 2097176
  51.8 4.9 %beams.5 = bf16[288,256]{1,0:T(8,128)(2,1)S(1)} custom-call(s32[1]{0:T(128)} %bitcast.1.first_ref, s32[1024,128]{1,0:T(8,128)S(1)} %copy-done, f32[2,4,256]{2,1,0:T(4,128)S(1)} %copy-done.4, bf16[32,1536,512]{2,1,0:T(8,128)(2,1)} %weights.1.weights_ref, bf16[32,32,1024]{2,1,0:T(8,128)(2,1)S(1)} %copy-done.1), custom_call_target="tpu_custom_call" | custom-call | flops 1610612736 | bytes 12582913 | tf_op jit(solution)/shard_map/beams/pallas_call | solution.py:519
  56.7 0.7 collective-permute-start.2
  57.4 9.9 %beams.4.own_ref = f32[768,256]{1,0:T(8,128)S(1)} custom-call(s32[1]{0:T(128)} %bitcast.1.first_ref, s32[1024,128]{1,0:T(8,128)S(1)} %copy-done, f32[2,4,256]{2,1,0:T(4,128)S(1)} %copy-done.4, bf16[32,1536,512]{2,1,0:T(8,128)(2,1)} %weights.1.weights_ref, bf16[32,32,1024]{2,1,0:T(8,128)(2,1)S(1)} %copy-done.1), custom_call_target="tpu_custom_call" | custom-call | flops 1 | bytes 1 | tf_op jit(solution)/shard_map/beams/pallas_call | solution.py:519
  67.3 0.0 copy-start.8
  67.3 0.0 copy-start.3
  67.3 0.0 collective-permute-done.2.late_ref
  67.3 0.0 collective-permute-done.1.early_ref
  67.3 2.1 %gather.1 = bf16[1536,128]{1,0:T(8,128)(2,1)} custom-call(f32[768,256]{1,0:T(8,128)S(1)} %beams.4.own_ref, bf16[480,256]{1,0:T(8,128)(2,1)S(1)} %collective-permute-done.1.early_ref, bf16[288,256]{1,0:T(8,128)(2,1)S(1)} %collective-permute-done.2.late_ref), custom_call_target="tpu_custom_call" | custom-call | tf_op jit(solution)/shard_map/gather/pallas_call | solution.py:582
  69.4 3.7 %all-to-all-start.1 = ((bf16[16,96,128]{2,1,0:T(8,128)(2,1)}), bf16[16,96,128]{2,1,0:T(8,128)(2,1)S(1)}, u32[]{:S(2)}, u32[]{:S(2)}) async-start(bf16[16,96,128]{2,1,0:T(8,128)(2,1)} %bitcast.8), calls=%async_computation.1 | async-start | bytes 786432 | tf_op jit(solution)/shard_map/all_to_all | solution.py:742
  73.1 0.0 copy-done.8
  73.1 0.1 mul.67
  73.2 0.3 fusion
  73.6 8.7 %all-to-all-done.1 = bf16[16,96,128]{2,1,0:T(8,128)(2,1)S(1)} async-done(((bf16[16,96,128]{2,1,0:T(8,128)(2,1)}), bf16[16,96,128]{2,1,0:T(8,128)(2,1)S(1)}, u32[]{:S(2)}, u32[]{:S(2)}) %all-to-all-start.1) | async-done | bytes 393248 | tf_op jit(solution)/shard_map/all_to_all | solution.py:742
  82.2 0.0 copy-done.3
  82.2 2.6 %series.1 = f32[6,32,1024]{2,1,0:T(8,128)} custom-call(s32[1]{0:T(128)} %bitcast.half_ref, bf16[1536,128]{1,0:T(8,128)(2,1)S(1)} %bitcast.16, f32[128,128]{1,0:T(8,128)S(1)} %get-tuple-element.12.cos_ref, f32[128,128]{1,0:T(8,128)S(1)} %get-tuple-element.11.sin_ref, bf16[2,2,512,512]{3,2,1,0:T(8,128)(2,1)S(1)} %copy-done.3), custom_call_target="tpu_custom_call" | custom-call | tf_op jit(solution)/shard_map/series/pallas_call | solution.py:659
  (7 shorter events, 0.0 us)
Async XLA Ops:
  0.0 5.6 %copy-start.2 = (bf16[128,6144]{1,0:T(8,128)(2,1)S(1)}, bf16[128,6144]{1,0:T(8,128)(2,1)}, u32[]{:S(2)}) copy-start(bf16[128,6144]{1,0:T(8,128)(2,1)} %samples_ref.1) | copy-start | bytes 4718596
  1.3 4.3 %collective-permute-start = (bf16[128,3072]{1,0:T(8,128)(2,1)S(1)}, bf16[128,3072]{1,0:T(8,128)(2,1)S(1)}, u32[]{:S(2)}, u32[]{:S(2)}) collective-permute-start(bf16[128,3072]{1,0:T(8,128)(2,1)S(1)} %slice.3), channel_id=1, source_target_pairs={{0,1},{2,3},{4,5},{6,7},{8,9},{10,11},{12,13},{14,15},{16,17},{18,... | collective-permute-start | bytes 2359304 | tf_op jit(solution)/shard_map/ppermute | solution.py:24
  11.0 5.9 %copy-start.5 = (s32[512,4]{0,1:T(4,128)S(1)}, s32[512,4]{0,1:T(4,128)}, u32[]{:S(2)}) copy-start(s32[512,4]{0,1:T(4,128)} %param.12) | copy-start | bytes 24580
  11.0 5.9 %copy-start.6 = (s32[2048]{0:T(1024)S(1)}, s32[2048]{0:T(1024)}, u32[]{:S(2)}) copy-start(s32[2048]{0:T(1024)} %param.11) | copy-start | bytes 24580
  11.0 5.9 %copy-start.7 = (s32[2048]{0:T(1024)S(1)}, s32[2048]{0:T(1024)}, u32[]{:S(2)}) copy-start(s32[2048]{0:T(1024)} %param.10) | copy-start | bytes 24580
  11.1 28.6 %all-to-all-start = ((bf16[16,384,128]{2,1,0:T(8,128)(2,1)}), bf16[16,384,128]{2,1,0:T(8,128)(2,1)S(1)}, u32[]{:S(2)}, u32[]{:S(2)}) async-start(bf16[16,384,128]{2,1,0:T(8,128)(2,1)} %bitcast.6), calls=%async_computation | async-start | bytes 3145728 | tf_op jit(solution)/shard_map/all_to_all | solution.py:704
  18.6 21.1 %copy-start = (s32[1024,128]{1,0:T(8,128)S(1)}, s32[1024,128]{1,0:T(8,128)}, u32[]{:S(2)}) copy-start(s32[1024,128]{1,0:T(8,128)} %broadcast_in_dim.2.code_ref) | copy-start | bytes 1572868
  18.6 21.1 %copy-start.4 = (f32[2,4,256]{2,1,0:T(4,128)S(1)}, f32[2,4,256]{2,1,0:T(4,128)}, u32[]{:S(2)}) copy-start(f32[2,4,256]{2,1,0:T(4,128)} %pad_maximum_fusion.1.pointing_ref) | copy-start | bytes 24580
  47.0 20.4 %collective-permute-start.1 = (bf16[480,256]{1,0:T(8,128)(2,1)S(1)}, bf16[480,256]{1,0:T(8,128)(2,1)S(1)}, u32[]{:S(2)}, u32[]{:S(2)}) collective-permute-start(bf16[480,256]{1,0:T(8,128)(2,1)S(1)} %get-tuple-element.8), channel_id=1, source_target_pairs={{0,24},{2,26},{4,28},{6,30},{8,16},{10,18},{12,20},{14,22},{16,8},... | collective-permute-start | bytes 737288 | tf_op jit(solution)/shard_map/ppermute | solution.py:733
  50.2 1.6 %copy-start.1 = (bf16[32,32,1024]{2,1,0:T(8,128)(2,1)S(1)}, bf16[32,32,1024]{2,1,0:T(8,128)(2,1)}, u32[]{:S(2)}) copy-start(bf16[32,32,1024]{2,1,0:T(8,128)(2,1)} %get-tuple-element.7.spectra_ref) | copy-start | bytes 6291460
  56.7 10.6 %collective-permute-start.2 = (bf16[288,256]{1,0:T(8,128)(2,1)S(1)}, bf16[288,256]{1,0:T(8,128)(2,1)S(1)}, u32[]{:S(2)}, u32[]{:S(2)}) collective-permute-start(bf16[288,256]{1,0:T(8,128)(2,1)S(1)} %beams.5), channel_id=1, source_target_pairs={{0,24},{2,26},{4,28},{6,30},{8,16},{10,18},{12,20},{14,22},{16,8},... | collective-permute-start | bytes 442376 | tf_op jit(solution)/shard_map/ppermute | solution.py:737
  67.3 5.8 %copy-start.8 = (f32[32]{0:T(128)S(1)}, f32[32]{0:T(128)}, u32[]{:S(2)}) copy-start(f32[32]{0:T(128)} %param.13) | copy-start | bytes 388
  67.3 14.9 %copy-start.3 = (bf16[2,2,512,512]{3,2,1,0:T(8,128)(2,1)S(1)}, bf16[2,2,512,512]{3,2,1,0:T(8,128)(2,1)}, u32[]{:S(2)}) copy-start(bf16[2,2,512,512]{3,2,1,0:T(8,128)(2,1)} %constant.109.clone.basis_ref) | copy-start | bytes 6291460
  69.4 12.8 %all-to-all-start.1 = ((bf16[16,96,128]{2,1,0:T(8,128)(2,1)}), bf16[16,96,128]{2,1,0:T(8,128)(2,1)S(1)}, u32[]{:S(2)}, u32[]{:S(2)}) async-start(bf16[16,96,128]{2,1,0:T(8,128)(2,1)} %bitcast.8), calls=%async_computation.1 | async-start | bytes 786432 | tf_op jit(solution)/shard_map/all_to_all | solution.py:742

commit v8 on v7

--- a/solution.py
+++ b/solution.py
@@ -444,7 +444,7 @@
         source = weights_ref.at[there, pl.ds(skipped, made_feeds)]
         copies.append(pltpu.make_async_copy(source, stored.at[place], sems.at[piece]))
     ahead = min(5, pieces)
-    soon = ahead if raw else 2
+    soon = ahead if raw else 3
     for copy in copies[:soon]:
         copy.start()
 

time: 85.5 us -> 85.5 us (level)
  no operation moved by 1% of the time
where the time goes in v8:
time: 85.5 us; the launch traced here: 85 us
  Pallas kernels  51.9 us (61%)
  starting transfers between devices  16.5 us (19%)
  waiting for transfers between devices  10.5 us (12%)
  local copies, waits for them, and re-layouts  4.03 us (5%)
  other arithmetic  1.77 us (2%)
    pallas_call x3, Pallas kernels, partial_beams(): pl.pallas_call(functools.partial(beams_kernel, layout, which, step, piece...  21.4 us
    pallas_call x1, Pallas kernels, make_weights(): pl.pallas_call(functools.partial(weights_kernel, 32, step), grid=(sum(til...  20.3 us
    all_to_all x1, waiting for transfers between devices, halves_body(): lax.all_to_all(gathered, GROUP, 0, 0, tiled=True).reshape(-1, LANES)  8.68 us
    all_to_all x1, starting transfers between devices, halves_body(): received = lax.all_to_all(spectra, GROUP, 0, 0, tiled=True)  5.84 us
    pallas_call x1, Pallas kernels, spectra_rows(): pl.pallas_call(functools.partial(spectra_kernel, frames_here, group), in_...  5.44 us
    all_to_all x1, starting transfers between devices, halves_body(): lax.all_to_all(gathered, GROUP, 0, 0, tiled=True).reshape(-1, LANES)  4.26 us
    ppermute x1, starting transfers between devices, halves_body(): early = lax.ppermute(early, ('half', 'near'), swap)  3.25 us
    pallas_call x1, Pallas kernels, make_series(): pl.pallas_call(functools.partial(series_kernel, beams_here), in_specs=[pl...  2.62 us
  transfers between devices with their start and end apart: 5, of which 3 were waited for; matrix products, arithmetic and copies ran while one was open for 3% of the time, Pallas kernels for 41%

profile of v8, /device:TPU:0, one launch (start us, length us, event | category | flops | bytes accessed | tf_op | source)
XLA Modules:
  0.0 85.0 jit_solution(10563336206000178627)
XLA Ops:
  0.0 0.0 copy-start.2
  0.0 1.3 %slice.3 = bf16[128,3072]{1,0:T(8,128)(2,1)S(1)} slice(bf16[128,6144]{1,0:T(8,128)(2,1)} %samples_ref.1), slice={[0:128], [3072:6144]} | slice | bytes 1572864 | tf_op jit(solution)/shard_map/slice | solution.py:698
  1.3 2.4 %collective-permute-start = (bf16[128,3072]{1,0:T(8,128)(2,1)S(1)}, bf16[128,3072]{1,0:T(8,128)(2,1)S(1)}, u32[]{:S(2)}, u32[]{:S(2)}) collective-permute-start(bf16[128,3072]{1,0:T(8,128)(2,1)S(1)} %slice.3), channel_id=1, source_target_pairs={{0,1},{2,3},{4,5},{6,7},{8,9},{10,11},{12,13},{14,15},{16,17},{18,... | collective-permute-start | bytes 2359304 | tf_op jit(solution)/shard_map/ppermute | solution.py:24
  3.7 0.8 pad_maximum_fusion.taps_in_ref
  4.5 1.0 %collective-permute-done.tail_ref = bf16[128,3072]{1,0:T(8,128)(2,1)S(1)} collective-permute-done((bf16[128,3072]{1,0:T(8,128)(2,1)S(1)}, bf16[128,3072]{1,0:T(8,128)(2,1)S(1)}, u32[]{:S(2)}, u32[]{:S(2)}) %collective-permute-start) | collective-permute-done | bytes 786464 | tf_op jit(solution)/shard_map/ppermute | solution.py:24
  5.6 0.0 copy-done.2
  5.6 5.4 %spectra.1 = bf16[6144,128]{1,0:T(8,128)(2,1)} custom-call(s32[1]{0:T(128)} %bitcast.half_ref, bf16[128,6144]{1,0:T(8,128)(2,1)S(1)} %copy-done.2, bf16[128,3072]{1,0:T(8,128)(2,1)S(1)} %collective-permute-done.tail_ref, f32[8,1024]{1,0:T(8,128)S(1)} %pad_maximum_fusion.taps_in_ref, bf16[2,2,512,512]{3,2,1,0:T(8,128)(2,1)} %constant.108.clone.basis_ref), custom_call_target="tpu_custom_call" | custom-call | tf_op jit(solution)/shard_map/spectra/pallas_call | solution.py:267
  11.0 0.0 copy-start.5
  11.0 0.0 copy-start.6
  11.0 0.0 copy-start.7
  11.1 5.8 %all-to-all-start = ((bf16[16,384,128]{2,1,0:T(8,128)(2,1)}), bf16[16,384,128]{2,1,0:T(8,128)(2,1)S(1)}, u32[]{:S(2)}, u32[]{:S(2)}) async-start(bf16[16,384,128]{2,1,0:T(8,128)(2,1)} %bitcast.6), calls=%async_computation | async-start | bytes 3145728 | tf_op jit(solution)/shard_map/all_to_all | solution.py:704
  16.9 0.0 copy-done.5
  17.0 0.0 copy-done.6
  17.0 0.0 copy-done.7
  17.0 0.6 pad_maximum_fusion.1.pointing_ref
  17.6 1.0 %broadcast_in_dim.2.code_ref = s32[1024,128]{1,0:T(8,128)} broadcast(s32[1024]{0:T(1024)S(1)} %dynamic-slice_add_fusion), dimensions={0} | broadcast | bytes 528384 | tf_op jit(solution)/shard_map/broadcast_in_dim | solution.py:712
  18.6 0.0 copy-start
  18.6 0.0 copy-start.4
  18.6 20.3 %weights.1.weights_ref = bf16[32,1536,512]{2,1,0:T(8,128)(2,1)} custom-call(s32[1]{0:T(128)} %bitcast.1.first_ref, s32[1024,128]{1,0:T(8,128)} %broadcast_in_dim.2.code_ref, f32[2,4,256]{2,1,0:T(4,128)} %pad_maximum_fusion.1.pointing_ref), custom_call_target="tpu_custom_call" | custom-call | flops 100663296 | bytes 50331648 | tf_op jit(solution)/shard_map/weights/pallas_call | solution.py:358
  38.9 0.7 all-to-all-done
  39.7 0.0 copy-done
  39.7 0.0 copy-done.4
  39.7 7.3 %beams.3 = (bf16[480,256]{1,0:T(8,128)(2,1)S(1)}, bf16[32,32,1024]{2,1,0:T(8,128)(2,1)}) custom-call(s32[1]{0:T(128)} %bitcast.1.first_ref, s32[1024,128]{1,0:T(8,128)S(1)} %copy-done, f32[2,4,256]{2,1,0:T(4,128)S(1)} %copy-done.4, bf16[32,1536,512]{2,1,0:T(8,128)(2,1)} %weights.1.weights_ref, bf16[6144,128]{1,0:T(8,128)(2,1)S(1)} %bitcast.15), custom_call_target="tpu_custom_call" | custom-call | flops 2684354560 | bytes 20971520 | tf_op jit(solution)/shard_map/beams/pallas_call | solution.py:519
  47.0 3.3 %collective-permute-start.1 = (bf16[480,256]{1,0:T(8,128)(2,1)S(1)}, bf16[480,256]{1,0:T(8,128)(2,1)S(1)}, u32[]{:S(2)}, u32[]{:S(2)}) collective-permute-start(bf16[480,256]{1,0:T(8,128)(2,1)S(1)} %get-tuple-element.8), channel_id=1, source_target_pairs={{0,24},{2,26},{4,28},{6,30},{8,16},{10,18},{12,20},{14,22},{16,8},... | collective-permute-start | bytes 737288 | tf_op jit(solution)/shard_map/ppermute | solution.py:733
  50.2 0.0 copy-start.1
  50.2 1.6 %copy-done.1 = bf16[32,32,1024]{2,1,0:T(8,128)(2,1)S(1)} copy-done((bf16[32,32,1024]{2,1,0:T(8,128)(2,1)S(1)}, bf16[32,32,1024]{2,1,0:T(8,128)(2,1)}, u32[]{:S(2)}) %copy-start.1) | copy-done | bytes 2097176
  51.8 4.6 %beams.5 = bf16[288,256]{1,0:T(8,128)(2,1)S(1)} custom-call(s32[1]{0:T(128)} %bitcast.1.first_ref, s32[1024,128]{1,0:T(8,128)S(1)} %copy-done, f32[2,4,256]{2,1,0:T(4,128)S(1)} %copy-done.4, bf16[32,1536,512]{2,1,0:T(8,128)(2,1)} %weights.1.weights_ref, bf16[32,32,1024]{2,1,0:T(8,128)(2,1)S(1)} %copy-done.1), custom_call_target="tpu_custom_call" | custom-call | flops 1610612736 | bytes 12582913 | tf_op jit(solution)/shard_map/beams/pallas_call | solution.py:519
  56.5 0.7 collective-permute-start.2
  57.2 9.5 %beams.4.own_ref = f32[768,256]{1,0:T(8,128)S(1)} custom-call(s32[1]{0:T(128)} %bitcast.1.first_ref, s32[1024,128]{1,0:T(8,128)S(1)} %copy-done, f32[2,4,256]{2,1,0:T(4,128)S(1)} %copy-done.4, bf16[32,1536,512]{2,1,0:T(8,128)(2,1)} %weights.1.weights_ref, bf16[32,32,1024]{2,1,0:T(8,128)(2,1)S(1)} %copy-done.1), custom_call_target="tpu_custom_call" | custom-call | flops 1 | bytes 1 | tf_op jit(solution)/shard_map/beams/pallas_call | solution.py:519
  66.7 0.0 copy-start.8
  66.7 0.0 copy-start.3
  66.7 0.0 collective-permute-done.2.late_ref
  66.7 0.0 collective-permute-done.1.early_ref
  66.7 2.1 %gather.1 = bf16[1536,128]{1,0:T(8,128)(2,1)} custom-call(f32[768,256]{1,0:T(8,128)S(1)} %beams.4.own_ref, bf16[480,256]{1,0:T(8,128)(2,1)S(1)} %collective-permute-done.1.early_ref, bf16[288,256]{1,0:T(8,128)(2,1)S(1)} %collective-permute-done.2.late_ref), custom_call_target="tpu_custom_call" | custom-call | tf_op jit(solution)/shard_map/gather/pallas_call | solution.py:582
  68.8 4.3 %all-to-all-start.1 = ((bf16[16,96,128]{2,1,0:T(8,128)(2,1)}), bf16[16,96,128]{2,1,0:T(8,128)(2,1)S(1)}, u32[]{:S(2)}, u32[]{:S(2)}) async-start(bf16[16,96,128]{2,1,0:T(8,128)(2,1)} %bitcast.8), calls=%async_computation.1 | async-start | bytes 786432 | tf_op jit(solution)/shard_map/all_to_all | solution.py:742
  73.1 0.0 copy-done.8
  73.1 0.1 mul.67
  73.2 0.3 fusion
  73.6 8.7 %all-to-all-done.1 = bf16[16,96,128]{2,1,0:T(8,128)(2,1)S(1)} async-done(((bf16[16,96,128]{2,1,0:T(8,128)(2,1)}), bf16[16,96,128]{2,1,0:T(8,128)(2,1)S(1)}, u32[]{:S(2)}, u32[]{:S(2)}) %all-to-all-start.1) | async-done | bytes 393248 | tf_op jit(solution)/shard_map/all_to_all | solution.py:742
  82.2 0.0 copy-done.3
  82.2 2.6 %series.1 = f32[6,32,1024]{2,1,0:T(8,128)} custom-call(s32[1]{0:T(128)} %bitcast.half_ref, bf16[1536,128]{1,0:T(8,128)(2,1)S(1)} %bitcast.16, f32[128,128]{1,0:T(8,128)S(1)} %get-tuple-element.12.cos_ref, f32[128,128]{1,0:T(8,128)S(1)} %get-tuple-element.11.sin_ref, bf16[2,2,512,512]{3,2,1,0:T(8,128)(2,1)S(1)} %copy-done.3), custom_call_target="tpu_custom_call" | custom-call | tf_op jit(solution)/shard_map/series/pallas_call | solution.py:659
  (7 shorter events, 0.0 us)
Async XLA Ops:
  0.0 5.6 %copy-start.2 = (bf16[128,6144]{1,0:T(8,128)(2,1)S(1)}, bf16[128,6144]{1,0:T(8,128)(2,1)}, u32[]{:S(2)}) copy-start(bf16[128,6144]{1,0:T(8,128)(2,1)} %samples_ref.1) | copy-start | bytes 4718596
  1.3 4.3 %collective-permute-start = (bf16[128,3072]{1,0:T(8,128)(2,1)S(1)}, bf16[128,3072]{1,0:T(8,128)(2,1)S(1)}, u32[]{:S(2)}, u32[]{:S(2)}) collective-permute-start(bf16[128,3072]{1,0:T(8,128)(2,1)S(1)} %slice.3), channel_id=1, source_target_pairs={{0,1},{2,3},{4,5},{6,7},{8,9},{10,11},{12,13},{14,15},{16,17},{18,... | collective-permute-start | bytes 2359304 | tf_op jit(solution)/shard_map/ppermute | solution.py:24
  11.0 5.9 %copy-start.5 = (s32[512,4]{0,1:T(4,128)S(1)}, s32[512,4]{0,1:T(4,128)}, u32[]{:S(2)}) copy-start(s32[512,4]{0,1:T(4,128)} %param.12) | copy-start | bytes 24580
  11.0 5.9 %copy-start.6 = (s32[2048]{0:T(1024)S(1)}, s32[2048]{0:T(1024)}, u32[]{:S(2)}) copy-start(s32[2048]{0:T(1024)} %param.11) | copy-start | bytes 24580
  11.0 5.9 %copy-start.7 = (s32[2048]{0:T(1024)S(1)}, s32[2048]{0:T(1024)}, u32[]{:S(2)}) copy-start(s32[2048]{0:T(1024)} %param.10) | copy-start | bytes 24580
  11.1 28.6 %all-to-all-start = ((bf16[16,384,128]{2,1,0:T(8,128)(2,1)}), bf16[16,384,128]{2,1,0:T(8,128)(2,1)S(1)}, u32[]{:S(2)}, u32[]{:S(2)}) async-start(bf16[16,384,128]{2,1,0:T(8,128)(2,1)} %bitcast.6), calls=%async_computation | async-start | bytes 3145728 | tf_op jit(solution)/shard_map/all_to_all | solution.py:704
  18.6 21.1 %copy-start = (s32[1024,128]{1,0:T(8,128)S(1)}, s32[1024,128]{1,0:T(8,128)}, u32[]{:S(2)}) copy-start(s32[1024,128]{1,0:T(8,128)} %broadcast_in_dim.2.code_ref) | copy-start | bytes 1572868
  18.6 21.1 %copy-start.4 = (f32[2,4,256]{2,1,0:T(4,128)S(1)}, f32[2,4,256]{2,1,0:T(4,128)}, u32[]{:S(2)}) copy-start(f32[2,4,256]{2,1,0:T(4,128)} %pad_maximum_fusion.1.pointing_ref) | copy-start | bytes 24580
  47.0 19.7 %collective-permute-start.1 = (bf16[480,256]{1,0:T(8,128)(2,1)S(1)}, bf16[480,256]{1,0:T(8,128)(2,1)S(1)}, u32[]{:S(2)}, u32[]{:S(2)}) collective-permute-start(bf16[480,256]{1,0:T(8,128)(2,1)S(1)} %get-tuple-element.8), channel_id=1, source_target_pairs={{0,24},{2,26},{4,28},{6,30},{8,16},{10,18},{12,20},{14,22},{16,8},... | collective-permute-start | bytes 737288 | tf_op jit(solution)/shard_map/ppermute | solution.py:733
  50.2 1.6 %copy-start.1 = (bf16[32,32,1024]{2,1,0:T(8,128)(2,1)S(1)}, bf16[32,32,1024]{2,1,0:T(8,128)(2,1)}, u32[]{:S(2)}) copy-start(bf16[32,32,1024]{2,1,0:T(8,128)(2,1)} %get-tuple-element.7.spectra_ref) | copy-start | bytes 6291460
  56.5 10.2 %collective-permute-start.2 = (bf16[288,256]{1,0:T(8,128)(2,1)S(1)}, bf16[288,256]{1,0:T(8,128)(2,1)S(1)}, u32[]{:S(2)}, u32[]{:S(2)}) collective-permute-start(bf16[288,256]{1,0:T(8,128)(2,1)S(1)} %beams.5), channel_id=1, source_target_pairs={{0,24},{2,26},{4,28},{6,30},{8,16},{10,18},{12,20},{14,22},{16,8},... | collective-permute-start | bytes 442376 | tf_op jit(solution)/shard_map/ppermute | solution.py:737
  66.7 6.4 %copy-start.8 = (f32[32]{0:T(128)S(1)}, f32[32]{0:T(128)}, u32[]{:S(2)}) copy-start(f32[32]{0:T(128)} %param.13) | copy-start | bytes 388
  66.7 15.6 %copy-start.3 = (bf16[2,2,512,512]{3,2,1,0:T(8,128)(2,1)S(1)}, bf16[2,2,512,512]{3,2,1,0:T(8,128)(2,1)}, u32[]{:S(2)}) copy-start(bf16[2,2,512,512]{3,2,1,0:T(8,128)(2,1)} %constant.109.clone.basis_ref) | copy-start | bytes 6291460
  68.8 13.4 %all-to-all-start.1 = ((bf16[16,96,128]{2,1,0:T(8,128)(2,1)}), bf16[16,96,128]{2,1,0:T(8,128)(2,1)S(1)}, u32[]{:S(2)}, u32[]{:S(2)}) async-start(bf16[16,96,128]{2,1,0:T(8,128)(2,1)} %bitcast.8), calls=%async_computation.1 | async-start | bytes 786432 | tf_op jit(solution)/shard_map/all_to_all | solution.py:742
